TPU v7x, 128 devices: a whole 4x4x4 slice. The times are simulated.
128 devices in a mesh: row: 8 (over y_hi, x), col: 16 (over z, y_lo, core).
Axes of the slice: x: 4, y: 4 (y_hi: 2, y_lo: 2; y = y_hi * 2 + y_lo), z: 4, core: 2. Of those that a mesh axis runs over, the one named last changes fastest.
Arguments:
- density: bfloat16 [2, 2944, 5888], P(None, 'row', 'col'), may hold values from -6 to 6
- pattern: int32 [2, 128, 256], P(None, 'row', 'col'), may hold values 0 or 1
- keep: int32 [2, 128, 256], P(None, 'row', 'col'), may hold values 0 or 1
- owner: int32 [128, 512, 1], P(('row', 'col')), may hold values from 0 to 127; in each aligned block of 512 rows (0 to 511, 512 to 1023, ..., all dimensions but the last counted through in order) at most 12 rows name the same one
Outputs:
- owned: bfloat16 [128, 128, 12, 529], P(('row', 'col'))
Inputs may be any that keep to these rules, and one draw needn't show every extreme that they name: Within the blocks of one device, no owner is named more than 12 times.
All inputs are finite; a program needn't handle non-finite values. No bound on the sum of `pattern` or of `keep` on one device may be relied on, other than what follows from the above.
Results may differ from a plain program's by a relative error of at most 0.0022.
Values may be sent and summed in bfloat16 or wider, within the bound.
A program may use at most 64 MiB of HBM per device.

v0:
```python
import jax
import jax.numpy as jnp
from jax import lax
from jax.sharding import PartitionSpec as P

BS = 23


def passed_along(value, axis, by):
    count = lax.axis_size(axis)
    return lax.ppermute(value, axis, [(i, (i + by) % count) for i in range(count)])


def expand(mask, width):
    grown = jnp.repeat(jnp.repeat(mask, width, axis=1), width, axis=2)
    return grown.astype(jnp.bfloat16)


def align_left(piece, amount, levels):
    for level in range(levels):
        moved = passed_along(piece, "col", -(1 << level))
        piece = jnp.where((amount >> level) % 2 == 1, moved, piece)
    return piece


def align_right(piece, amount, levels):
    for level in range(levels):
        moved = passed_along(piece, "row", -(1 << level))
        piece = jnp.where((amount >> level) % 2 == 1, moved, piece)
    return piece


def product(left, right, start, steps, row_size):
    width = left.shape[2]

    def multiply(total, left_now, right_now, step):
        index = (start + step) % steps
        half = index // row_size
        piece = lax.dynamic_index_in_dim(right_now, half, 0, keepdims=False)
        term = jnp.dot(
            left_now.reshape(2 * width, width), piece, preferred_element_type=jnp.float32
        )
        return total + term.reshape(2, width, width)

    total = multiply(jnp.zeros((2, width, width), jnp.float32), left, right, 0)

    def advance(step, carry):
        total_now, left_now, right_now = carry
        left_now = passed_along(left_now, "col", -1)
        right_now = passed_along(right_now, "row", -1)
        return (multiply(total_now, left_now, right_now, step), left_now, right_now)

    total, left, right = lax.fori_loop(1, steps, advance, (total, left, right))
    return (total, left)


def per_device(density, pattern, keep, owner):
    row_size = lax.axis_size("row")
    col_size = lax.axis_size("col")
    row_at = lax.axis_index("row")
    col_at = lax.axis_index("col")
    levels = row_size.bit_length() - 1
    blocks_side = pattern.shape[1]
    width = density.shape[1]
    order = width * col_size
    devices = row_size * col_size
    capacity = max(4, 6 * blocks_side * blocks_side // devices)
    mask_pat = expand(pattern, BS)
    mat = density * mask_pat
    start = row_at + col_at
    left_first = align_left(mat, row_at, levels)
    right_first = align_right(mat, col_at % row_size, levels)
    total, left_last = product(left_first, right_first, start, col_size, row_size)
    square = (total / order * mask_pat.astype(jnp.float32)).astype(jnp.bfloat16)
    left_second = align_left(mat, row_at, levels)
    right_second = align_right(square, col_at % row_size, levels)
    cube, unused = product(left_second, right_second, start, col_size, row_size)
    mask_keep = expand(keep, BS).astype(jnp.float32)
    update = (mask_keep * (1.5 * mat.astype(jnp.float32) - 0.5 * cube)).astype(jnp.bfloat16)
    blocks = update.reshape(2, blocks_side, BS, blocks_side, BS).transpose(0, 1, 3, 2, 4)
    blocks = blocks.reshape(2 * blocks_side * blocks_side, BS * BS)
    targets = owner[0, :, 0]
    onehot = (targets[:, None] == jnp.arange(devices, dtype=jnp.int32)[None, :]).astype(jnp.int32)
    ranks = jnp.cumsum(onehot, axis=0) - onehot
    slots = jnp.sum(ranks * onehot, axis=1)
    outgoing = jnp.zeros((devices, capacity, BS * BS), jnp.bfloat16).at[targets, slots].set(blocks)
    arrived = lax.all_to_all(outgoing, ("row", "col"), split_axis=0, concat_axis=0, tiled=True)
    return arrived.reshape(1, devices, capacity, BS * BS)


def solution(mesh):
    placed = (
        P(None, "row", "col"),
        P(None, "row", "col"),
        P(None, "row", "col"),
        P(("row", "col"), None, None),
    )
    return jax.shard_map(
        per_device,
        mesh=mesh,
        in_specs=placed,
        out_specs=P(("row", "col"), None, None, None),
        check_vma=False,
    )
```

profile of v0, /device:TPU:1, one launch (start us, length us, event | category | flops | bytes accessed | tf_op | source)
XLA Modules:
  0.0 1033.5 jit_solution(5690793928528158883)
XLA Ops:
  11.1 10.6 %collective-permute-done.7 = bf16[2,368,368]{1,0,2:T(2,128)(2,1)S(1)} collective-permute-done((bf16[2,368,368]{1,0,2:T(2,128)(2,1)S(1)}, bf16[2,368,368]{1,0,2:T(2,128)(2,1)S(1)}, u32[]{:S(2)}, u32[]{:S(2)}) %collective-permute-start.7) | collective-permute-done | bytes 541728 | tf_op jit(solution)/shard_map/ppermute | solution.py:11
  28.2 8.0 collective-permute-done.8
  40.7 12.2 %collective-permute-done.9 = bf16[2,368,368]{1,0,2:T(2,128)(2,1)S(1)} collective-permute-done((bf16[2,368,368]{1,0,2:T(2,128)(2,1)S(1)}, bf16[2,368,368]{1,0,2:T(2,128)(2,1)S(1)}, u32[]{:S(2)}, u32[]{:S(2)}) %collective-permute-start.9) | collective-permute-done | bytes 541728 | tf_op jit(solution)/shard_map/ppermute | solution.py:11
  59.7 413.1 %while.38 = (s32[]{:T(128)}, f32[2,368,368]{1,0,2:T(2,128)}, bf16[2,368,368]{2,1,0:T(8,128)(2,1)S(1)}, bf16[2,368,368]{2,1,0:T(8,128)(2,1)S(1)}, s32[]{:T(128)},...) while((s32[]{:T(128)}, f32[2,368,368]{1,0,2:T(2,128)}, ...), condition=%wide.region_4.5_spmd, body=%wide.region_3.4_spmd.sunk | while | flops 199615008 | bytes 13849090 | solution.py:53
  62.5 18.2 %collective-permute-start.1 = (bf16[2,368,368]{2,1,0:T(8,128)(2,1)S(1)}, bf16[2,368,368]{2,1,0:T(8,128)(2,1)S(1)}, u32[]{:S(2)}, u32[]{:S(2)}) collective-permute-start(bf16[2,368,368]{2,1,0:T(8,128)(2,1)S(1)} %get-tuple-element.409), channel_id=1, source_target_pairs={{0,112},{16,0},{32,16},{48,32},{64,48},{80,64},{96,80},{112,96},{1... | collective-permute-start | bytes 1625096 | tf_op jit(solution)/shard_map/while/body/eval_jaxpr/ppermute | solution.py:11
  80.7 9.4 collective-permute-done.1
  98.2 9.0 collective-permute-start.1
  107.2 8.2 collective-permute-done.1
  124.7 10.2 collective-permute-start.1
  134.9 8.2 collective-permute-done.1
  152.4 9.0 collective-permute-start.1
  161.4 8.2 collective-permute-done.1
  178.9 10.2 collective-permute-start.1
  189.1 8.2 collective-permute-done.1
  206.6 9.0 collective-permute-start.1
  215.6 8.2 collective-permute-done.1
  233.1 10.2 collective-permute-start.1
  243.4 8.2 collective-permute-done.1
  260.9 9.0 collective-permute-start.1
  269.9 7.9 collective-permute-done.1
  287.4 10.2 collective-permute-start.1
  297.6 7.9 collective-permute-done.1
  315.1 9.0 collective-permute-start.1
  324.1 7.9 collective-permute-done.1
  341.6 10.2 collective-permute-start.1
  351.8 7.9 collective-permute-done.1
  369.3 9.0 collective-permute-start.1
  395.8 10.2 collective-permute-start.1
  423.6 9.0 collective-permute-start.1
  450.1 10.2 collective-permute-start.1
  460.3 8.2 collective-permute-done.1
  498.8 9.1 collective-permute-done.12
  513.2 417.5 %while.39 = (s32[]{:T(128)}, f32[2,368,368]{1,0,2:T(2,128)}, bf16[2,368,368]{2,1,0:T(8,128)(2,1)S(1)}, bf16[2,368,368]{2,1,0:T(8,128)(2,1)S(1)}, s32[]{:T(128)},...) while((s32[]{:T(128)}, f32[2,368,368]{1,0,2:T(2,128)}, ...), condition=%wide.region_6.7_spmd, body=%wide.region_5.6_spmd.sunk | while | flops 199615008 | bytes 13849090 | solution.py:53
  513.2 17.0 %collective-permute-start.2 = (bf16[2,368,368]{2,1,0:T(8,128)(2,1)S(1)}, bf16[2,368,368]{2,1,0:T(8,128)(2,1)S(1)}, u32[]{:S(2)}, u32[]{:S(2)}) collective-permute-start(bf16[2,368,368]{2,1,0:T(8,128)(2,1)S(1)} %get-tuple-element.447), channel_id=1, source_target_pairs={{0,15},{1,0},{2,1},{3,2},{4,3},{5,4},{6,5},{7,6},{8,7},{9,8},{10,9... | collective-permute-start | bytes 1625096 | tf_op jit(solution)/shard_map/while/body/eval_jaxpr/ppermute | solution.py:11
  530.2 8.3 collective-permute-start.3
  557.8 8.4 collective-permute-start.3
  583.6 9.1 collective-permute-start.3
  592.8 8.2 collective-permute-done.3
  610.3 10.1 collective-permute-start.3
  620.4 8.2 collective-permute-done.3
  637.9 9.1 collective-permute-start.3
  647.0 8.2 collective-permute-done.3
  664.5 10.1 collective-permute-start.3
  674.6 8.2 collective-permute-done.3
  692.1 9.1 collective-permute-start.3
  701.2 8.2 collective-permute-done.3
  718.7 10.1 collective-permute-start.3
  728.8 8.2 collective-permute-done.3
  746.3 9.1 collective-permute-start.3
  755.5 8.2 collective-permute-done.3
  773.0 10.1 collective-permute-start.3
  783.1 8.2 collective-permute-done.3
  800.6 9.1 collective-permute-start.3
  809.7 8.2 collective-permute-done.3
  827.2 10.1 collective-permute-start.3
  837.3 8.2 collective-permute-done.3
  854.8 9.1 collective-permute-start.3
  863.9 8.2 collective-permute-done.3
  881.4 10.1 collective-permute-start.3
  891.5 8.2 collective-permute-done.3
  909.0 9.1 collective-permute-start.3
  918.2 8.2 collective-permute-done.3
  947.2 27.8 %scatter_fusion = bf16[128,12,529]{2,0,1:T(8,128)(2,1)S(1)} fusion(bf16[128,12,529]{2,0,1:T(8,128)(2,1)S(1)} %broadcast_in_dim.18, s32[512]{0:T(512)S(1)} %bitcast.110, bf16[512,529]{1,0:T(8,128)(2,1)S(1)} %copy-done.3), kind=kCustom, calls=%fused_computation | custom fusion | bytes 1629184 | tf_op jit(solution)/shard_map/scatter | solution.py:86
  976.2 54.3 %all_to_all.5 = bf16[128,12,529]{2,1,0:T(8,128)(2,1)S(1)} all-to-all(bf16[128,12,529]{2,1,0:T(8,128)(2,1)S(1)} %copy.54), channel_id=1, replica_groups=mesh['row'=8,'col'=16] {'row','col'}, dimensions={0} | all-to-all | bytes 3250176 | tf_op jit(solution)/shard_map/all_to_all | solution.py:87
  (288 shorter events, 395.4 us)
Async XLA Ops:
  4.2 17.5 %collective-permute-start.7 = (bf16[2,368,368]{1,0,2:T(2,128)(2,1)S(1)}, bf16[2,368,368]{1,0,2:T(2,128)(2,1)S(1)}, u32[]{:S(2)}, u32[]{:S(2)}) collective-permute-start(bf16[2,368,368]{1,0,2:T(2,128)(2,1)S(1)} %bitcast_multiply_fusion.1), channel_id=1, source_target_pairs={{0,112},{16,0},{32,16},{48,32},{64,48},{80,64},{96,80},{112,96},{1... | collective-permute-start | bytes 1625096 | tf_op jit(solution)/shard_map/ppermute | solution.py:11
  21.8 14.3 %collective-permute-start.8 = (bf16[2,368,368]{1,0,2:T(2,128)(2,1)S(1)}, bf16[2,368,368]{1,0,2:T(2,128)(2,1)S(1)}, u32[]{:S(2)}, u32[]{:S(2)}) collective-permute-start(bf16[2,368,368]{1,0,2:T(2,128)(2,1)S(1)} %bitcast.119), channel_id=1, source_target_pairs={{0,96},{16,112},{32,0},{48,16},{64,32},{80,48},{96,64},{112,80},{1... | collective-permute-start | bytes 1625096 | tf_op jit(solution)/shard_map/ppermute | solution.py:11
  24.3 14.1 %collective-permute-start.5 = (bf16[2,368,368]{1,0,2:T(2,128)(2,1)S(1)}, bf16[2,368,368]{1,0,2:T(2,128)(2,1)S(1)}, u32[]{:S(2)}, u32[]{:S(2)}) collective-permute-start(bf16[2,368,368]{1,0,2:T(2,128)(2,1)S(1)} %bitcast.118), channel_id=1, source_target_pairs={{0,14},{1,15},{2,0},{3,1},{4,2},{5,3},{6,4},{7,5},{8,6},{9,7},{10,... | collective-permute-start | bytes 1625096 | tf_op jit(solution)/shard_map/ppermute | solution.py:11
  36.2 16.6 %collective-permute-start.9 = (bf16[2,368,368]{1,0,2:T(2,128)(2,1)S(1)}, bf16[2,368,368]{1,0,2:T(2,128)(2,1)S(1)}, u32[]{:S(2)}, u32[]{:S(2)}) collective-permute-start(bf16[2,368,368]{1,0,2:T(2,128)(2,1)S(1)} %bitcast.120), channel_id=1, source_target_pairs={{0,64},{16,80},{32,96},{48,112},{64,0},{80,16},{96,32},{112,48},{1... | collective-permute-start | bytes 1625096 | tf_op jit(solution)/shard_map/ppermute | solution.py:11
  38.6 17.2 %collective-permute-start.6 = (bf16[2,368,368]{1,0,2:T(2,128)(2,1)S(1)}, bf16[2,368,368]{1,0,2:T(2,128)(2,1)S(1)}, u32[]{:S(2)}, u32[]{:S(2)}) collective-permute-start(bf16[2,368,368]{1,0,2:T(2,128)(2,1)S(1)} %bitcast.121), channel_id=1, source_target_pairs={{0,12},{1,13},{2,14},{3,15},{4,0},{5,1},{6,2},{7,3},{8,4},{9,5},{1... | collective-permute-start | bytes 1625096 | tf_op jit(solution)/shard_map/ppermute | solution.py:11
  59.7 20.9 %collective-permute-start = (bf16[2,368,368]{2,1,0:T(8,128)(2,1)S(1)}, bf16[2,368,368]{2,1,0:T(8,128)(2,1)S(1)}, u32[]{:S(2)}, u32[]{:S(2)}) collective-permute-start(bf16[2,368,368]{2,1,0:T(8,128)(2,1)S(1)} %get-tuple-element.408), channel_id=1, source_target_pairs={{0,15},{1,0},{2,1},{3,2},{4,3},{5,4},{6,5},{7,6},{8,7},{9,8},{10,9... | collective-permute-start | bytes 1625096 | tf_op jit(solution)/shard_map/while/body/eval_jaxpr/ppermute | solution.py:11
  62.5 27.6 %collective-permute-start.1 = (bf16[2,368,368]{2,1,0:T(8,128)(2,1)S(1)}, bf16[2,368,368]{2,1,0:T(8,128)(2,1)S(1)}, u32[]{:S(2)}, u32[]{:S(2)}) collective-permute-start(bf16[2,368,368]{2,1,0:T(8,128)(2,1)S(1)} %get-tuple-element.409), channel_id=1, source_target_pairs={{0,112},{16,0},{32,16},{48,32},{64,48},{80,64},{96,80},{112,96},{1... | collective-permute-start | bytes 1625096 | tf_op jit(solution)/shard_map/while/body/eval_jaxpr/ppermute | solution.py:11
  98.2 17.2 %collective-permute-start.1 = (bf16[2,368,368]{2,1,0:T(8,128)(2,1)S(1)}, bf16[2,368,368]{2,1,0:T(8,128)(2,1)S(1)}, u32[]{:S(2)}, u32[]{:S(2)}) collective-permute-start(bf16[2,368,368]{2,1,0:T(8,128)(2,1)S(1)} %get-tuple-element.409), channel_id=1, source_target_pairs={{0,112},{16,0},{32,16},{48,32},{64,48},{80,64},{96,80},{112,96},{1... | collective-permute-start | bytes 1625096 | tf_op jit(solution)/shard_map/while/body/eval_jaxpr/ppermute | solution.py:11
  119.7 15.2 %collective-permute-start = (bf16[2,368,368]{2,1,0:T(8,128)(2,1)S(1)}, bf16[2,368,368]{2,1,0:T(8,128)(2,1)S(1)}, u32[]{:S(2)}, u32[]{:S(2)}) collective-permute-start(bf16[2,368,368]{2,1,0:T(8,128)(2,1)S(1)} %get-tuple-element.408), channel_id=1, source_target_pairs={{0,15},{1,0},{2,1},{3,2},{4,3},{5,4},{6,5},{7,6},{8,7},{9,8},{10,9... | collective-permute-start | bytes 1625096 | tf_op jit(solution)/shard_map/while/body/eval_jaxpr/ppermute | solution.py:11
  124.7 18.4 %collective-permute-start.1 = (bf16[2,368,368]{2,1,0:T(8,128)(2,1)S(1)}, bf16[2,368,368]{2,1,0:T(8,128)(2,1)S(1)}, u32[]{:S(2)}, u32[]{:S(2)}) collective-permute-start(bf16[2,368,368]{2,1,0:T(8,128)(2,1)S(1)} %get-tuple-element.409), channel_id=1, source_target_pairs={{0,112},{16,0},{32,16},{48,32},{64,48},{80,64},{96,80},{112,96},{1... | collective-permute-start | bytes 1625096 | tf_op jit(solution)/shard_map/while/body/eval_jaxpr/ppermute | solution.py:11
  147.4 14.0 %collective-permute-start = (bf16[2,368,368]{2,1,0:T(8,128)(2,1)S(1)}, bf16[2,368,368]{2,1,0:T(8,128)(2,1)S(1)}, u32[]{:S(2)}, u32[]{:S(2)}) collective-permute-start(bf16[2,368,368]{2,1,0:T(8,128)(2,1)S(1)} %get-tuple-element.408), channel_id=1, source_target_pairs={{0,15},{1,0},{2,1},{3,2},{4,3},{5,4},{6,5},{7,6},{8,7},{9,8},{10,9... | collective-permute-start | bytes 1625096 | tf_op jit(solution)/shard_map/while/body/eval_jaxpr/ppermute | solution.py:11
  152.4 17.2 %collective-permute-start.1 = (bf16[2,368,368]{2,1,0:T(8,128)(2,1)S(1)}, bf16[2,368,368]{2,1,0:T(8,128)(2,1)S(1)}, u32[]{:S(2)}, u32[]{:S(2)}) collective-permute-start(bf16[2,368,368]{2,1,0:T(8,128)(2,1)S(1)} %get-tuple-element.409), channel_id=1, source_target_pairs={{0,112},{16,0},{32,16},{48,32},{64,48},{80,64},{96,80},{112,96},{1... | collective-permute-start | bytes 1625096 | tf_op jit(solution)/shard_map/while/body/eval_jaxpr/ppermute | solution.py:11
  173.9 15.2 %collective-permute-start = (bf16[2,368,368]{2,1,0:T(8,128)(2,1)S(1)}, bf16[2,368,368]{2,1,0:T(8,128)(2,1)S(1)}, u32[]{:S(2)}, u32[]{:S(2)}) collective-permute-start(bf16[2,368,368]{2,1,0:T(8,128)(2,1)S(1)} %get-tuple-element.408), channel_id=1, source_target_pairs={{0,15},{1,0},{2,1},{3,2},{4,3},{5,4},{6,5},{7,6},{8,7},{9,8},{10,9... | collective-permute-start | bytes 1625096 | tf_op jit(solution)/shard_map/while/body/eval_jaxpr/ppermute | solution.py:11
  178.9 18.4 %collective-permute-start.1 = (bf16[2,368,368]{2,1,0:T(8,128)(2,1)S(1)}, bf16[2,368,368]{2,1,0:T(8,128)(2,1)S(1)}, u32[]{:S(2)}, u32[]{:S(2)}) collective-permute-start(bf16[2,368,368]{2,1,0:T(8,128)(2,1)S(1)} %get-tuple-element.409), channel_id=1, source_target_pairs={{0,112},{16,0},{32,16},{48,32},{64,48},{80,64},{96,80},{112,96},{1... | collective-permute-start | bytes 1625096 | tf_op jit(solution)/shard_map/while/body/eval_jaxpr/ppermute | solution.py:11
  201.7 14.0 %collective-permute-start = (bf16[2,368,368]{2,1,0:T(8,128)(2,1)S(1)}, bf16[2,368,368]{2,1,0:T(8,128)(2,1)S(1)}, u32[]{:S(2)}, u32[]{:S(2)}) collective-permute-start(bf16[2,368,368]{2,1,0:T(8,128)(2,1)S(1)} %get-tuple-element.408), channel_id=1, source_target_pairs={{0,15},{1,0},{2,1},{3,2},{4,3},{5,4},{6,5},{7,6},{8,7},{9,8},{10,9... | collective-permute-start | bytes 1625096 | tf_op jit(solution)/shard_map/while/body/eval_jaxpr/ppermute | solution.py:11
  206.6 17.2 %collective-permute-start.1 = (bf16[2,368,368]{2,1,0:T(8,128)(2,1)S(1)}, bf16[2,368,368]{2,1,0:T(8,128)(2,1)S(1)}, u32[]{:S(2)}, u32[]{:S(2)}) collective-permute-start(bf16[2,368,368]{2,1,0:T(8,128)(2,1)S(1)} %get-tuple-element.409), channel_id=1, source_target_pairs={{0,112},{16,0},{32,16},{48,32},{64,48},{80,64},{96,80},{112,96},{1... | collective-permute-start | bytes 1625096 | tf_op jit(solution)/shard_map/while/body/eval_jaxpr/ppermute | solution.py:11
  228.2 15.2 %collective-permute-start = (bf16[2,368,368]{2,1,0:T(8,128)(2,1)S(1)}, bf16[2,368,368]{2,1,0:T(8,128)(2,1)S(1)}, u32[]{:S(2)}, u32[]{:S(2)}) collective-permute-start(bf16[2,368,368]{2,1,0:T(8,128)(2,1)S(1)} %get-tuple-element.408), channel_id=1, source_target_pairs={{0,15},{1,0},{2,1},{3,2},{4,3},{5,4},{6,5},{7,6},{8,7},{9,8},{10,9... | collective-permute-start | bytes 1625096 | tf_op jit(solution)/shard_map/while/body/eval_jaxpr/ppermute | solution.py:11
  233.1 18.4 %collective-permute-start.1 = (bf16[2,368,368]{2,1,0:T(8,128)(2,1)S(1)}, bf16[2,368,368]{2,1,0:T(8,128)(2,1)S(1)}, u32[]{:S(2)}, u32[]{:S(2)}) collective-permute-start(bf16[2,368,368]{2,1,0:T(8,128)(2,1)S(1)} %get-tuple-element.409), channel_id=1, source_target_pairs={{0,112},{16,0},{32,16},{48,32},{64,48},{80,64},{96,80},{112,96},{1... | collective-permute-start | bytes 1625096 | tf_op jit(solution)/shard_map/while/body/eval_jaxpr/ppermute | solution.py:11
  255.9 14.0 %collective-permute-start = (bf16[2,368,368]{2,1,0:T(8,128)(2,1)S(1)}, bf16[2,368,368]{2,1,0:T(8,128)(2,1)S(1)}, u32[]{:S(2)}, u32[]{:S(2)}) collective-permute-start(bf16[2,368,368]{2,1,0:T(8,128)(2,1)S(1)} %get-tuple-element.408), channel_id=1, source_target_pairs={{0,15},{1,0},{2,1},{3,2},{4,3},{5,4},{6,5},{7,6},{8,7},{9,8},{10,9... | collective-permute-start | bytes 1625096 | tf_op jit(solution)/shard_map/while/body/eval_jaxpr/ppermute | solution.py:11
  260.9 16.9 %collective-permute-start.1 = (bf16[2,368,368]{2,1,0:T(8,128)(2,1)S(1)}, bf16[2,368,368]{2,1,0:T(8,128)(2,1)S(1)}, u32[]{:S(2)}, u32[]{:S(2)}) collective-permute-start(bf16[2,368,368]{2,1,0:T(8,128)(2,1)S(1)} %get-tuple-element.409), channel_id=1, source_target_pairs={{0,112},{16,0},{32,16},{48,32},{64,48},{80,64},{96,80},{112,96},{1... | collective-permute-start | bytes 1625096 | tf_op jit(solution)/shard_map/while/body/eval_jaxpr/ppermute | solution.py:11
  282.1 15.5 %collective-permute-start = (bf16[2,368,368]{2,1,0:T(8,128)(2,1)S(1)}, bf16[2,368,368]{2,1,0:T(8,128)(2,1)S(1)}, u32[]{:S(2)}, u32[]{:S(2)}) collective-permute-start(bf16[2,368,368]{2,1,0:T(8,128)(2,1)S(1)} %get-tuple-element.408), channel_id=1, source_target_pairs={{0,15},{1,0},{2,1},{3,2},{4,3},{5,4},{6,5},{7,6},{8,7},{9,8},{10,9... | collective-permute-start | bytes 1625096 | tf_op jit(solution)/shard_map/while/body/eval_jaxpr/ppermute | solution.py:11
  287.4 18.1 %collective-permute-start.1 = (bf16[2,368,368]{2,1,0:T(8,128)(2,1)S(1)}, bf16[2,368,368]{2,1,0:T(8,128)(2,1)S(1)}, u32[]{:S(2)}, u32[]{:S(2)}) collective-permute-start(bf16[2,368,368]{2,1,0:T(8,128)(2,1)S(1)} %get-tuple-element.409), channel_id=1, source_target_pairs={{0,112},{16,0},{32,16},{48,32},{64,48},{80,64},{96,80},{112,96},{1... | collective-permute-start | bytes 1625096 | tf_op jit(solution)/shard_map/while/body/eval_jaxpr/ppermute | solution.py:11
  309.8 14.3 %collective-permute-start = (bf16[2,368,368]{2,1,0:T(8,128)(2,1)S(1)}, bf16[2,368,368]{2,1,0:T(8,128)(2,1)S(1)}, u32[]{:S(2)}, u32[]{:S(2)}) collective-permute-start(bf16[2,368,368]{2,1,0:T(8,128)(2,1)S(1)} %get-tuple-element.408), channel_id=1, source_target_pairs={{0,15},{1,0},{2,1},{3,2},{4,3},{5,4},{6,5},{7,6},{8,7},{9,8},{10,9... | collective-permute-start | bytes 1625096 | tf_op jit(solution)/shard_map/while/body/eval_jaxpr/ppermute | solution.py:11
  315.1 16.9 %collective-permute-start.1 = (bf16[2,368,368]{2,1,0:T(8,128)(2,1)S(1)}, bf16[2,368,368]{2,1,0:T(8,128)(2,1)S(1)}, u32[]{:S(2)}, u32[]{:S(2)}) collective-permute-start(bf16[2,368,368]{2,1,0:T(8,128)(2,1)S(1)} %get-tuple-element.409), channel_id=1, source_target_pairs={{0,112},{16,0},{32,16},{48,32},{64,48},{80,64},{96,80},{112,96},{1... | collective-permute-start | bytes 1625096 | tf_op jit(solution)/shard_map/while/body/eval_jaxpr/ppermute | solution.py:11
  336.3 15.5 %collective-permute-start = (bf16[2,368,368]{2,1,0:T(8,128)(2,1)S(1)}, bf16[2,368,368]{2,1,0:T(8,128)(2,1)S(1)}, u32[]{:S(2)}, u32[]{:S(2)}) collective-permute-start(bf16[2,368,368]{2,1,0:T(8,128)(2,1)S(1)} %get-tuple-element.408), channel_id=1, source_target_pairs={{0,15},{1,0},{2,1},{3,2},{4,3},{5,4},{6,5},{7,6},{8,7},{9,8},{10,9... | collective-permute-start | bytes 1625096 | tf_op jit(solution)/shard_map/while/body/eval_jaxpr/ppermute | solution.py:11
  341.6 18.1 %collective-permute-start.1 = (bf16[2,368,368]{2,1,0:T(8,128)(2,1)S(1)}, bf16[2,368,368]{2,1,0:T(8,128)(2,1)S(1)}, u32[]{:S(2)}, u32[]{:S(2)}) collective-permute-start(bf16[2,368,368]{2,1,0:T(8,128)(2,1)S(1)} %get-tuple-element.409), channel_id=1, source_target_pairs={{0,112},{16,0},{32,16},{48,32},{64,48},{80,64},{96,80},{112,96},{1... | collective-permute-start | bytes 1625096 | tf_op jit(solution)/shard_map/while/body/eval_jaxpr/ppermute | solution.py:11
  364.1 14.3 %collective-permute-start = (bf16[2,368,368]{2,1,0:T(8,128)(2,1)S(1)}, bf16[2,368,368]{2,1,0:T(8,128)(2,1)S(1)}, u32[]{:S(2)}, u32[]{:S(2)}) collective-permute-start(bf16[2,368,368]{2,1,0:T(8,128)(2,1)S(1)} %get-tuple-element.408), channel_id=1, source_target_pairs={{0,15},{1,0},{2,1},{3,2},{4,3},{5,4},{6,5},{7,6},{8,7},{9,8},{10,9... | collective-permute-start | bytes 1625096 | tf_op jit(solution)/shard_map/while/body/eval_jaxpr/ppermute | solution.py:11
  369.3 16.9 %collective-permute-start.1 = (bf16[2,368,368]{2,1,0:T(8,128)(2,1)S(1)}, bf16[2,368,368]{2,1,0:T(8,128)(2,1)S(1)}, u32[]{:S(2)}, u32[]{:S(2)}) collective-permute-start(bf16[2,368,368]{2,1,0:T(8,128)(2,1)S(1)} %get-tuple-element.409), channel_id=1, source_target_pairs={{0,112},{16,0},{32,16},{48,32},{64,48},{80,64},{96,80},{112,96},{1... | collective-permute-start | bytes 1625096 | tf_op jit(solution)/shard_map/while/body/eval_jaxpr/ppermute | solution.py:11
  390.6 15.5 %collective-permute-start = (bf16[2,368,368]{2,1,0:T(8,128)(2,1)S(1)}, bf16[2,368,368]{2,1,0:T(8,128)(2,1)S(1)}, u32[]{:S(2)}, u32[]{:S(2)}) collective-permute-start(bf16[2,368,368]{2,1,0:T(8,128)(2,1)S(1)} %get-tuple-element.408), channel_id=1, source_target_pairs={{0,15},{1,0},{2,1},{3,2},{4,3},{5,4},{6,5},{7,6},{8,7},{9,8},{10,9... | collective-permute-start | bytes 1625096 | tf_op jit(solution)/shard_map/while/body/eval_jaxpr/ppermute | solution.py:11
  395.8 18.1 %collective-permute-start.1 = (bf16[2,368,368]{2,1,0:T(8,128)(2,1)S(1)}, bf16[2,368,368]{2,1,0:T(8,128)(2,1)S(1)}, u32[]{:S(2)}, u32[]{:S(2)}) collective-permute-start(bf16[2,368,368]{2,1,0:T(8,128)(2,1)S(1)} %get-tuple-element.409), channel_id=1, source_target_pairs={{0,112},{16,0},{32,16},{48,32},{64,48},{80,64},{96,80},{112,96},{1... | collective-permute-start | bytes 1625096 | tf_op jit(solution)/shard_map/while/body/eval_jaxpr/ppermute | solution.py:11
  418.3 14.3 %collective-permute-start = (bf16[2,368,368]{2,1,0:T(8,128)(2,1)S(1)}, bf16[2,368,368]{2,1,0:T(8,128)(2,1)S(1)}, u32[]{:S(2)}, u32[]{:S(2)}) collective-permute-start(bf16[2,368,368]{2,1,0:T(8,128)(2,1)S(1)} %get-tuple-element.408), channel_id=1, source_target_pairs={{0,15},{1,0},{2,1},{3,2},{4,3},{5,4},{6,5},{7,6},{8,7},{9,8},{10,9... | collective-permute-start | bytes 1625096 | tf_op jit(solution)/shard_map/while/body/eval_jaxpr/ppermute | solution.py:11
  423.6 16.9 %collective-permute-start.1 = (bf16[2,368,368]{2,1,0:T(8,128)(2,1)S(1)}, bf16[2,368,368]{2,1,0:T(8,128)(2,1)S(1)}, u32[]{:S(2)}, u32[]{:S(2)}) collective-permute-start(bf16[2,368,368]{2,1,0:T(8,128)(2,1)S(1)} %get-tuple-element.409), channel_id=1, source_target_pairs={{0,112},{16,0},{32,16},{48,32},{64,48},{80,64},{96,80},{112,96},{1... | collective-permute-start | bytes 1625096 | tf_op jit(solution)/shard_map/while/body/eval_jaxpr/ppermute | solution.py:11
  444.8 15.5 %collective-permute-start = (bf16[2,368,368]{2,1,0:T(8,128)(2,1)S(1)}, bf16[2,368,368]{2,1,0:T(8,128)(2,1)S(1)}, u32[]{:S(2)}, u32[]{:S(2)}) collective-permute-start(bf16[2,368,368]{2,1,0:T(8,128)(2,1)S(1)} %get-tuple-element.408), channel_id=1, source_target_pairs={{0,15},{1,0},{2,1},{3,2},{4,3},{5,4},{6,5},{7,6},{8,7},{9,8},{10,9... | collective-permute-start | bytes 1625096 | tf_op jit(solution)/shard_map/while/body/eval_jaxpr/ppermute | solution.py:11
  450.1 18.4 %collective-permute-start.1 = (bf16[2,368,368]{2,1,0:T(8,128)(2,1)S(1)}, bf16[2,368,368]{2,1,0:T(8,128)(2,1)S(1)}, u32[]{:S(2)}, u32[]{:S(2)}) collective-permute-start(bf16[2,368,368]{2,1,0:T(8,128)(2,1)S(1)} %get-tuple-element.409), channel_id=1, source_target_pairs={{0,112},{16,0},{32,16},{48,32},{64,48},{80,64},{96,80},{112,96},{1... | collective-permute-start | bytes 1625096 | tf_op jit(solution)/shard_map/while/body/eval_jaxpr/ppermute | solution.py:11
  513.2 25.3 %collective-permute-start.2 = (bf16[2,368,368]{2,1,0:T(8,128)(2,1)S(1)}, bf16[2,368,368]{2,1,0:T(8,128)(2,1)S(1)}, u32[]{:S(2)}, u32[]{:S(2)}) collective-permute-start(bf16[2,368,368]{2,1,0:T(8,128)(2,1)S(1)} %get-tuple-element.447), channel_id=1, source_target_pairs={{0,15},{1,0},{2,1},{3,2},{4,3},{5,4},{6,5},{7,6},{8,7},{9,8},{10,9... | collective-permute-start | bytes 1625096 | tf_op jit(solution)/shard_map/while/body/eval_jaxpr/ppermute | solution.py:11
  530.2 15.9 %collective-permute-start.3 = (bf16[2,368,368]{2,1,0:T(8,128)(2,1)S(1)}, bf16[2,368,368]{2,1,0:T(8,128)(2,1)S(1)}, u32[]{:S(2)}, u32[]{:S(2)}) collective-permute-start(bf16[2,368,368]{2,1,0:T(8,128)(2,1)S(1)} %get-tuple-element.448), channel_id=1, source_target_pairs={{0,112},{16,0},{32,16},{48,32},{64,48},{80,64},{96,80},{112,96},{1... | collective-permute-start | bytes 1625096 | tf_op jit(solution)/shard_map/while/body/eval_jaxpr/ppermute | solution.py:11
  550.4 15.7 %collective-permute-start.2 = (bf16[2,368,368]{2,1,0:T(8,128)(2,1)S(1)}, bf16[2,368,368]{2,1,0:T(8,128)(2,1)S(1)}, u32[]{:S(2)}, u32[]{:S(2)}) collective-permute-start(bf16[2,368,368]{2,1,0:T(8,128)(2,1)S(1)} %get-tuple-element.447), channel_id=1, source_target_pairs={{0,15},{1,0},{2,1},{3,2},{4,3},{5,4},{6,5},{7,6},{8,7},{9,8},{10,9... | collective-permute-start | bytes 1625096 | tf_op jit(solution)/shard_map/while/body/eval_jaxpr/ppermute | solution.py:11
  557.8 16.2 %collective-permute-start.3 = (bf16[2,368,368]{2,1,0:T(8,128)(2,1)S(1)}, bf16[2,368,368]{2,1,0:T(8,128)(2,1)S(1)}, u32[]{:S(2)}, u32[]{:S(2)}) collective-permute-start(bf16[2,368,368]{2,1,0:T(8,128)(2,1)S(1)} %get-tuple-element.448), channel_id=1, source_target_pairs={{0,112},{16,0},{32,16},{48,32},{64,48},{80,64},{96,80},{112,96},{1... | collective-permute-start | bytes 1625096 | tf_op jit(solution)/shard_map/while/body/eval_jaxpr/ppermute | solution.py:11
  578.4 14.4 %collective-permute-start.2 = (bf16[2,368,368]{2,1,0:T(8,128)(2,1)S(1)}, bf16[2,368,368]{2,1,0:T(8,128)(2,1)S(1)}, u32[]{:S(2)}, u32[]{:S(2)}) collective-permute-start(bf16[2,368,368]{2,1,0:T(8,128)(2,1)S(1)} %get-tuple-element.447), channel_id=1, source_target_pairs={{0,15},{1,0},{2,1},{3,2},{4,3},{5,4},{6,5},{7,6},{8,7},{9,8},{10,9... | collective-permute-start | bytes 1625096 | tf_op jit(solution)/shard_map/while/body/eval_jaxpr/ppermute | solution.py:11
  583.6 17.3 %collective-permute-start.3 = (bf16[2,368,368]{2,1,0:T(8,128)(2,1)S(1)}, bf16[2,368,368]{2,1,0:T(8,128)(2,1)S(1)}, u32[]{:S(2)}, u32[]{:S(2)}) collective-permute-start(bf16[2,368,368]{2,1,0:T(8,128)(2,1)S(1)} %get-tuple-element.448), channel_id=1, source_target_pairs={{0,112},{16,0},{32,16},{48,32},{64,48},{80,64},{96,80},{112,96},{1... | collective-permute-start | bytes 1625096 | tf_op jit(solution)/shard_map/while/body/eval_jaxpr/ppermute | solution.py:11
  605.3 15.1 %collective-permute-start.2 = (bf16[2,368,368]{2,1,0:T(8,128)(2,1)S(1)}, bf16[2,368,368]{2,1,0:T(8,128)(2,1)S(1)}, u32[]{:S(2)}, u32[]{:S(2)}) collective-permute-start(bf16[2,368,368]{2,1,0:T(8,128)(2,1)S(1)} %get-tuple-element.447), channel_id=1, source_target_pairs={{0,15},{1,0},{2,1},{3,2},{4,3},{5,4},{6,5},{7,6},{8,7},{9,8},{10,9... | collective-permute-start | bytes 1625096 | tf_op jit(solution)/shard_map/while/body/eval_jaxpr/ppermute | solution.py:11
  610.3 18.3 %collective-permute-start.3 = (bf16[2,368,368]{2,1,0:T(8,128)(2,1)S(1)}, bf16[2,368,368]{2,1,0:T(8,128)(2,1)S(1)}, u32[]{:S(2)}, u32[]{:S(2)}) collective-permute-start(bf16[2,368,368]{2,1,0:T(8,128)(2,1)S(1)} %get-tuple-element.448), channel_id=1, source_target_pairs={{0,112},{16,0},{32,16},{48,32},{64,48},{80,64},{96,80},{112,96},{1... | collective-permute-start | bytes 1625096 | tf_op jit(solution)/shard_map/while/body/eval_jaxpr/ppermute | solution.py:11
  632.9 14.1 %collective-permute-start.2 = (bf16[2,368,368]{2,1,0:T(8,128)(2,1)S(1)}, bf16[2,368,368]{2,1,0:T(8,128)(2,1)S(1)}, u32[]{:S(2)}, u32[]{:S(2)}) collective-permute-start(bf16[2,368,368]{2,1,0:T(8,128)(2,1)S(1)} %get-tuple-element.447), channel_id=1, source_target_pairs={{0,15},{1,0},{2,1},{3,2},{4,3},{5,4},{6,5},{7,6},{8,7},{9,8},{10,9... | collective-permute-start | bytes 1625096 | tf_op jit(solution)/shard_map/while/body/eval_jaxpr/ppermute | solution.py:11
  637.9 17.3 %collective-permute-start.3 = (bf16[2,368,368]{2,1,0:T(8,128)(2,1)S(1)}, bf16[2,368,368]{2,1,0:T(8,128)(2,1)S(1)}, u32[]{:S(2)}, u32[]{:S(2)}) collective-permute-start(bf16[2,368,368]{2,1,0:T(8,128)(2,1)S(1)} %get-tuple-element.448), channel_id=1, source_target_pairs={{0,112},{16,0},{32,16},{48,32},{64,48},{80,64},{96,80},{112,96},{1... | collective-permute-start | bytes 1625096 | tf_op jit(solution)/shard_map/while/body/eval_jaxpr/ppermute | solution.py:11
  659.5 15.1 %collective-permute-start.2 = (bf16[2,368,368]{2,1,0:T(8,128)(2,1)S(1)}, bf16[2,368,368]{2,1,0:T(8,128)(2,1)S(1)}, u32[]{:S(2)}, u32[]{:S(2)}) collective-permute-start(bf16[2,368,368]{2,1,0:T(8,128)(2,1)S(1)} %get-tuple-element.447), channel_id=1, source_target_pairs={{0,15},{1,0},{2,1},{3,2},{4,3},{5,4},{6,5},{7,6},{8,7},{9,8},{10,9... | collective-permute-start | bytes 1625096 | tf_op jit(solution)/shard_map/while/body/eval_jaxpr/ppermute | solution.py:11
  664.5 18.3 %collective-permute-start.3 = (bf16[2,368,368]{2,1,0:T(8,128)(2,1)S(1)}, bf16[2,368,368]{2,1,0:T(8,128)(2,1)S(1)}, u32[]{:S(2)}, u32[]{:S(2)}) collective-permute-start(bf16[2,368,368]{2,1,0:T(8,128)(2,1)S(1)} %get-tuple-element.448), channel_id=1, source_target_pairs={{0,112},{16,0},{32,16},{48,32},{64,48},{80,64},{96,80},{112,96},{1... | collective-permute-start | bytes 1625096 | tf_op jit(solution)/shard_map/while/body/eval_jaxpr/ppermute | solution.py:11
  687.1 14.1 %collective-permute-start.2 = (bf16[2,368,368]{2,1,0:T(8,128)(2,1)S(1)}, bf16[2,368,368]{2,1,0:T(8,128)(2,1)S(1)}, u32[]{:S(2)}, u32[]{:S(2)}) collective-permute-start(bf16[2,368,368]{2,1,0:T(8,128)(2,1)S(1)} %get-tuple-element.447), channel_id=1, source_target_pairs={{0,15},{1,0},{2,1},{3,2},{4,3},{5,4},{6,5},{7,6},{8,7},{9,8},{10,9... | collective-permute-start | bytes 1625096 | tf_op jit(solution)/shard_map/while/body/eval_jaxpr/ppermute | solution.py:11
  692.1 17.3 %collective-permute-start.3 = (bf16[2,368,368]{2,1,0:T(8,128)(2,1)S(1)}, bf16[2,368,368]{2,1,0:T(8,128)(2,1)S(1)}, u32[]{:S(2)}, u32[]{:S(2)}) collective-permute-start(bf16[2,368,368]{2,1,0:T(8,128)(2,1)S(1)} %get-tuple-element.448), channel_id=1, source_target_pairs={{0,112},{16,0},{32,16},{48,32},{64,48},{80,64},{96,80},{112,96},{1... | collective-permute-start | bytes 1625096 | tf_op jit(solution)/shard_map/while/body/eval_jaxpr/ppermute | solution.py:11
  713.8 15.1 %collective-permute-start.2 = (bf16[2,368,368]{2,1,0:T(8,128)(2,1)S(1)}, bf16[2,368,368]{2,1,0:T(8,128)(2,1)S(1)}, u32[]{:S(2)}, u32[]{:S(2)}) collective-permute-start(bf16[2,368,368]{2,1,0:T(8,128)(2,1)S(1)} %get-tuple-element.447), channel_id=1, source_target_pairs={{0,15},{1,0},{2,1},{3,2},{4,3},{5,4},{6,5},{7,6},{8,7},{9,8},{10,9... | collective-permute-start | bytes 1625096 | tf_op jit(solution)/shard_map/while/body/eval_jaxpr/ppermute | solution.py:11
  718.7 18.3 %collective-permute-start.3 = (bf16[2,368,368]{2,1,0:T(8,128)(2,1)S(1)}, bf16[2,368,368]{2,1,0:T(8,128)(2,1)S(1)}, u32[]{:S(2)}, u32[]{:S(2)}) collective-permute-start(bf16[2,368,368]{2,1,0:T(8,128)(2,1)S(1)} %get-tuple-element.448), channel_id=1, source_target_pairs={{0,112},{16,0},{32,16},{48,32},{64,48},{80,64},{96,80},{112,96},{1... | collective-permute-start | bytes 1625096 | tf_op jit(solution)/shard_map/while/body/eval_jaxpr/ppermute | solution.py:11
  741.4 14.1 %collective-permute-start.2 = (bf16[2,368,368]{2,1,0:T(8,128)(2,1)S(1)}, bf16[2,368,368]{2,1,0:T(8,128)(2,1)S(1)}, u32[]{:S(2)}, u32[]{:S(2)}) collective-permute-start(bf16[2,368,368]{2,1,0:T(8,128)(2,1)S(1)} %get-tuple-element.447), channel_id=1, source_target_pairs={{0,15},{1,0},{2,1},{3,2},{4,3},{5,4},{6,5},{7,6},{8,7},{9,8},{10,9... | collective-permute-start | bytes 1625096 | tf_op jit(solution)/shard_map/while/body/eval_jaxpr/ppermute | solution.py:11
  746.3 17.3 %collective-permute-start.3 = (bf16[2,368,368]{2,1,0:T(8,128)(2,1)S(1)}, bf16[2,368,368]{2,1,0:T(8,128)(2,1)S(1)}, u32[]{:S(2)}, u32[]{:S(2)}) collective-permute-start(bf16[2,368,368]{2,1,0:T(8,128)(2,1)S(1)} %get-tuple-element.448), channel_id=1, source_target_pairs={{0,112},{16,0},{32,16},{48,32},{64,48},{80,64},{96,80},{112,96},{1... | collective-permute-start | bytes 1625096 | tf_op jit(solution)/shard_map/while/body/eval_jaxpr/ppermute | solution.py:11
  768.0 15.1 %collective-permute-start.2 = (bf16[2,368,368]{2,1,0:T(8,128)(2,1)S(1)}, bf16[2,368,368]{2,1,0:T(8,128)(2,1)S(1)}, u32[]{:S(2)}, u32[]{:S(2)}) collective-permute-start(bf16[2,368,368]{2,1,0:T(8,128)(2,1)S(1)} %get-tuple-element.447), channel_id=1, source_target_pairs={{0,15},{1,0},{2,1},{3,2},{4,3},{5,4},{6,5},{7,6},{8,7},{9,8},{10,9... | collective-permute-start | bytes 1625096 | tf_op jit(solution)/shard_map/while/body/eval_jaxpr/ppermute | solution.py:11
  773.0 18.3 %collective-permute-start.3 = (bf16[2,368,368]{2,1,0:T(8,128)(2,1)S(1)}, bf16[2,368,368]{2,1,0:T(8,128)(2,1)S(1)}, u32[]{:S(2)}, u32[]{:S(2)}) collective-permute-start(bf16[2,368,368]{2,1,0:T(8,128)(2,1)S(1)} %get-tuple-element.448), channel_id=1, source_target_pairs={{0,112},{16,0},{32,16},{48,32},{64,48},{80,64},{96,80},{112,96},{1... | collective-permute-start | bytes 1625096 | tf_op jit(solution)/shard_map/while/body/eval_jaxpr/ppermute | solution.py:11
  795.6 14.1 %collective-permute-start.2 = (bf16[2,368,368]{2,1,0:T(8,128)(2,1)S(1)}, bf16[2,368,368]{2,1,0:T(8,128)(2,1)S(1)}, u32[]{:S(2)}, u32[]{:S(2)}) collective-permute-start(bf16[2,368,368]{2,1,0:T(8,128)(2,1)S(1)} %get-tuple-element.447), channel_id=1, source_target_pairs={{0,15},{1,0},{2,1},{3,2},{4,3},{5,4},{6,5},{7,6},{8,7},{9,8},{10,9... | collective-permute-start | bytes 1625096 | tf_op jit(solution)/shard_map/while/body/eval_jaxpr/ppermute | solution.py:11
  800.6 17.3 %collective-permute-start.3 = (bf16[2,368,368]{2,1,0:T(8,128)(2,1)S(1)}, bf16[2,368,368]{2,1,0:T(8,128)(2,1)S(1)}, u32[]{:S(2)}, u32[]{:S(2)}) collective-permute-start(bf16[2,368,368]{2,1,0:T(8,128)(2,1)S(1)} %get-tuple-element.448), channel_id=1, source_target_pairs={{0,112},{16,0},{32,16},{48,32},{64,48},{80,64},{96,80},{112,96},{1... | collective-permute-start | bytes 1625096 | tf_op jit(solution)/shard_map/while/body/eval_jaxpr/ppermute | solution.py:11
  822.2 15.1 %collective-permute-start.2 = (bf16[2,368,368]{2,1,0:T(8,128)(2,1)S(1)}, bf16[2,368,368]{2,1,0:T(8,128)(2,1)S(1)}, u32[]{:S(2)}, u32[]{:S(2)}) collective-permute-start(bf16[2,368,368]{2,1,0:T(8,128)(2,1)S(1)} %get-tuple-element.447), channel_id=1, source_target_pairs={{0,15},{1,0},{2,1},{3,2},{4,3},{5,4},{6,5},{7,6},{8,7},{9,8},{10,9... | collective-permute-start | bytes 1625096 | tf_op jit(solution)/shard_map/while/body/eval_jaxpr/ppermute | solution.py:11
  827.2 18.3 %collective-permute-start.3 = (bf16[2,368,368]{2,1,0:T(8,128)(2,1)S(1)}, bf16[2,368,368]{2,1,0:T(8,128)(2,1)S(1)}, u32[]{:S(2)}, u32[]{:S(2)}) collective-permute-start(bf16[2,368,368]{2,1,0:T(8,128)(2,1)S(1)} %get-tuple-element.448), channel_id=1, source_target_pairs={{0,112},{16,0},{32,16},{48,32},{64,48},{80,64},{96,80},{112,96},{1... | collective-permute-start | bytes 1625096 | tf_op jit(solution)/shard_map/while/body/eval_jaxpr/ppermute | solution.py:11
  849.8 14.1 %collective-permute-start.2 = (bf16[2,368,368]{2,1,0:T(8,128)(2,1)S(1)}, bf16[2,368,368]{2,1,0:T(8,128)(2,1)S(1)}, u32[]{:S(2)}, u32[]{:S(2)}) collective-permute-start(bf16[2,368,368]{2,1,0:T(8,128)(2,1)S(1)} %get-tuple-element.447), channel_id=1, source_target_pairs={{0,15},{1,0},{2,1},{3,2},{4,3},{5,4},{6,5},{7,6},{8,7},{9,8},{10,9... | collective-permute-start | bytes 1625096 | tf_op jit(solution)/shard_map/while/body/eval_jaxpr/ppermute | solution.py:11
  854.8 17.3 %collective-permute-start.3 = (bf16[2,368,368]{2,1,0:T(8,128)(2,1)S(1)}, bf16[2,368,368]{2,1,0:T(8,128)(2,1)S(1)}, u32[]{:S(2)}, u32[]{:S(2)}) collective-permute-start(bf16[2,368,368]{2,1,0:T(8,128)(2,1)S(1)} %get-tuple-element.448), channel_id=1, source_target_pairs={{0,112},{16,0},{32,16},{48,32},{64,48},{80,64},{96,80},{112,96},{1... | collective-permute-start | bytes 1625096 | tf_op jit(solution)/shard_map/while/body/eval_jaxpr/ppermute | solution.py:11
  876.5 15.1 %collective-permute-start.2 = (bf16[2,368,368]{2,1,0:T(8,128)(2,1)S(1)}, bf16[2,368,368]{2,1,0:T(8,128)(2,1)S(1)}, u32[]{:S(2)}, u32[]{:S(2)}) collective-permute-start(bf16[2,368,368]{2,1,0:T(8,128)(2,1)S(1)} %get-tuple-element.447), channel_id=1, source_target_pairs={{0,15},{1,0},{2,1},{3,2},{4,3},{5,4},{6,5},{7,6},{8,7},{9,8},{10,9... | collective-permute-start | bytes 1625096 | tf_op jit(solution)/shard_map/while/body/eval_jaxpr/ppermute | solution.py:11
  881.4 18.3 %collective-permute-start.3 = (bf16[2,368,368]{2,1,0:T(8,128)(2,1)S(1)}, bf16[2,368,368]{2,1,0:T(8,128)(2,1)S(1)}, u32[]{:S(2)}, u32[]{:S(2)}) collective-permute-start(bf16[2,368,368]{2,1,0:T(8,128)(2,1)S(1)} %get-tuple-element.448), channel_id=1, source_target_pairs={{0,112},{16,0},{32,16},{48,32},{64,48},{80,64},{96,80},{112,96},{1... | collective-permute-start | bytes 1625096 | tf_op jit(solution)/shard_map/while/body/eval_jaxpr/ppermute | solution.py:11
  904.1 14.1 %collective-permute-start.2 = (bf16[2,368,368]{2,1,0:T(8,128)(2,1)S(1)}, bf16[2,368,368]{2,1,0:T(8,128)(2,1)S(1)}, u32[]{:S(2)}, u32[]{:S(2)}) collective-permute-start(bf16[2,368,368]{2,1,0:T(8,128)(2,1)S(1)} %get-tuple-element.447), channel_id=1, source_target_pairs={{0,15},{1,0},{2,1},{3,2},{4,3},{5,4},{6,5},{7,6},{8,7},{9,8},{10,9... | collective-permute-start | bytes 1625096 | tf_op jit(solution)/shard_map/while/body/eval_jaxpr/ppermute | solution.py:11
  909.0 17.3 %collective-permute-start.3 = (bf16[2,368,368]{2,1,0:T(8,128)(2,1)S(1)}, bf16[2,368,368]{2,1,0:T(8,128)(2,1)S(1)}, u32[]{:S(2)}, u32[]{:S(2)}) collective-permute-start(bf16[2,368,368]{2,1,0:T(8,128)(2,1)S(1)} %get-tuple-element.448), channel_id=1, source_target_pairs={{0,112},{16,0},{32,16},{48,32},{64,48},{80,64},{96,80},{112,96},{1... | collective-permute-start | bytes 1625096 | tf_op jit(solution)/shard_map/while/body/eval_jaxpr/ppermute | solution.py:11
  (11 other events, 95.5 us)
where the time goes:
time: 1040 us; the launch traced here: 1030 us
  starting transfers between devices  481 us (46%)
  waiting for transfers between devices  299 us (29%)
  other arithmetic  91.6 us (9%)
  local copies, waits for them, and re-layouts  90.3 us (9%)
  blocking collectives  54.3 us (5%)
  matrix products  16.3 us (2%)
    ppermute x69, starting transfers between devices, passed_along(): lax.ppermute(value, axis, [(i, (i + by) % count) for i in range(count)])  481 us
    ppermute x69, waiting for transfers between devices, passed_along(): lax.ppermute(value, axis, [(i, (i + by) % count) for i in range(count)])  299 us
    add x30, other arithmetic, multiply(): return total + term.reshape(2, width, width)  85.1 us
    all_to_all x1, blocking collectives, per_device(): lax.all_to_all(outgoing, ('row', 'col'), split_axis=0, concat_axis=0, til...  54.3 us
    scatter x2, local copies, waits for them, and re-layouts, per_device(): jnp.zeros((devices, capacity, BS * BS), jnp.bfloat16).at[targets, slots]  29 us
    reshape x30, local copies, waits for them, and re-layouts, multiply(): return total + term.reshape(2, width, width)  26.3 us
  transfers between devices with their start and end apart: 69, of which 37 were waited for; matrix products, arithmetic and copies ran while one was open for 0% of the time, Pallas kernels for 0%

commit v1 on v0

v1 whole, which is shorter than its diff:
```python
import jax
import jax.numpy as jnp
from jax import lax
from jax.experimental import pallas as pl
from jax.experimental.pallas import tpu as pltpu
from jax.sharding import PartitionSpec as P

BS = 23
PB = 16
W = BS * PB
WP = 384
ORDER = 5888
NROW = 8
NCOL = 16
DEVICES = NROW * NCOL
CAP = 12
CAPP = 16
ENT = BS * BS
ENTP = 640
MESH = pl.DeviceIdType.MESH
F32 = jnp.float32
BF16 = jnp.bfloat16


def grow_columns(mask):
    block = lax.broadcasted_iota(jnp.int32, (PB, WP), 0)
    col = lax.broadcasted_iota(jnp.int32, (PB, WP), 1)
    spread = jnp.where((col >= block * BS) & (col < block * BS + BS), 1.0, 0.0).astype(BF16)
    return jnp.dot(mask, spread, preferred_element_type=F32).astype(BF16)


def grow(mask):
    wide = grow_columns(mask.astype(F32).astype(BF16))
    row = lax.broadcasted_iota(jnp.int32, (W, PB), 0)
    block = lax.broadcasted_iota(jnp.int32, (W, PB), 1)
    spread = jnp.where((row >= block * BS) & (row < block * BS + BS), 1.0, 0.0).astype(BF16)
    return jnp.dot(spread, wide, preferred_element_type=F32)


def products(dens, pat, keep, out, left, right, sq, relay, mask, acc, send, recv):
    r = lax.axis_index("row")
    c = lax.axis_index("col")
    x, yh = lax.rem(r, 4), lax.div(r, 4)
    z, yl, core = lax.div(c, 4), lax.rem(lax.div(c, 2), 2), lax.rem(c, 2)

    def col(dz, dyl, dcore):
        ycol = (1 - yl) if dyl else yl
        ccol = (1 - core) if dcore else core
        return lax.rem(z + dz + 4, 4) * 4 + ycol * 2 + ccol

    def row(dx, dyh):
        yrow = (1 - yh) if dyh else yh
        return yrow * 4 + lax.rem(x + dx + 4, 4)

    sib = (r, col(0, 0, 1))
    ya = (r, col(0, 1, 0))
    yb = (row(0, 1), col(0, 1, 0))
    zs = {1: (r, col(1, 0, 0)), -1: (r, col(-1, 0, 0))}
    xs = {1: (row(1, 0), c), -1: (row(-1, 0), c)}

    numbers = {}
    started = {}
    arriving = {}

    def at(buf, slot, h):
        return buf.at[slot, h, pl.ds(0, W)]

    def copy(name, src, dst, dev, here):
        k = numbers.setdefault(name, len(numbers))
        op = pltpu.make_async_remote_copy(
            src_ref=src, dst_ref=dst, send_sem=send.at[k], recv_sem=recv.at[k],
            device_id=dev, device_id_type=MESH)
        op.start()
        started[name] = op
        arriving[name] = pltpu.make_async_remote_copy(
            src_ref=here, dst_ref=here, send_sem=send.at[k], recv_sem=recv.at[k],
            device_id=dev, device_id_type=MESH)

    def got(name):
        arriving[name].wait_recv()

    barrier = pltpu.get_barrier_semaphore()
    for dev in (sib, ya, yb, zs[1], zs[-1], xs[1], xs[-1]):
        pl.semaphore_signal(barrier, inc=1, device_id=dev, device_id_type=MESH)

    for h in range(2):
        m = grow(pat[h])
        mask[h] = m.astype(BF16)
        left[c, h, :, pl.ds(256, 128)] = jnp.zeros((W, 128), BF16)
        left[c, h, :, pl.ds(0, W)] = dens[h] * m[:, :W].astype(BF16)
        right[r, h, pl.ds(0, W)] = left[c, h]
    zero = jnp.zeros((2, WP - W, WP), BF16)

    def clear(k, carry):
        right[k, :, pl.ds(W, WP - W)] = zero
        sq[k, :, pl.ds(W, WP - W)] = zero
        return carry

    lax.fori_loop(0, NROW, clear, 0)
    pl.semaphore_wait(barrier, 7)

    def send_left(name, h, dev, there, here):
        s = col(*there)
        copy((name, h), at(left, s, h), at(left, s, h), dev, at(left, col(*here), h))

    def send_sib(h, dz, dyl):
        send_left(("c", dz, dyl), h, sib, (dz, dyl, 0), (dz, dyl, 1))

    def send_row(buf, name, h, dev, there, here):
        s = row(*there)
        copy((name, h), at(buf, s, h), at(buf, s, h), dev, at(buf, row(*here), h))

    for h in range(2):
        send_left("a", h, ya, (0, 0, 0), (0, 1, 0))
        for d in (1, -1):
            send_left(("z", d), h, zs[d], (0, 0, 0), (-d, 0, 0))
            send_row(right, ("x", d), h, xs[d], (0, 0), (-d, 0))
        send_sib(h, 0, 0)

    for h in range(2):
        got(("a", h))
        copy(("b", h), at(left, col(0, 1, 0), h), at(right, r, h), yb, at(right, row(0, 1), h))
        for d in (1, -1):
            send_left(("za", d), h, zs[d], (0, 1, 0), (-d, 1, 0))
        send_sib(h, 0, 1)
        for d in (1, -1):
            got((("z", d), h))
            if (h == 0) == (d == 1):
                send_left(("f", d), h, zs[d], (-d, 0, 0), (-2 * d, 0, 0))
            send_sib(h, -d, 0)
            got((("x", d), h))
            if (h == 0) == (d == 1):
                send_row(right, ("g", d), h, xs[d], (-d, 0), (-2 * d, 0))
    for h in range(2):
        got(("b", h))
        for d in (1, -1):
            send_row(right, ("xb", d), h, xs[d], (0, 1), (-d, 1))
    for h in range(2):
        for d in (1, -1):
            got((("za", d), h))
            if (h == 0) == (d == 1):
                send_left(("fa", d), h, zs[d], (-d, 1, 0), (-2 * d, 1, 0))
            send_sib(h, -d, 1)
    for h, d in ((0, 1), (1, -1)):
        got((("f", d), h))
        send_sib(h, 2, 0)
    for h in range(2):
        for d in (1, -1):
            got((("xb", d), h))
            if (h == 0) == (d == 1):
                send_row(right, ("gb", d), h, xs[d], (-d, 1), (-2 * d, 1))
    for h, d in ((0, 1), (1, -1)):
        got((("fa", d), h))
        send_sib(h, 2, 1)
    for h, d in ((0, 1), (1, -1)):
        got((("g", d), h))
    for h, d in ((0, 1), (1, -1)):
        got((("gb", d), h))
    for dz in (0, 1, -1, 2):
        for dyl in (0, 1):
            for h in range(2):
                got((("c", dz, dyl), h))

    def first(k, carry):
        term = jnp.dot(left[k].reshape(2 * W, WP), right[lax.rem(k, NROW), lax.div(k, NROW)],
                       preferred_element_type=F32)
        acc[...] += term
        return carry

    acc[...] = jnp.zeros_like(acc)
    lax.fori_loop(0, NCOL, first, 0)

    for h in range(2):
        sq[r, h, pl.ds(0, W)] = (acc[pl.ds(h * W, W), :] / ORDER * mask[h].astype(F32)).astype(BF16)
        near, far = (ya, yb) if h == 0 else (yb, ya)
        copy(("p", h), at(sq, r, h), relay.at[h], near, relay.at[h])
        for d in (1, -1):
            send_row(sq, ("sx", d), h, xs[d], (0, 0), (-d, 0))
    for h in range(2):
        got(("p", h))
        far = yb if h == 0 else ya
        slot = r if h == 0 else row(0, 1)
        copy(("q", h), relay.at[h], at(sq, slot, h), far, at(sq, row(0, 1), h))
    for h in range(2):
        for d in (1, -1):
            got((("sx", d), h))
            if (h == 0) == (d == 1):
                send_row(sq, ("sg", d), h, xs[d], (-d, 0), (-2 * d, 0))
    for h in range(2):
        got(("q", h))
        for d in (1, -1):
            send_row(sq, ("sxb", d), h, xs[d], (0, 1), (-d, 1))

    acc[...] = jnp.zeros_like(acc)

    def second(slot):
        for h in range(2):
            acc[...] += jnp.dot(left[h * NROW + slot].reshape(2 * W, WP), sq[slot, h],
                                preferred_element_type=F32)

    for dx, dyh in ((0, 0), (1, 0), (-1, 0), (0, 1)):
        second(row(dx, dyh))
    for h in range(2):
        for d in (1, -1):
            got((("sxb", d), h))
            if (h == 0) == (d == 1):
                send_row(sq, ("sgb", d), h, xs[d], (-d, 1), (-2 * d, 1))
    for h, d in ((0, 1), (1, -1)):
        got((("sg", d), h))
    for dx, dyh in ((1, 1), (-1, 1), (2, 0)):
        second(row(dx, dyh))
    for h, d in ((0, 1), (1, -1)):
        got((("sgb", d), h))
    second(row(2, 1))

    for h in range(2):
        mat = left[c, h].astype(F32)
        new = grow(keep[h]) * (1.5 * mat - 0.5 * acc[pl.ds(h * W, W), :])
        for k in range(WP // 128):
            out[h, k] = new[:, k * 128 : k * 128 + 128]
    for op in started.values():
        op.wait_send()


N_COPIES = 60


def two_products(density, pattern, keep):
    vmem = pl.BlockSpec(memory_space=pltpu.VMEM)
    return pl.pallas_call(
        products,
        out_shape=jax.ShapeDtypeStruct((2, WP // 128, W, 128), F32),
        in_specs=[vmem] * 3,
        out_specs=vmem,
        scratch_shapes=[
            pltpu.VMEM((NCOL, 2, W, WP), BF16),
            pltpu.VMEM((NROW, 2, WP, WP), BF16),
            pltpu.VMEM((NROW, 2, WP, WP), BF16),
            pltpu.VMEM((2, W, WP), BF16),
            pltpu.VMEM((2, W, WP), BF16),
            pltpu.VMEM((2 * W, WP), F32),
            pltpu.SemaphoreType.DMA((N_COPIES,)),
            pltpu.SemaphoreType.DMA((N_COPIES,)),
        ],
        compiler_params=pltpu.CompilerParams(
            collective_id=0, has_side_effects=True, vmem_limit_bytes=48 * 1024 * 1024),
        name="two_products",
    )(density, pattern, keep)


def route(update, owner_col, owner_row, out, blocks):
    bc = lax.broadcasted_iota(jnp.int32, (PB, WP), 0)
    col = lax.broadcasted_iota(jnp.int32, (PB, WP), 1)
    pick = jnp.where((col >= bc * BS) & (col < bc * BS + BS), 1.0, 0.0)[None]
    lane = lax.broadcasted_iota(jnp.int32, (WP, 256), 0)
    shift = lax.broadcasted_iota(jnp.int32, (WP, 256), 1) - (lane - lane // BS * BS)
    for w in range(3):
        base = w * 256
        total = jnp.zeros((2 * PB * PB, 256), F32)
        for i in range(BS):
            if i * BS + BS <= base or i * BS >= base + 256:
                continue
            place = jnp.where(shift == i * BS - base, 1.0, 0.0).astype(BF16)
            rows = []
            for h in range(2):
                u = jnp.concatenate(
                    [update[h, k, pl.ds(i, PB, stride=BS), :] for k in range(WP // 128)], axis=1)
                rows.append((u[:, None, :] * pick).astype(BF16).reshape(PB * PB, WP))
            total = total + jnp.dot(jnp.concatenate(rows, axis=0), place, preferred_element_type=F32)
        n = min(256, ENTP - base)
        blocks[:, pl.ds(base, n)] = total[:, :n].astype(BF16)

    n = 2 * PB * PB
    same = owner_col[...] == owner_row[...]
    earlier = lax.broadcasted_iota(jnp.int32, (n, n), 0) < lax.broadcasted_iota(jnp.int32, (n, n), 1)
    rank = jnp.sum(jnp.where(same & earlier, 1.0, 0.0), axis=0, keepdims=True).astype(jnp.int32)
    key = owner_row[...] * CAPP + rank
    step = 512
    for k in range(0, DEVICES * CAPP, step):
        at = lax.broadcasted_iota(jnp.int32, (step, n), 0) + k
        hot = jnp.where(at == key, 1.0, 0.0).astype(BF16)
        out[pl.ds(k, step), :] = jnp.dot(hot, blocks[...], preferred_element_type=F32).astype(BF16)


def routed(update, owner):
    vmem = pl.BlockSpec(memory_space=pltpu.VMEM)
    owner = owner.reshape(-1)
    return pl.pallas_call(
        route,
        out_shape=jax.ShapeDtypeStruct((DEVICES * CAPP, ENTP), BF16),
        in_specs=[vmem] * 3,
        out_specs=vmem,
        scratch_shapes=[pltpu.VMEM((2 * PB * PB, ENTP), BF16)],
        compiler_params=pltpu.CompilerParams(vmem_limit_bytes=48 * 1024 * 1024),
        name="route",
    )(update, owner[:, None], owner[None, :])


def per_device(density, pattern, keep, owner):
    update = two_products(density, pattern, keep)
    outgoing = routed(update, owner).reshape(DEVICES, CAPP, ENTP)
    outgoing = outgoing[:, :CAP, :ENT]
    arrived = lax.all_to_all(outgoing, ("row", "col"), split_axis=0, concat_axis=0, tiled=True)
    return arrived[None]


def solution(mesh):
    placed = (
        P(None, "row", "col"),
        P(None, "row", "col"),
        P(None, "row", "col"),
        P(("row", "col"), None, None),
    )
    return jax.shard_map(
        per_device,
        mesh=mesh,
        in_specs=placed,
        out_specs=P(("row", "col"), None, None, None),
        check_vma=False,
    )
```

time: 1040 us -> 155 us (0.15)
  starting transfers between devices: 481 us -> 0 us
  waiting for transfers between devices: 299 us -> 0 us
  Pallas kernels: 0 us -> 104 us
  other arithmetic: 91.6 us -> 0 us
  local copies, waits for them, and re-layouts: 90.3 us -> 6.98 us
  matrix products: 16.3 us -> 0 us
  blocking collectives: 54.3 us -> 43.6 us
    ppermute x69 -> x0, starting transfers between devices: 481 us -> none  [passed_along(): lax.ppermute(value, axis, [(i, (i + by) % count) for i in range(count)])]
    ppermute x69 -> x0, waiting for transfers between devices: 299 us -> none  [passed_along(): lax.ppermute(value, axis, [(i, (i + by) % count) for i in range(count)])]
    pallas_call x0 -> x2, Pallas kernels: none -> 104 us  [the longest x1 98.7 us: two_products(): pl.pallas_call(products, out_shape=jax.ShapeDtypeStruct((2, WP // 128, W,...]
    add x30 -> x0, other arithmetic: 85.1 us -> none  [multiply(): return total + term.reshape(2, width, width)]
    reshape x34 -> x0, local copies, waits for them, and re-layouts: 42.4 us -> none  [the longest x30 26.3 us: multiply(): return total + term.reshape(2, width, width)]
    scatter x2 -> x0, local copies, waits for them, and re-layouts: 29 us -> none  [per_device(): jnp.zeros((devices, capacity, BS * BS), jnp.bfloat16).at[targets, slots]]
    dot_general x32 -> x0, matrix products: 16.3 us -> none  [multiply(): jnp.dot(left_now.reshape(2 * width, width), piece, preferred_element_type...]
    all_to_all x1, blocking collectives: 54.3 us -> 43.6 us  [per_device(): lax.all_to_all(outgoing, ('row', 'col'), split_axis=0, concat_axis=0, til...]
  transfers between devices with their start and end apart: 69 -> 0, of which waited for: 37 -> 0; matrix products, arithmetic and copies ran while one was open for 0% -> 0% of each run, Pallas kernels for 0% -> 0%
where the time goes in v1:
time: 155 us
  Pallas kernels  104 us (67%)
  blocking collectives  43.6 us (28%)
  local copies, waits for them, and re-layouts  6.98 us (5%)
    pallas_call x1, Pallas kernels, two_products(): pl.pallas_call(products, out_shape=jax.ShapeDtypeStruct((2, WP // 128, W,...  98.7 us
    all_to_all x1, blocking collectives, per_device(): lax.all_to_all(outgoing, ('row', 'col'), split_axis=0, concat_axis=0, til...  43.6 us
    pallas_call x1, Pallas kernels, routed(): pl.pallas_call(route, out_shape=jax.ShapeDtypeStruct((DEVICES * CAPP, ENT...  5.35 us
    unnamed x8, local copies, waits for them, and re-layouts  3.16 us

profile of v1, /device:TPU:1, one launch (start us, length us, event | category | flops | bytes accessed | tf_op | source)
XLA Modules:
  0.0 154.6 jit_solution(1357528427334903498)
XLA Ops:
  0.0 0.8 copy.8.owner_col
  0.8 0.0 copy-start
  0.8 1.0 copy-done
  1.9 0.0 copy-start.1
  1.9 0.7 copy-done.1
  2.6 0.0 copy-start.2
  2.6 0.7 copy-done.2
  3.3 98.7 %two_products.1.update = f32[2,3,368,128]{3,2,1,0:T(8,128)S(1)} custom-call(bf16[2,368,368]{2,1,0:T(8,128)(2,1)S(1)} %copy-done, s32[2,16,16]{2,1,0:T(8,128)S(1)} %copy-done.1, s32[2,16,16]{2,1,0:T(8,128)S(1)} %copy-done.2), custom_call_target="tpu_custom_call" | custom-call | tf_op jit(solution)/shard_map/two_products/pallas_call | solution.py:230
  102.0 0.0 copy-start.3
  102.0 0.7 copy-done.3
  102.7 5.3 %route.1 = bf16[2048,640]{1,0:T(8,128)(2,1)S(1)} custom-call(f32[2,3,368,128]{3,2,1,0:T(8,128)S(1)} %two_products.1.update, s32[512,1]{1,0:T(8,128)S(1)} %copy.8.owner_col, s32[1,512]{1,0:T(1,128)S(1)} %bitcast.7), custom_call_target="tpu_custom_call" | custom-call | tf_op jit(solution)/shard_map/route/pallas_call | solution.py:288
  108.0 43.6 %all_to_all.5 = bf16[128,12,529]{2,1,0:T(8,128)(2,1)S(1)} all-to-all(bf16[128,12,529]{2,1,0:T(8,128)(2,1)S(1)} %bitcast.5), channel_id=1, replica_groups=mesh['row'=8,'col'=16] {'row','col'}, dimensions={0} | all-to-all | bytes 3250176 | tf_op jit(solution)/shard_map/all_to_all | solution.py:303
  151.6 3.0 %copy.9 = bf16[1,128,12,529]{1,3,2,0:T(8,128)(2,1)} copy(bf16[1,128,12,529]{3,2,1,0:T(8,128)(2,1)S(1)} %bitcast.8) | data formatting | bytes 3250176 | tf_op jit(solution)/shard_map/broadcast_in_dim | solution.py:304
Async XLA Ops:
  0.8 1.1 copy-start
  1.9 0.7 copy-start.1
  2.6 0.7 copy-start.2
  102.0 0.7 copy-start.3

commit v2 on v1

--- a/solution.py
+++ b/solution.py
@@ -14,9 +14,9 @@
 NCOL = 16
 DEVICES = NROW * NCOL
 CAP = 12
-CAPP = 16
 ENT = BS * BS
-ENTP = 640
+ROWS = 16
+LANES = 512
 MESH = pl.DeviceIdType.MESH
 F32 = jnp.float32
 BF16 = jnp.bfloat16
@@ -172,7 +172,7 @@
 
     for h in range(2):
         sq[r, h, pl.ds(0, W)] = (acc[pl.ds(h * W, W), :] / ORDER * mask[h].astype(F32)).astype(BF16)
-        near, far = (ya, yb) if h == 0 else (yb, ya)
+        near = ya if h == 0 else yb
         copy(("p", h), at(sq, r, h), relay.at[h], near, relay.at[h])
         for d in (1, -1):
             send_row(sq, ("sx", d), h, xs[d], (0, 0), (-d, 0))
@@ -249,14 +249,20 @@
 
 
 def route(update, owner_col, owner_row, out, blocks):
+    n = 2 * PB * PB
     bc = lax.broadcasted_iota(jnp.int32, (PB, WP), 0)
     col = lax.broadcasted_iota(jnp.int32, (PB, WP), 1)
     pick = jnp.where((col >= bc * BS) & (col < bc * BS + BS), 1.0, 0.0)[None]
     lane = lax.broadcasted_iota(jnp.int32, (WP, 256), 0)
     shift = lax.broadcasted_iota(jnp.int32, (WP, 256), 1) - (lane - lane // BS * BS)
+    same = owner_col[...] == owner_row[...]
+    one = lax.broadcasted_iota(jnp.int32, (n, n), 0)
+    two = lax.broadcasted_iota(jnp.int32, (n, n), 1)
+    rank = jnp.sum(jnp.where(same & (one < two), 1.0, 0.0), axis=0, keepdims=True).astype(jnp.int32)
+    rank_col = jnp.sum(jnp.where(same & (two < one), 1.0, 0.0), axis=1, keepdims=True).astype(jnp.int32)
     for w in range(3):
         base = w * 256
-        total = jnp.zeros((2 * PB * PB, 256), F32)
+        total = jnp.zeros((n, 256), F32)
         for i in range(BS):
             if i * BS + BS <= base or i * BS >= base + 256:
                 continue
@@ -267,18 +273,22 @@
                     [update[h, k, pl.ds(i, PB, stride=BS), :] for k in range(WP // 128)], axis=1)
                 rows.append((u[:, None, :] * pick).astype(BF16).reshape(PB * PB, WP))
             total = total + jnp.dot(jnp.concatenate(rows, axis=0), place, preferred_element_type=F32)
-        n = min(256, ENTP - base)
-        blocks[:, pl.ds(base, n)] = total[:, :n].astype(BF16)
-
-    n = 2 * PB * PB
-    same = owner_col[...] == owner_row[...]
-    earlier = lax.broadcasted_iota(jnp.int32, (n, n), 0) < lax.broadcasted_iota(jnp.int32, (n, n), 1)
-    rank = jnp.sum(jnp.where(same & earlier, 1.0, 0.0), axis=0, keepdims=True).astype(jnp.int32)
-    key = owner_row[...] * CAPP + rank
+        if w < 2:
+            blocks[pl.ds(0, n), pl.ds(base, 256)] = total.astype(BF16)
+        else:
+            for k in range(4):
+                mine = (rank_col >= 3 * k) & (rank_col < 3 * k + 3)
+                blocks[pl.ds(n, n), pl.ds(128 * k, 128)] = jnp.where(mine, total[:, :128], 0.0).astype(BF16)
+
+    third = rank - lax.div(rank, 3) * 3
+    key = owner_row[...] * ROWS + rank
+    tail_key = owner_row[...] * ROWS + CAP + third
     step = 512
-    for k in range(0, DEVICES * CAPP, step):
+    for k in range(0, DEVICES * ROWS, step):
         at = lax.broadcasted_iota(jnp.int32, (step, n), 0) + k
-        hot = jnp.where(at == key, 1.0, 0.0).astype(BF16)
+        head = jnp.where(at == key, 1.0, 0.0).astype(BF16)
+        tail = jnp.where(at == tail_key, 1.0, 0.0).astype(BF16)
+        hot = jnp.concatenate([head, tail], axis=1)
         out[pl.ds(k, step), :] = jnp.dot(hot, blocks[...], preferred_element_type=F32).astype(BF16)
 
 
@@ -287,21 +297,120 @@
     owner = owner.reshape(-1)
     return pl.pallas_call(
         route,
-        out_shape=jax.ShapeDtypeStruct((DEVICES * CAPP, ENTP), BF16),
+        out_shape=jax.ShapeDtypeStruct((DEVICES * ROWS, LANES), BF16),
         in_specs=[vmem] * 3,
         out_specs=vmem,
-        scratch_shapes=[pltpu.VMEM((2 * PB * PB, ENTP), BF16)],
+        scratch_shapes=[pltpu.VMEM((4 * PB * PB, LANES), BF16)],
         compiler_params=pltpu.CompilerParams(vmem_limit_bytes=48 * 1024 * 1024),
         name="route",
     )(update, owner[:, None], owner[None, :])
 
 
+def exchange(outgoing, arrived, send, recv, own):
+    r = lax.axis_index("row")
+    c = lax.axis_index("col")
+    x, yh = lax.rem(r, 4), lax.div(r, 4)
+    z, yl, core = lax.div(c, 4), lax.rem(lax.div(c, 2), 2), lax.rem(c, 2)
+    me = r * NCOL + c
+
+    def partner(i, sign):
+        dcore, dz = lax.rem(i, 2), lax.rem(lax.div(i, 2), 4)
+        dyl, dyh, dx = lax.rem(lax.div(i, 8), 2), lax.rem(lax.div(i, 16), 2), lax.div(i, 32)
+        row = lax.rem(yh + dyh, 2) * 4 + lax.rem(x + sign * dx + 4, 4)
+        col = lax.rem(z + sign * dz + 4, 4) * 4 + lax.rem(yl + dyl, 2) * 2 + lax.rem(core + dcore, 2)
+        return row, col
+
+    def copy(i):
+        row, col = partner(i, 1)
+        at = pl.multiple_of((row * NCOL + col) * ROWS, ROWS)
+        return pltpu.make_async_remote_copy(
+            src_ref=outgoing.at[pl.ds(at, ROWS)],
+            dst_ref=arrived.at[pl.ds(pl.multiple_of(me * ROWS, ROWS), ROWS)],
+            send_sem=send.at[i], recv_sem=recv.at[i], device_id=(row, col), device_id_type=MESH)
+
+    def arrival(i):
+        row, col = partner(i, -1)
+        here = arrived.at[pl.ds(pl.multiple_of((row * NCOL + col) * ROWS, ROWS), ROWS)]
+        return pltpu.make_async_remote_copy(
+            src_ref=here, dst_ref=here, send_sem=send.at[i], recv_sem=recv.at[i],
+            device_id=(row, col), device_id_type=MESH)
+
+    barrier = pltpu.get_barrier_semaphore()
+
+    def greet(i, carry):
+        pl.semaphore_signal(barrier, inc=1, device_id=partner(i, 1), device_id_type=MESH)
+        return carry
+
+    lax.fori_loop(1, DEVICES, greet, 0)
+    mine = pl.ds(pl.multiple_of(me * ROWS, ROWS), ROWS)
+    keep = pltpu.make_async_copy(outgoing.at[mine], arrived.at[mine], own)
+    keep.start()
+    pl.semaphore_wait(barrier, DEVICES - 1)
+
+    def start(i, carry):
+        copy(lax.rem(i * 45, DEVICES)).start()
+        return carry
+
+    def finish(i, carry):
+        arrival(lax.rem(i * 45, DEVICES)).wait_recv()
+        return carry
+
+    def sent(i, carry):
+        copy(i).wait_send()
+        return carry
+
+    lax.fori_loop(1, DEVICES, start, 0)
+    keep.wait()
+    lax.fori_loop(1, DEVICES, finish, 0)
+    lax.fori_loop(1, DEVICES, sent, 0)
+
+
+def exchanged(outgoing):
+    vmem = pl.BlockSpec(memory_space=pltpu.VMEM)
+    return pl.pallas_call(
+        exchange,
+        out_shape=jax.ShapeDtypeStruct(outgoing.shape, outgoing.dtype),
+        in_specs=[vmem],
+        out_specs=vmem,
+        scratch_shapes=[
+            pltpu.SemaphoreType.DMA((DEVICES,)),
+            pltpu.SemaphoreType.DMA((DEVICES,)),
+            pltpu.SemaphoreType.DMA,
+        ],
+        compiler_params=pltpu.CompilerParams(
+            collective_id=1, has_side_effects=True, vmem_limit_bytes=32 * 1024 * 1024),
+        name="exchange",
+    )(outgoing)
+
+
+def unpack(arrived, out, wide):
+    for k in range(LANES // 128):
+        wide[k] = arrived[:, pl.ds(128 * k, 128)].astype(F32)
+    for s in range(CAP):
+        for k in range(LANES // 128):
+            part = wide[k, pl.ds(s, DEVICES, stride=ROWS), :]
+            out[s, pl.ds(128 * k, 128), :] = part.T.astype(BF16)
+        tail = wide[s // 3, pl.ds(CAP + s % 3, DEVICES, stride=ROWS), :]
+        out[s, pl.ds(LANES, ENT - LANES), :] = tail.T[: ENT - LANES].astype(BF16)
+
+
+def unpacked(arrived):
+    vmem = pl.BlockSpec(memory_space=pltpu.VMEM)
+    out = pl.pallas_call(
+        unpack,
+        out_shape=jax.ShapeDtypeStruct((CAP, ENT, DEVICES), BF16),
+        in_specs=[vmem],
+        out_specs=vmem,
+        scratch_shapes=[pltpu.VMEM((LANES // 128, DEVICES * ROWS, 128), F32)],
+        compiler_params=pltpu.CompilerParams(vmem_limit_bytes=32 * 1024 * 1024),
+        name="unpack",
+    )(arrived)
+    return out.transpose(2, 0, 1)[None]
+
+
 def per_device(density, pattern, keep, owner):
     update = two_products(density, pattern, keep)
-    outgoing = routed(update, owner).reshape(DEVICES, CAPP, ENTP)
-    outgoing = outgoing[:, :CAP, :ENT]
-    arrived = lax.all_to_all(outgoing, ("row", "col"), split_axis=0, concat_axis=0, tiled=True)
-    return arrived[None]
+    return unpacked(exchanged(routed(update, owner)))
 
 
 def solution(mesh):

time: 155 us -> 152 us (0.981)
  Pallas kernels: 104 us -> 148 us
  blocking collectives: 43.6 us -> 0 us
  local copies, waits for them, and re-layouts: 6.98 us -> 3.98 us
    pallas_call x1 -> x3, Pallas kernels: 5.35 us -> 49 us  [the longest x1 40.1 us: exchanged(): pl.pallas_call(exchange, out_shape=jax.ShapeDtypeStruct(outgoing.shape, o...]
    all_to_all x1 -> x0, blocking collectives: 43.6 us -> none  [per_device(): lax.all_to_all(outgoing, ('row', 'col'), split_axis=0, concat_axis=0, til...]
    broadcast_in_dim x1 -> x0, local copies, waits for them, and re-layouts: 3 us -> none  [per_device(): return arrived[None]]
where the time goes in v2:
time: 152 us
  Pallas kernels  148 us (97%)
  local copies, waits for them, and re-layouts  3.98 us (3%)
    pallas_call x1, Pallas kernels, two_products(): pl.pallas_call(products, out_shape=jax.ShapeDtypeStruct((2, WP // 128, W,...  98.7 us
    pallas_call x1, Pallas kernels, exchanged(): pl.pallas_call(exchange, out_shape=jax.ShapeDtypeStruct(outgoing.shape, o...  40.1 us
    pallas_call x1, Pallas kernels, routed(): pl.pallas_call(route, out_shape=jax.ShapeDtypeStruct((DEVICES * ROWS, LAN...  6 us
    unnamed x8, local copies, waits for them, and re-layouts  3.16 us

profile of v2, /device:TPU:1, one launch (start us, length us, event | category | flops | bytes accessed | tf_op | source)
XLA Modules:
  0.0 151.7 jit_solution(8855223527089296298)
XLA Ops:
  0.0 0.8 copy.5.owner_col
  0.8 0.0 copy-start
  0.8 1.0 copy-done
  1.9 0.0 copy-start.1
  1.9 0.7 copy-done.1
  2.6 0.0 copy-start.2
  2.6 0.7 copy-done.2
  3.3 98.7 %two_products.1.update = f32[2,3,368,128]{3,2,1,0:T(8,128)S(1)} custom-call(bf16[2,368,368]{2,1,0:T(8,128)(2,1)S(1)} %copy-done, s32[2,16,16]{2,1,0:T(8,128)S(1)} %copy-done.1, s32[2,16,16]{2,1,0:T(8,128)S(1)} %copy-done.2), custom_call_target="tpu_custom_call" | custom-call | tf_op jit(solution)/shard_map/two_products/pallas_call | solution.py:230
  102.0 0.0 copy-start.3
  102.0 0.7 copy-done.3
  102.7 6.0 %route.1.outgoing = bf16[2048,512]{1,0:T(8,128)(2,1)S(1)} custom-call(f32[2,3,368,128]{3,2,1,0:T(8,128)S(1)} %two_products.1.update, s32[512,1]{1,0:T(8,128)S(1)} %copy.5.owner_col, s32[1,512]{1,0:T(1,128)S(1)} %bitcast.6), custom_call_target="tpu_custom_call" | custom-call | tf_op jit(solution)/shard_map/route/pallas_call | solution.py:298
  108.7 40.1 %exchange.1.arrived = bf16[2048,512]{1,0:T(8,128)(2,1)S(1)} custom-call(bf16[2048,512]{1,0:T(8,128)(2,1)S(1)} %route.1.outgoing), custom_call_target="tpu_custom_call" | custom-call | tf_op jit(solution)/shard_map/exchange/pallas_call | solution.py:370
  148.8 3.0 %unpack.1 = bf16[12,529,128]{2,1,0:T(8,128)(2,1)} custom-call(bf16[2048,512]{1,0:T(8,128)(2,1)S(1)} %exchange.1.arrived), custom_call_target="tpu_custom_call" | custom-call | tf_op jit(solution)/shard_map/unpack/pallas_call | solution.py:399
Async XLA Ops:
  0.8 1.1 copy-start
  1.9 0.7 copy-start.1
  2.6 0.7 copy-start.2
  102.0 0.7 copy-start.3

commit v3 on v0

v3 whole, which is shorter than its diff:
```python
import jax
import jax.numpy as jnp
from jax import lax
from jax.experimental import pallas as pl
from jax.experimental.pallas import tpu as pltpu
from jax.sharding import PartitionSpec as P

BS = 23
PB = 16
W = BS * PB
WP = 384
ORDER = 5888
NROW = 8
NCOL = 16
DEVICES = NROW * NCOL
CAP = 12
ENT = BS * BS
ROWS = 16
LANES = 512
SPLIT1 = 288
SPLIT2 = 240
MESH = pl.DeviceIdType.MESH
F32 = jnp.float32
BF16 = jnp.bfloat16


def grow_columns(mask):
    block = lax.broadcasted_iota(jnp.int32, (PB, WP), 0)
    col = lax.broadcasted_iota(jnp.int32, (PB, WP), 1)
    spread = jnp.where((col >= block * BS) & (col < block * BS + BS), 1.0, 0.0).astype(BF16)
    return jnp.dot(mask, spread, preferred_element_type=F32).astype(BF16)


def grow(mask):
    wide = grow_columns(mask.astype(F32).astype(BF16))
    row = lax.broadcasted_iota(jnp.int32, (W, PB), 0)
    block = lax.broadcasted_iota(jnp.int32, (W, PB), 1)
    spread = jnp.where((row >= block * BS) & (row < block * BS + BS), 1.0, 0.0).astype(BF16)
    return jnp.dot(spread, wide, preferred_element_type=F32)


def whole_step(
    dens_in, pat_in, keep_in, owner_in, arrived,
    dens, pat, keep, owner, left, right, sq, mask, kept, acc, update, place, hot, blocks, outgoing,
    send, recv, exchange_send, exchange_recv, local,
):
    r = lax.axis_index("row")
    c = lax.axis_index("col")
    x, yh = lax.rem(r, 4), lax.div(r, 4)
    z, yl, core = lax.div(c, 4), lax.rem(lax.div(c, 2), 2), lax.rem(c, 2)
    me = r * NCOL + c

    def col(dz, dyl, dcore=0):
        ycol = (1 - yl) if dyl else yl
        ccol = (1 - core) if dcore else core
        return lax.rem(z + dz + 4, 4) * 4 + ycol * 2 + ccol

    def row(dx, dyh):
        yrow = (1 - yh) if dyh else yh
        return yrow * 4 + lax.rem(x + dx + 4, 4)

    sib = (r, col(0, 0, 1))
    ya = (r, col(0, 1))
    yb = (row(0, 1), col(0, 1))
    yy = (row(0, 1), c)
    zs = {1: (r, col(1, 0)), -1: (r, col(-1, 0))}
    xs = {1: (row(1, 0), c), -1: (row(-1, 0), c)}

    fetches = [
        pltpu.make_async_copy(src, dst, local.at[k])
        for k, (src, dst) in enumerate(((pat_in, pat), (dens_in, dens), (keep_in, keep), (owner_in, owner)))
    ]
    for fetch in fetches:
        fetch.start()
    barrier = pltpu.get_barrier_semaphore()
    for dev in (sib, ya, yb, yy, zs[1], zs[-1], xs[1], xs[-1]):
        pl.semaphore_signal(barrier, inc=1, device_id=dev, device_id_type=MESH)

    started = []
    arriving = {}

    def start(name, src, dst, dev, here):
        k = len(started)
        op = pltpu.make_async_remote_copy(
            src_ref=src, dst_ref=dst, send_sem=send.at[k], recv_sem=recv.at[k],
            device_id=dev, device_id_type=MESH)
        op.start()
        started.append(op)
        arriving[name] = pltpu.make_async_remote_copy(
            src_ref=here, dst_ref=here, send_sem=send.at[k], recv_sem=recv.at[k],
            device_id=dev, device_id_type=MESH)

    def got(*names):
        for name in names:
            arriving[name].wait_recv()

    ALL, LO, HI = (0, W), (0, SPLIT1), (SPLIT1, W)
    LO2, HI2 = (0, SPLIT2), (SPLIT2, W)

    def part(buf, slot, h, rows):
        return buf.at[slot, h, pl.ds(rows[0], rows[1] - rows[0])]

    def go_left(name, dev, there, here, h, rows=ALL):
        s = col(*there)
        start((name, h, rows), part(left, s, h, rows), part(left, s, h, rows), dev, part(left, col(*here), h, rows))

    def go_sib(h, dz, dyl):
        go_left(("c", dz, dyl), sib, (dz, dyl, 0), (dz, dyl, 1), h)

    def go(buf, name, dev, there, here, h, rows=ALL):
        s = row(*there)
        start((name, h, rows), part(buf, s, h, rows), part(buf, s, h, rows), dev, part(buf, row(*here), h, rows))

    fetches[0].wait()
    fetches[1].wait()
    for h in range(2):
        m = grow(pat[h]).astype(BF16)
        left[c, h, :, pl.ds(256, 128)] = jnp.zeros((W, 128), BF16)
        left[c, h, :, pl.ds(0, W)] = dens[h] * m[:, :W]
        mask[h] = m
        if h == 0:
            pl.semaphore_wait(barrier, 8)
        go_left("a", ya, (0, 0), (0, 1), h)
        for d in (1, -1):
            go_left(("z", d), zs[d], (0, 0), (-d, 0), h)
            start((("x", d), h, ALL), part(left, c, h, ALL), part(right, r, h, ALL), xs[d], part(right, row(-d, 0), h, ALL))
        go_sib(h, 0, 0)

    for h in range(2):
        right[r, h, pl.ds(0, W)] = left[c, h]
    zero = jnp.zeros((2, WP - W, WP), BF16)

    def clear(k, carry):
        right[k, :, pl.ds(W, WP - W)] = zero
        sq[k, :, pl.ds(W, WP - W)] = zero
        return carry

    lax.fori_loop(0, NROW, clear, 0)
    acc[...] = jnp.zeros_like(acc)
    fetches[2].wait()
    fetches[3].wait()
    for h in range(2):
        kept[h] = grow(keep[h]).astype(BF16)

    got(("a", 0, ALL))
    start(("b", 0, ALL), part(left, col(0, 1), 0, ALL), part(right, r, 0, ALL), yb, part(right, row(0, 1), 0, ALL))
    go_left(("za", -1), zs[-1], (0, 1), (1, 1), 0)
    go_sib(0, 0, 1)
    got((("z", 1), 0, ALL))
    go_left(("ay", 1), ya, (-1, 0), (-1, 1), 0, LO)
    go_sib(0, -1, 0)
    got((("z", -1), 0, ALL))
    go_sib(0, 1, 0)
    got((("x", 1), 0, ALL))
    go(right, ("g", 1), xs[1], (-1, 0), (2, 0), 0)
    go(right, ("ys", 1), yy, (-1, 0), (-1, 1), 0, LO)
    got((("x", -1), 0, ALL))
    routing_tables(owner, place, hot)
    got(("a", 1, ALL))
    start(("b", 1, ALL), part(left, col(0, 1), 1, ALL), part(right, r, 1, ALL), yb, part(right, row(0, 1), 1, ALL))
    go_left(("za", 1), zs[1], (0, 1), (-1, 1), 1)
    go_left(("za", 1), zs[1], (0, 1), (-1, 1), 0, HI)
    go_sib(1, 0, 1)
    got((("z", 1), 1, ALL))
    go_left(("f", 1), zs[1], (-1, 0), (2, 0), 0)
    go_sib(1, -1, 0)
    got((("z", -1), 1, ALL))
    go_left(("f", -1), zs[-1], (1, 0), (2, 0), 1)
    go_left(("ay", -1), ya, (1, 0), (1, 1), 1, LO)
    go_left(("za", -1), zs[-1], (0, 1), (1, 1), 1, HI)
    go_sib(1, 1, 0)
    got(("b", 0, ALL))
    go(right, ("xb", -1), xs[-1], (0, 1), (1, 1), 0)
    go(right, ("xb", 1), xs[1], (0, 1), (-1, 1), 0, HI)
    got((("x", 1), 1, ALL), (("x", -1), 1, ALL))
    go(right, ("g", -1), xs[-1], (1, 0), (2, 0), 1)
    go(right, ("ys", -1), yy, (1, 0), (1, 1), 1, LO)
    got(("b", 1, ALL))
    go(right, ("xb", 1), xs[1], (0, 1), (-1, 1), 1, LO)
    go(right, ("xb", 1), xs[1], (0, 1), (-1, 1), 1, HI)
    go(right, ("xb", -1), xs[-1], (0, 1), (1, 1), 1, HI)
    got((("za", -1), 0, ALL))
    go_left(("fa", -1), zs[-1], (1, 1), (2, 1), 0)
    go_sib(0, 1, 1)
    got((("za", 1), 1, ALL))
    go_left(("fa", 1), zs[1], (-1, 1), (2, 1), 1)
    go_sib(1, -1, 1)
    got((("xb", -1), 0, ALL))
    go(right, ("gb", -1), xs[-1], (1, 1), (2, 1), 0)
    got((("f", 1), 0, ALL))
    go_sib(0, 2, 0)
    got((("f", -1), 1, ALL))
    go_sib(1, 2, 0)
    got((("xb", 1), 1, LO))
    go(right, ("gb", 1), xs[1], (-1, 1), (2, 1), 1, LO)
    got((("xb", 1), 1, HI))
    go(right, ("gb", 1), xs[1], (-1, 1), (2, 1), 1, HI)
    got((("za", 1), 0, HI), (("ay", 1), 0, LO))
    go_sib(0, -1, 1)
    got((("za", -1), 1, HI), (("ay", -1), 1, LO))
    go_sib(1, 1, 1)
    got((("g", 1), 0, ALL), (("g", -1), 1, ALL))
    got((("xb", 1), 0, HI), (("ys", 1), 0, LO), (("xb", -1), 1, HI), (("ys", -1), 1, LO))
    for h in range(2):
        got(*[(("c", dz, dyl), h, ALL) for dz in (0, 1, -1, 2) for dyl in (0, 1) if (dz, dyl) != (2, 1)])

    def multiply(p, buf):
        two = jnp.concatenate([left[2 * p].reshape(2 * W, WP), left[2 * p + 1].reshape(2 * W, WP)], axis=1)
        rows = buf[pl.ds(lax.rem(2 * p, NROW), 2), lax.div(p, 4)].reshape(2 * WP, WP)
        acc[...] += jnp.dot(two, rows, preferred_element_type=F32)

    def is_late(p):
        zp, yp = lax.div(p, 2), lax.rem(p, 2)
        in_left = (zp == lax.rem(z + 2, 4)) & (yp == 1 - yl)
        in_right = (lax.rem(zp, 2) == 1 - yh) & (yp == lax.div(lax.rem(x + 2, 4), 2))
        return in_left | in_right

    def early(p, carry):
        @pl.when(jnp.logical_not(is_late(p)))
        def _():
            multiply(p, right)
        return carry

    def late(p, carry):
        @pl.when(is_late(p))
        def _():
            multiply(p, right)
        return carry

    lax.fori_loop(0, NCOL // 2, early, 0)
    got((("fa", -1), 0, ALL))
    go_sib(0, 2, 1)
    got((("fa", 1), 1, ALL))
    go_sib(1, 2, 1)
    got((("gb", -1), 0, ALL), (("gb", 1), 1, LO), (("gb", 1), 1, HI))
    got((("c", 2, 1), 0, ALL), (("c", 2, 1), 1, ALL))
    lax.fori_loop(0, NCOL // 2, late, 0)

    for h in range(2):
        sq[r, h, pl.ds(0, W)] = (acc[pl.ds(h * W, W), :] / ORDER * mask[h].astype(F32)).astype(BF16)
        for d in (1, -1):
            go(sq, ("sx", d), xs[d], (0, 0), (-d, 0), h)
        go(sq, "sy", yy, (0, 0), (0, 1), h)
    acc[...] = jnp.zeros_like(acc)
    got(("sy", 0, ALL))
    go(sq, ("sxb", -1), xs[-1], (0, 1), (1, 1), 0, LO2)
    got((("sx", 1), 0, ALL))
    go(sq, ("sys", 1), yy, (-1, 0), (-1, 1), 0)
    got((("sx", -1), 0, ALL))
    got(("sy", 1, ALL))
    go(sq, ("sxb", 1), xs[1], (0, 1), (-1, 1), 1, LO2)
    got((("sx", 1), 1, ALL))
    go(sq, ("sg", 1), xs[1], (-1, 0), (2, 0), 0)
    go(sq, ("sye", 1), yy, (-1, 0), (-1, 1), 1, HI2)
    go(sq, ("sye", -1), yy, (1, 0), (1, 1), 0, HI2)
    got((("sx", -1), 1, ALL))
    go(sq, ("sg", -1), xs[-1], (1, 0), (2, 0), 1)
    go(sq, ("sys", -1), yy, (1, 0), (1, 1), 1)

    def second(yhp, pair):
        for h in range(2):
            multiply((2 * h + yhp) * 2 + pair, sq)

    near = lax.div(x, 2)
    second(yh, near)
    got((("sxb", -1), 0, LO2))
    go(sq, ("sgb", -1), xs[-1], (1, 1), (2, 1), 0, LO2)
    got((("sxb", 1), 1, LO2))
    go(sq, ("sgb", 1), xs[1], (-1, 1), (2, 1), 1, LO2)
    got((("sye", -1), 0, HI2))
    go(sq, ("sgb", -1), xs[-1], (1, 1), (2, 1), 0, HI2)
    got((("sye", 1), 1, HI2))
    go(sq, ("sgb", 1), xs[1], (-1, 1), (2, 1), 1, HI2)
    got((("sg", 1), 0, ALL), (("sg", -1), 1, ALL))
    second(yh, 1 - near)
    got((("sys", 1), 0, ALL), (("sys", -1), 1, ALL))
    second(1 - yh, near)
    got(*[(("sgb", d), h, rows) for d, h in ((-1, 0), (1, 1)) for rows in (LO2, HI2)])
    second(1 - yh, 1 - near)

    for h in range(2):
        mat = left[c, h].astype(F32)
        new = kept[h].astype(F32) * (1.5 * mat - 0.5 * acc[pl.ds(h * W, W), :])
        for k in range(WP // 128):
            update[h, k] = new[:, k * 128 : k * 128 + 128]

    fill(update, owner, place, hot, blocks, outgoing)

    def partner(i, sign):
        dcore, dz = lax.rem(i, 2), lax.rem(lax.div(i, 2), 4)
        dyl, dyh, dx = lax.rem(lax.div(i, 8), 2), lax.rem(lax.div(i, 16), 2), lax.div(i, 32)
        to_row = lax.rem(yh + dyh, 2) * 4 + lax.rem(x + sign * dx + 4, 4)
        to_col = lax.rem(z + sign * dz + 4, 4) * 4 + lax.rem(yl + dyl, 2) * 2 + lax.rem(core + dcore, 2)
        return to_row, to_col

    def rows_of(buf, device):
        return buf.at[pl.ds(pl.multiple_of(device * ROWS, ROWS), ROWS)]

    def message(i):
        to_row, to_col = partner(i, 1)
        return pltpu.make_async_remote_copy(
            src_ref=rows_of(outgoing, to_row * NCOL + to_col), dst_ref=rows_of(arrived, me),
            send_sem=exchange_send.at[i], recv_sem=exchange_recv.at[i],
            device_id=(to_row, to_col), device_id_type=MESH)

    def arrival(i):
        from_row, from_col = partner(i, -1)
        here = rows_of(arrived, from_row * NCOL + from_col)
        return pltpu.make_async_remote_copy(
            src_ref=here, dst_ref=here, send_sem=exchange_send.at[i], recv_sem=exchange_recv.at[i],
            device_id=(from_row, from_col), device_id_type=MESH)

    def start_message(i, carry):
        message(lax.rem(i * 37, DEVICES)).start()
        return carry

    def finish_message(i, carry):
        arrival(lax.rem(i * 37, DEVICES)).wait_recv()
        return carry

    def message_sent(i, carry):
        message(i).wait_send()
        return carry

    lax.fori_loop(1, DEVICES, start_message, 0)
    own = pltpu.make_async_copy(rows_of(outgoing, me), rows_of(arrived, me), local.at[4])
    own.start()
    for op in started:
        op.wait_send()
    own.wait()
    lax.fori_loop(1, DEVICES, finish_message, 0)
    lax.fori_loop(1, DEVICES, message_sent, 0)


N_BLOCKS = 2 * PB * PB
WINDOWS = [
    (w, i) for w in range(3) for i in range(BS) if i * BS + BS > w * 256 and i * BS < w * 256 + 256
]


def ranks(owner_row):
    owner = jnp.broadcast_to(owner_row.astype(F32), (8, N_BLOCKS))
    same = owner.T[:, :1] == owner[:1]
    one = lax.broadcasted_iota(jnp.int32, (N_BLOCKS, N_BLOCKS), 0)
    two = lax.broadcasted_iota(jnp.int32, (N_BLOCKS, N_BLOCKS), 1)
    rank = jnp.sum(jnp.where(same & (one < two), 1.0, 0.0), axis=0, keepdims=True).astype(jnp.int32)
    rank_col = jnp.sum(jnp.where(same & (two < one), 1.0, 0.0), axis=1, keepdims=True).astype(jnp.int32)
    return rank, rank_col


def routing_tables(owner, place, hot):
    lane = lax.broadcasted_iota(jnp.int32, (WP, 256), 0)
    shift = lax.broadcasted_iota(jnp.int32, (WP, 256), 1) - (lane - lax.div(lane, BS) * BS)
    for k, (w, i) in enumerate(WINDOWS):
        place[k] = jnp.where(shift == i * BS - w * 256, 1.0, 0.0).astype(BF16)
    rank, _ = ranks(owner[...])
    third = rank - lax.div(rank, 3) * 3
    key = owner[...] * ROWS + rank
    tail_key = owner[...] * ROWS + CAP + third
    step = 512
    for k in range(0, DEVICES * ROWS, step):
        at = lax.broadcasted_iota(jnp.int32, (step, N_BLOCKS), 0) + k
        hot[pl.ds(k, step), pl.ds(0, N_BLOCKS)] = jnp.where(at == key, 1.0, 0.0).astype(BF16)
        hot[pl.ds(k, step), pl.ds(N_BLOCKS, N_BLOCKS)] = jnp.where(at == tail_key, 1.0, 0.0).astype(BF16)


def fill(update, owner, place, hot, blocks, outgoing):
    n = N_BLOCKS
    bc = lax.broadcasted_iota(jnp.int32, (PB, WP), 0)
    entry = lax.broadcasted_iota(jnp.int32, (PB, WP), 1)
    pick = jnp.where((entry >= bc * BS) & (entry < bc * BS + BS), 1.0, 0.0)[None]
    _, rank_col = ranks(owner[...])
    for w in range(3):
        total = jnp.zeros((n, 256), F32)
        for k, (wk, i) in enumerate(WINDOWS):
            if wk != w:
                continue
            rows = []
            for h in range(2):
                u = jnp.concatenate(
                    [update[h, j, pl.ds(i, PB, stride=BS), :] for j in range(WP // 128)], axis=1)
                rows.append((u[:, None, :] * pick).astype(BF16).reshape(PB * PB, WP))
            total = total + jnp.dot(jnp.concatenate(rows, axis=0), place[k], preferred_element_type=F32)
        if w < 2:
            blocks[pl.ds(0, n), pl.ds(256 * w, 256)] = total.astype(BF16)
        else:
            for j in range(4):
                mine = (rank_col >= 3 * j) & (rank_col < 3 * j + 3)
                blocks[pl.ds(n, n), pl.ds(128 * j, 128)] = jnp.where(mine, total[:, :128], 0.0).astype(BF16)
    step = 512
    for k in range(0, DEVICES * ROWS, step):
        outgoing[pl.ds(k, step), :] = jnp.dot(
            hot[pl.ds(k, step), :], blocks[...], preferred_element_type=F32).astype(BF16)


N_COPIES = 72


def stepped(density, pattern, keep, owner):
    anywhere = pl.BlockSpec(memory_space=pl.ANY)
    owner = owner.reshape(1, N_BLOCKS)
    return pl.pallas_call(
        whole_step,
        out_shape=jax.ShapeDtypeStruct((DEVICES * ROWS, LANES), BF16),
        in_specs=[anywhere] * 4,
        out_specs=pl.BlockSpec(memory_space=pltpu.VMEM),
        scratch_shapes=[
            pltpu.VMEM(density.shape, BF16),
            pltpu.VMEM(pattern.shape, jnp.int32),
            pltpu.VMEM(keep.shape, jnp.int32),
            pltpu.VMEM(owner.shape, jnp.int32),
            pltpu.VMEM((NCOL, 2, W, WP), BF16),
            pltpu.VMEM((NROW, 2, WP, WP), BF16),
            pltpu.VMEM((NROW, 2, WP, WP), BF16),
            pltpu.VMEM((2, W, WP), BF16),
            pltpu.VMEM((2, W, WP), BF16),
            pltpu.VMEM((2 * W, WP), F32),
            pltpu.VMEM((2, WP // 128, W, 128), F32),
            pltpu.VMEM((len(WINDOWS), WP, 256), BF16),
            pltpu.VMEM((DEVICES * ROWS, 2 * N_BLOCKS), BF16),
            pltpu.VMEM((2 * N_BLOCKS, LANES), BF16),
            pltpu.VMEM((DEVICES * ROWS, LANES), BF16),
            pltpu.SemaphoreType.DMA((N_COPIES,)),
            pltpu.SemaphoreType.DMA((N_COPIES,)),
            pltpu.SemaphoreType.DMA((DEVICES,)),
            pltpu.SemaphoreType.DMA((DEVICES,)),
            pltpu.SemaphoreType.DMA((5,)),
        ],
        compiler_params=pltpu.CompilerParams(
            collective_id=0, has_side_effects=True, vmem_limit_bytes=54 * 1024 * 1024),
        name="whole_step",
    )(density, pattern, keep, owner)


def unpack(arrived, out, wide):
    for k in range(LANES // 128):
        wide[k] = arrived[:, pl.ds(128 * k, 128)].astype(F32)
    for s in range(CAP):
        for k in range(LANES // 128):
            part = wide[k, pl.ds(s, DEVICES, stride=ROWS), :]
            out[s, pl.ds(128 * k, 128), :] = part.T.astype(BF16)
        tail = wide[s // 3, pl.ds(CAP + s % 3, DEVICES, stride=ROWS), :]
        out[s, pl.ds(LANES, ENT - LANES), :] = tail.T[: ENT - LANES].astype(BF16)


def unpacked(arrived):
    vmem = pl.BlockSpec(memory_space=pltpu.VMEM)
    out = pl.pallas_call(
        unpack,
        out_shape=jax.ShapeDtypeStruct((CAP, ENT, DEVICES), BF16),
        in_specs=[vmem],
        out_specs=vmem,
        scratch_shapes=[pltpu.VMEM((LANES // 128, DEVICES * ROWS, 128), F32)],
        compiler_params=pltpu.CompilerParams(vmem_limit_bytes=32 * 1024 * 1024),
        name="unpack",
    )(arrived)
    return out.transpose(2, 0, 1)[None]


def per_device(density, pattern, keep, owner):
    return unpacked(stepped(density, pattern, keep, owner))


def solution(mesh):
    placed = (
        P(None, "row", "col"),
        P(None, "row", "col"),
        P(None, "row", "col"),
        P(("row", "col"), None, None),
    )
    return jax.shard_map(
        per_device,
        mesh=mesh,
        in_specs=placed,
        out_specs=P(("row", "col"), None, None, None),
        check_vma=False,
    )
```

time: 1040 us -> 126 us (0.12)
  starting transfers between devices: 481 us -> 0 us
  waiting for transfers between devices: 299 us -> 0 us
  Pallas kernels: 0 us -> 124 us
  other arithmetic: 91.6 us -> 0 us
  local copies, waits for them, and re-layouts: 90.3 us -> 1.58 us
  blocking collectives: 54.3 us -> 0 us
  matrix products: 16.3 us -> 0 us
    ppermute x69 -> x0, starting transfers between devices: 481 us -> none  [passed_along(): lax.ppermute(value, axis, [(i, (i + by) % count) for i in range(count)])]
    ppermute x69 -> x0, waiting for transfers between devices: 299 us -> none  [passed_along(): lax.ppermute(value, axis, [(i, (i + by) % count) for i in range(count)])]
    pallas_call x0 -> x2, Pallas kernels: none -> 124 us  [the longest x1 121 us: stepped(): pl.pallas_call(whole_step, out_shape=jax.ShapeDtypeStruct((DEVICES * ROWS...]
    add x30 -> x0, other arithmetic: 85.1 us -> none  [multiply(): return total + term.reshape(2, width, width)]
    all_to_all x1 -> x0, blocking collectives: 54.3 us -> none  [per_device(): lax.all_to_all(outgoing, ('row', 'col'), split_axis=0, concat_axis=0, til...]
    reshape x34 -> x0, local copies, waits for them, and re-layouts: 42.4 us -> none  [the longest x30 26.3 us: multiply(): return total + term.reshape(2, width, width)]
    scatter x2 -> x0, local copies, waits for them, and re-layouts: 29 us -> none  [per_device(): jnp.zeros((devices, capacity, BS * BS), jnp.bfloat16).at[targets, slots]]
    dot_general x32 -> x0, matrix products: 16.3 us -> none  [multiply(): jnp.dot(left_now.reshape(2 * width, width), piece, preferred_element_type...]
  transfers between devices with their start and end apart: 69 -> 0, of which waited for: 37 -> 0; matrix products, arithmetic and copies ran while one was open for 0% -> 0% of each run, Pallas kernels for 0% -> 0%
where the time goes in v3:
time: 126 us
  Pallas kernels  124 us (98%)
  local copies, waits for them, and re-layouts  1.58 us (1%)
    pallas_call x1, Pallas kernels, stepped(): pl.pallas_call(whole_step, out_shape=jax.ShapeDtypeStruct((DEVICES * ROWS...  121 us
    pallas_call x1, Pallas kernels, unpacked(): pl.pallas_call(unpack, out_shape=jax.ShapeDtypeStruct((CAP, ENT, DEVICES)...  2.97 us

profile of v3, /device:TPU:1, one launch (start us, length us, event | category | flops | bytes accessed | tf_op | source)
XLA Modules:
  0.0 125.8 jit_solution(2385538611919564550)
XLA Ops:
  0.0 121.2 %whole_step.1.arrived = bf16[2048,512]{1,0:T(8,128)(2,1)} custom-call(bf16[2,368,368]{2,1,0:T(8,128)(2,1)} %dens_in.1, s32[2,16,16]{2,1,0:T(8,128)} %pat_in.1, s32[2,16,16]{2,1,0:T(8,128)} %keep_in.1, s32[1,512]{1,0:T(1,128)} %bitcast.4), custom_call_target="tpu_custom_call" | custom-call | tf_op jit(solution)/shard_map/whole_step/pallas_call | solution.py:402
  121.2 0.0 copy-start
  121.2 1.6 %copy-done = bf16[2048,512]{1,0:T(8,128)(2,1)S(1)} copy-done((bf16[2048,512]{1,0:T(8,128)(2,1)S(1)}, bf16[2048,512]{1,0:T(8,128)(2,1)}, u32[]{:S(2)}) %copy-start) | copy-done | bytes 2097176
  122.8 3.0 %unpack.1 = bf16[12,529,128]{2,1,0:T(8,128)(2,1)} custom-call(bf16[2048,512]{1,0:T(8,128)(2,1)S(1)} %copy-done), custom_call_target="tpu_custom_call" | custom-call | tf_op jit(solution)/shard_map/unpack/pallas_call | solution.py:448
Async XLA Ops:
  121.2 1.6 %copy-start = (bf16[2048,512]{1,0:T(8,128)(2,1)S(1)}, bf16[2048,512]{1,0:T(8,128)(2,1)}, u32[]{:S(2)}) copy-start(bf16[2048,512]{1,0:T(8,128)(2,1)} %whole_step.1.arrived) | copy-start | bytes 6291460

commit v4 on v3

v4 whole, which is shorter than its diff:
```python
import jax
import jax.numpy as jnp
from jax import lax
from jax.experimental import pallas as pl
from jax.experimental.pallas import tpu as pltpu
from jax.sharding import PartitionSpec as P

BS = 23
PB = 16
W = BS * PB
WP = 384
ORDER = 5888
NROW = 8
NCOL = 16
DEVICES = NROW * NCOL
CAP = 12
ENT = BS * BS
ROWS = 16
LANES = 384
TAIL = 21
MESH = pl.DeviceIdType.MESH
F32 = jnp.float32
BF16 = jnp.bfloat16


QUARTERS = ((0, 0, 192), (0, 192, W), (1, 0, 192), (1, 192, W))

OWN, SEND, WAIT, DO = range(4)
LEFT, SIBLING, RIGHT, SQUARE = range(4)
CORE, YA, YB, YY, ZP, ZM, XP, XM = range(8)
PREPARE, EARLY, NEAR_OWN, FAR_OWN, NEAR_OTHER, FAR_OTHER = range(6)
FIRST_GATHER = (
    (OWN, 0), (SEND, LEFT, 1, 0, 0, LEFT, 0, 0, ZM), (SEND, LEFT, -1, 0, 0, LEFT, 0, 0, ZP),
    (SEND, RIGHT, -1, 0, 0, RIGHT, 0, 0, XP), (SEND, LEFT, -1, 0, 1, LEFT, 0, 0, ZP),
    (SEND, RIGHT, 1, 0, 1, RIGHT, 0, 0, XM), (SEND, LEFT, 0, 1, 0, LEFT, 0, 0, YA),
    (SEND, LEFT, 1, 0, 1, LEFT, 0, 0, ZM), (SEND, RIGHT, 1, 0, 0, RIGHT, 0, 0, XM),
    (SEND, RIGHT, -1, 0, 1, RIGHT, 0, 0, XP), (SEND, LEFT, 0, 1, 1, LEFT, 0, 0, YA),
    (SEND, SIBLING, 0, 0, 0, LEFT, 0, 0, CORE), (SEND, SIBLING, 0, 0, 1, LEFT, 0, 0, CORE), (OWN, 1),
    (SEND, SIBLING, 0, 0, 2, LEFT, 0, 0, CORE), (SEND, SIBLING, 0, 0, 3, LEFT, 0, 0, CORE), (DO, PREPARE),
    (SEND, RIGHT, -1, 0, 2, RIGHT, 0, 0, XP), (SEND, LEFT, 1, 0, 2, LEFT, 0, 0, ZM),
    (SEND, RIGHT, 1, 0, 2, RIGHT, 0, 0, XM), (SEND, LEFT, 0, 1, 3, LEFT, 0, 0, YA),
    (SEND, LEFT, -1, 0, 2, LEFT, 0, 0, ZP), (WAIT, SIBLING, 0, 0, 0), (WAIT, SIBLING, 0, 0, 1),
    (WAIT, SIBLING, 0, 0, 2), (WAIT, SIBLING, 0, 0, 3), (WAIT, LEFT, 1, 0, 0),
    (SEND, SIBLING, 1, 0, 0, LEFT, 1, 0, CORE), (WAIT, LEFT, -1, 0, 0), (SEND, SIBLING, -1, 0, 0, LEFT, -1, 0, CORE),
    (SEND, LEFT, 2, 0, 0, LEFT, 1, 0, ZM), (WAIT, RIGHT, 1, 0, 1), (SEND, LEFT, 0, 1, 2, LEFT, 0, 0, YA),
    (SEND, RIGHT, -1, 0, 3, RIGHT, 0, 0, XP), (SEND, RIGHT, 1, 0, 3, RIGHT, 0, 0, XM),
    (SEND, LEFT, -1, 0, 3, LEFT, 0, 0, ZP), (WAIT, RIGHT, -1, 0, 0), (WAIT, LEFT, 0, 1, 0),
    (SEND, RIGHT, 0, 1, 0, LEFT, 0, 1, YB), (SEND, SIBLING, 0, 1, 0, LEFT, 0, 1, CORE), (WAIT, SIBLING, 1, 0, 0),
    (WAIT, SIBLING, -1, 0, 0), (WAIT, LEFT, 1, 0, 1), (SEND, SIBLING, 1, 0, 1, LEFT, 1, 0, CORE),
    (WAIT, SIBLING, 0, 1, 0), (WAIT, LEFT, -1, 0, 1), (SEND, SIBLING, -1, 0, 1, LEFT, -1, 0, CORE),
    (WAIT, RIGHT, -1, 0, 1), (SEND, LEFT, 2, 0, 1, LEFT, -1, 0, ZP), (SEND, LEFT, 1, 0, 3, LEFT, 0, 0, ZM),
    (SEND, RIGHT, 2, 0, 1, RIGHT, 1, 0, XM), (WAIT, RIGHT, 1, 0, 0), (SEND, LEFT, 1, 1, 0, LEFT, 1, 0, YA),
    (WAIT, LEFT, 0, 1, 1), (SEND, RIGHT, 0, 1, 1, LEFT, 0, 1, YB), (SEND, SIBLING, 0, 1, 1, LEFT, 0, 1, CORE),
    (WAIT, SIBLING, 1, 0, 1), (WAIT, SIBLING, -1, 0, 1), (WAIT, SIBLING, 0, 1, 1), (WAIT, LEFT, 1, 0, 2),
    (SEND, SIBLING, 1, 0, 2, LEFT, 1, 0, CORE), (SEND, LEFT, -1, 1, 1, LEFT, 0, 1, ZP),
    (SEND, LEFT, 2, 0, 2, LEFT, 1, 0, ZM), (WAIT, LEFT, -1, 0, 2), (SEND, RIGHT, 2, 0, 0, RIGHT, 1, 0, XM),
    (SEND, SIBLING, -1, 0, 2, LEFT, -1, 0, CORE), (WAIT, RIGHT, -1, 0, 2), (SEND, RIGHT, 2, 0, 2, RIGHT, -1, 0, XP),
    (WAIT, LEFT, 0, 1, 3), (SEND, SIBLING, 0, 1, 3, LEFT, 0, 1, CORE), (SEND, LEFT, 1, 1, 1, LEFT, 1, 0, YA),
    (SEND, RIGHT, 0, 1, 3, LEFT, 0, 1, YB), (WAIT, RIGHT, 1, 0, 2), (WAIT, RIGHT, 0, 1, 0),
    (SEND, RIGHT, -1, 1, 0, RIGHT, 0, 1, XP), (WAIT, SIBLING, 1, 0, 2), (WAIT, SIBLING, -1, 0, 2),
    (WAIT, SIBLING, 0, 1, 3), (WAIT, LEFT, -1, 0, 3), (SEND, LEFT, -1, 1, 3, LEFT, 0, 1, ZP),
    (SEND, SIBLING, -1, 0, 3, LEFT, -1, 0, CORE), (WAIT, RIGHT, -1, 0, 3), (WAIT, LEFT, 2, 0, 0),
    (SEND, LEFT, 1, 1, 3, LEFT, 0, 1, ZM), (SEND, SIBLING, 2, 0, 0, LEFT, 2, 0, CORE), (WAIT, RIGHT, 1, 0, 3),
    (SEND, RIGHT, 1, 1, 0, RIGHT, 0, 1, XM), (SEND, LEFT, -1, 1, 0, LEFT, -1, 0, YA), (WAIT, RIGHT, 0, 1, 1),
    (SEND, RIGHT, -1, 1, 1, RIGHT, 0, 1, XP), (WAIT, LEFT, 0, 1, 2), (SEND, RIGHT, 0, 1, 2, LEFT, 0, 1, YB),
    (SEND, SIBLING, 0, 1, 2, LEFT, 0, 1, CORE), (WAIT, SIBLING, -1, 0, 3), (WAIT, SIBLING, 2, 0, 0),
    (WAIT, LEFT, 2, 0, 1), (SEND, SIBLING, 2, 0, 1, LEFT, 2, 0, CORE), (SEND, LEFT, -1, 1, 2, LEFT, 0, 1, ZP),
    (WAIT, SIBLING, 0, 1, 2), (WAIT, LEFT, 1, 0, 3), (SEND, LEFT, 2, 0, 3, LEFT, 1, 0, ZM),
    (SEND, SIBLING, 1, 0, 3, LEFT, 1, 0, CORE), (WAIT, RIGHT, 2, 0, 1), (WAIT, RIGHT, 0, 1, 3),
    (SEND, RIGHT, -1, 1, 3, RIGHT, 0, 1, XP), (SEND, RIGHT, 1, 1, 3, RIGHT, 0, 1, XM),
    (SEND, RIGHT, 1, 1, 2, RIGHT, 1, 0, YY), (WAIT, RIGHT, 2, 0, 2), (WAIT, LEFT, 1, 1, 0),
    (SEND, SIBLING, 1, 1, 0, LEFT, 1, 1, CORE), (WAIT, SIBLING, 2, 0, 1), (WAIT, SIBLING, 1, 0, 3),
    (WAIT, SIBLING, 1, 1, 0), (WAIT, LEFT, -1, 1, 1), (SEND, SIBLING, -1, 1, 1, LEFT, -1, 1, CORE),
    (WAIT, LEFT, 2, 0, 2), (SEND, SIBLING, 2, 0, 2, LEFT, 2, 0, CORE), (SEND, LEFT, 1, 1, 2, LEFT, 0, 1, ZM),
    (WAIT, RIGHT, 2, 0, 0), (WAIT, RIGHT, -1, 1, 0), (SEND, RIGHT, 1, 1, 1, RIGHT, 0, 1, XM), (WAIT, LEFT, 1, 1, 1),
    (SEND, SIBLING, 1, 1, 1, LEFT, 1, 1, CORE), (WAIT, RIGHT, 0, 1, 2), (SEND, RIGHT, -1, 1, 2, RIGHT, 0, 1, XP),
    (SEND, LEFT, 2, 1, 2, LEFT, 2, 0, YA), (WAIT, SIBLING, -1, 1, 1), (WAIT, SIBLING, 2, 0, 2),
    (WAIT, SIBLING, 1, 1, 1), (WAIT, LEFT, -1, 1, 3), (SEND, LEFT, 2, 1, 3, LEFT, -1, 1, ZP),
    (SEND, SIBLING, -1, 1, 3, LEFT, -1, 1, CORE), (WAIT, LEFT, 1, 1, 3), (SEND, SIBLING, 1, 1, 3, LEFT, 1, 1, CORE),
    (WAIT, RIGHT, -1, 1, 1), (SEND, LEFT, 2, 1, 1, LEFT, 1, 1, ZM), (WAIT, RIGHT, 1, 1, 0),
    (SEND, RIGHT, 2, 0, 3, RIGHT, 1, 0, XM), (SEND, RIGHT, 2, 1, 1, RIGHT, -1, 1, XP), (WAIT, LEFT, -1, 1, 0),
    (SEND, LEFT, 2, 1, 0, LEFT, -1, 1, ZP), (SEND, SIBLING, -1, 1, 0, LEFT, -1, 1, CORE), (WAIT, SIBLING, -1, 1, 3),
    (SEND, RIGHT, 2, 1, 0, RIGHT, 2, 0, YY), (WAIT, SIBLING, 1, 1, 3), (WAIT, SIBLING, -1, 1, 0),
    (WAIT, LEFT, -1, 1, 2), (SEND, SIBLING, -1, 1, 2, LEFT, -1, 1, CORE), (WAIT, LEFT, 2, 0, 3),
    (SEND, SIBLING, 2, 0, 3, LEFT, 2, 0, CORE), (WAIT, RIGHT, -1, 1, 3), (WAIT, RIGHT, 1, 1, 3),
    (SEND, RIGHT, 2, 1, 3, RIGHT, -1, 1, XP), (WAIT, SIBLING, -1, 1, 2), (WAIT, RIGHT, 1, 1, 2),
    (SEND, RIGHT, 2, 1, 2, RIGHT, 1, 1, XM), (WAIT, SIBLING, 2, 0, 3), (WAIT, LEFT, 2, 1, 3),
    (SEND, SIBLING, 2, 1, 3, LEFT, 2, 1, CORE), (WAIT, LEFT, 1, 1, 2), (SEND, SIBLING, 1, 1, 2, LEFT, 1, 1, CORE),
    (WAIT, RIGHT, 1, 1, 1), (WAIT, RIGHT, -1, 1, 2), (WAIT, LEFT, 2, 1, 2),
    (SEND, SIBLING, 2, 1, 2, LEFT, 2, 1, CORE), (WAIT, SIBLING, 2, 1, 3), (WAIT, SIBLING, 1, 1, 2),
    (WAIT, SIBLING, 2, 1, 2), (WAIT, LEFT, 2, 1, 0), (SEND, SIBLING, 2, 1, 0, LEFT, 2, 1, CORE),
    (WAIT, LEFT, 2, 1, 1), (SEND, SIBLING, 2, 1, 1, LEFT, 2, 1, CORE), (WAIT, RIGHT, 2, 0, 3), (DO, EARLY),
    (WAIT, RIGHT, 2, 1, 1), (WAIT, SIBLING, 2, 1, 0), (WAIT, RIGHT, 2, 1, 0), (WAIT, SIBLING, 2, 1, 1),
    (WAIT, RIGHT, 2, 1, 3), (WAIT, RIGHT, 2, 1, 2),
)

SECOND_GATHER = (
    (OWN, 0), (SEND, SQUARE, 1, 0, 0, SQUARE, 0, 0, XM), (SEND, SQUARE, -1, 0, 1, SQUARE, 0, 0, XP),
    (SEND, SQUARE, -1, 0, 0, SQUARE, 0, 0, XP), (SEND, SQUARE, 0, 1, 1, SQUARE, 0, 0, YY),
    (SEND, SQUARE, 0, 1, 0, SQUARE, 0, 0, YY), (SEND, SQUARE, 1, 0, 1, SQUARE, 0, 0, XM), (OWN, 1),
    (WAIT, SQUARE, -1, 0, 1), (SEND, SQUARE, -1, 0, 3, SQUARE, 0, 0, XP), (SEND, SQUARE, 0, 1, 2, SQUARE, 0, 0, YY),
    (SEND, SQUARE, -1, 0, 2, SQUARE, 0, 0, XP), (SEND, SQUARE, 1, 0, 2, SQUARE, 0, 0, XM),
    (SEND, SQUARE, 1, 0, 3, SQUARE, 0, 0, XM), (WAIT, SQUARE, 1, 0, 0), (WAIT, SQUARE, 0, 1, 1),
    (SEND, SQUARE, 1, 1, 0, SQUARE, 1, 0, YY), (WAIT, SQUARE, 1, 0, 1), (WAIT, SQUARE, -1, 0, 0),
    (WAIT, SQUARE, 0, 1, 0), (SEND, SQUARE, 2, 0, 0, SQUARE, -1, 0, XP), (SEND, SQUARE, 2, 0, 1, SQUARE, 1, 0, XM),
    (SEND, SQUARE, 0, 1, 3, SQUARE, 0, 0, YY), (WAIT, SQUARE, -1, 0, 3), (WAIT, SQUARE, 1, 0, 2),
    (SEND, SQUARE, 1, 1, 1, SQUARE, 0, 1, XM), (WAIT, SQUARE, 0, 1, 2), (SEND, SQUARE, -1, 1, 0, SQUARE, 0, 1, XP),
    (SEND, SQUARE, 1, 1, 2, SQUARE, 1, 0, YY), (WAIT, SQUARE, 1, 0, 3), (SEND, SQUARE, 2, 0, 3, SQUARE, 1, 0, XM),
    (WAIT, SQUARE, -1, 0, 2), (DO, NEAR_OWN), (SEND, SQUARE, 2, 0, 2, SQUARE, -1, 0, XP),
    (SEND, SQUARE, -1, 1, 2, SQUARE, -1, 0, YY), (WAIT, SQUARE, 1, 1, 0), (WAIT, SQUARE, 2, 0, 1),
    (WAIT, SQUARE, 2, 0, 0), (WAIT, SQUARE, 0, 1, 3), (SEND, SQUARE, 2, 1, 0, SQUARE, 2, 0, YY),
    (SEND, SQUARE, 1, 1, 3, SQUARE, 0, 1, XM), (SEND, SQUARE, -1, 1, 3, SQUARE, 0, 1, XP), (WAIT, SQUARE, 1, 1, 1),
    (SEND, SQUARE, 2, 1, 1, SQUARE, 1, 1, XM), (WAIT, SQUARE, -1, 1, 0), (WAIT, SQUARE, 1, 1, 2),
    (SEND, SQUARE, -1, 1, 1, SQUARE, 0, 1, XP), (WAIT, SQUARE, 2, 0, 3), (WAIT, SQUARE, 2, 0, 2),
    (SEND, SQUARE, 2, 1, 2, SQUARE, 2, 0, YY), (DO, FAR_OWN), (WAIT, SQUARE, -1, 1, 2), (WAIT, SQUARE, 1, 1, 3),
    (SEND, SQUARE, 2, 1, 3, SQUARE, 1, 1, XM), (WAIT, SQUARE, -1, 1, 3), (WAIT, SQUARE, 2, 1, 0),
    (WAIT, SQUARE, 2, 1, 1), (WAIT, SQUARE, -1, 1, 1), (DO, NEAR_OTHER), (WAIT, SQUARE, 2, 1, 2),
    (WAIT, SQUARE, 2, 1, 3), (DO, FAR_OTHER),
)


def grow_columns(mask):
    block = lax.broadcasted_iota(jnp.int32, (PB, WP), 0)
    col = lax.broadcasted_iota(jnp.int32, (PB, WP), 1)
    spread = jnp.where((col >= block * BS) & (col < block * BS + BS), 1.0, 0.0).astype(BF16)
    return jnp.dot(mask, spread, preferred_element_type=F32).astype(BF16)


def grow(mask):
    wide = grow_columns(mask.astype(F32).astype(BF16))
    row = lax.broadcasted_iota(jnp.int32, (W, PB), 0)
    block = lax.broadcasted_iota(jnp.int32, (W, PB), 1)
    spread = jnp.where((row >= block * BS) & (row < block * BS + BS), 1.0, 0.0).astype(BF16)
    return jnp.dot(spread, wide, preferred_element_type=F32)


def whole_step(
    dens_in, pat_in, keep_in, owner_in, arrived, tails_arrived,
    dens, pat, keep, owner, left, right, sq, mask, kept, acc, update, place, hot, hot_tail, rank_at, tail_at, blocks, outgoing,
    tails, relay_in, relay_wide, relay_out, send, recv, exchange_send, exchange_recv, tail_send, tail_recv, local,
):
    r = lax.axis_index("row")
    c = lax.axis_index("col")
    x, yh = lax.rem(r, 4), lax.div(r, 4)
    z, yl, core = lax.div(c, 4), lax.rem(lax.div(c, 2), 2), lax.rem(c, 2)
    me = r * NCOL + c

    def col(dz, dyl, dcore=0):
        ycol = (1 - yl) if dyl else yl
        ccol = (1 - core) if dcore else core
        return lax.rem(z + dz + 4, 4) * 4 + ycol * 2 + ccol

    def row(dx, dyh):
        yrow = (1 - yh) if dyh else yh
        return yrow * 4 + lax.rem(x + dx + 4, 4)

    ways = {
        CORE: (r, col(0, 0, 1)),
        YA: (r, col(0, 1)),
        YB: (row(0, 1), col(0, 1)),
        YY: (row(0, 1), c),
        ZP: (r, col(1, 0)),
        ZM: (r, col(-1, 0)),
        XP: (row(1, 0), c),
        XM: (row(-1, 0), c),
    }

    fetches = [
        pltpu.make_async_copy(src, dst, local.at[k])
        for k, (src, dst) in enumerate(((pat_in, pat), (dens_in, dens), (keep_in, keep), (owner_in, owner)))
    ]
    for fetch in fetches:
        fetch.start()
    barrier = pltpu.get_barrier_semaphore()
    for dev in ways.values():
        pl.semaphore_signal(barrier, inc=1, device_id=dev, device_id_type=MESH)

    started = []
    arriving = {}

    def piece(buf, slot, q):
        h, first, end = QUARTERS[q]
        return buf.at[slot, h, pl.ds(first, end - first)]

    def find(kind, d, f, q):
        if kind == LEFT:
            return piece(left, col(d, f), q)
        if kind == SIBLING:
            return piece(left, col(d, f, 1), q)
        return piece(right if kind == RIGHT else sq, row(d, f), q)

    def start(kind, d, f, q, from_kind, from_d, from_f, way):
        k = len(started)
        if kind == RIGHT:
            src = piece(left, c, q) if (from_d, from_f) == (0, 0) else find(from_kind, from_d, from_f, q)
            dst = piece(right, r if from_kind == LEFT else row(from_d, from_f), q)
        else:
            src = dst = find(from_kind, from_d, from_f, q)
        op = pltpu.make_async_remote_copy(
            src_ref=src, dst_ref=dst, send_sem=send.at[k], recv_sem=recv.at[k],
            device_id=ways[way], device_id_type=MESH)
        op.start()
        started.append(op)
        here = find(kind, d, f, q)
        arriving[kind, d, f, q] = pltpu.make_async_remote_copy(
            src_ref=here, dst_ref=here, send_sem=send.at[k], recv_sem=recv.at[k],
            device_id=ways[way], device_id_type=MESH)

    def follow(table, own, work):
        for op, *what in table:
            if op == OWN:
                own(what[0])
            elif op == SEND:
                start(*what)
            elif op == WAIT:
                arriving[tuple(what)].wait_recv()
            else:
                work[what[0]]()

    def multiply(p, buf, h, fresh=False):
        if h is None:
            two = [left[2 * p + k].reshape(2 * W, WP) for k in range(2)]
            at = pl.ds(0, 2 * W)
        else:
            two = [left[2 * p + k, h] for k in range(2)]
            at = pl.ds(h * W, W)
        rows = buf[pl.ds(lax.rem(2 * p, NROW), 2), lax.div(p, 4)].reshape(2 * WP, WP)
        term = jnp.dot(jnp.concatenate(two, axis=1), rows, preferred_element_type=F32)
        acc[at, :] = term if fresh else acc[at, :] + term

    def is_late(p):
        zp, yp = lax.div(p, 2), lax.rem(p, 2)
        in_left = (zp == lax.rem(z + 2, 4)) & (yp == 1 - yl)
        in_right = (lax.rem(zp, 2) == 1 - yh) & (yp == lax.div(lax.rem(x + 2, 4), 2))
        return in_left | in_right

    def own_density(h):
        m = grow(pat[h]).astype(BF16)
        left[c, h, :, pl.ds(256, 128)] = jnp.zeros((W, 128), BF16)
        left[c, h, :, pl.ds(0, W)] = dens[h] * m[:, :W]
        mask[h] = m
        if h == 0:
            pl.semaphore_wait(barrier, len(ways))

    def prepare():
        for h in range(2):
            right[r, h, pl.ds(0, W)] = left[c, h]
        zero = jnp.zeros((2, WP - W, WP), BF16)

        def clear(k, carry):
            right[k, :, pl.ds(W, WP - W)] = zero
            sq[k, :, pl.ds(W, WP - W)] = zero
            return carry

        lax.fori_loop(0, NROW, clear, 0)
        acc[...] = jnp.zeros_like(acc)
        fetches[2].wait()
        fetches[3].wait()
        for h in range(2):
            kept[h] = grow(keep[h]).astype(BF16)
        routing_tables(owner, place, hot, hot_tail, rank_at, tail_at)

    def early():
        def add(p, carry):
            @pl.when(jnp.logical_not(is_late(p)))
            def _():
                multiply(p, right, None)
            return carry

        lax.fori_loop(0, NCOL // 2, add, 0)

    fetches[0].wait()
    fetches[1].wait()
    follow(FIRST_GATHER, own_density, {PREPARE: prepare, EARLY: early})

    def own_square(h):
        def add(p, carry):
            @pl.when(is_late(p))
            def _():
                multiply(p, right, h)
            return carry

        lax.fori_loop(0, NCOL // 2, add, 0)
        sq[r, h, pl.ds(0, W)] = (acc[pl.ds(h * W, W), :] / ORDER * mask[h].astype(F32)).astype(BF16)

    near = lax.div(x, 2)

    def second(yhp, pair, fresh=False):
        for h in range(2):
            multiply((2 * h + yhp) * 2 + pair, sq, None, fresh and h == 0)

    follow(SECOND_GATHER, own_square, {
        NEAR_OWN: lambda: second(yh, near, True),
        FAR_OWN: lambda: second(yh, 1 - near),
        NEAR_OTHER: lambda: second(1 - yh, near),
        FAR_OTHER: lambda: second(1 - yh, 1 - near),
    })

    for h in range(2):
        mat = left[c, h].astype(F32)
        new = kept[h].astype(F32) * (1.5 * mat - 0.5 * acc[pl.ds(h * W, W), :])
        for k in range(WP // 128):
            update[h, k] = new[:, k * 128 : k * 128 + 128]

    fill(update, rank_at, tail_at, place, hot, hot_tail, blocks, outgoing, tails)

    def partner(i, sign):
        dcore, dz = lax.rem(i, 2), lax.rem(lax.div(i, 2), 4)
        dyl, dyh, dx = lax.rem(lax.div(i, 8), 2), lax.rem(lax.div(i, 16), 2), lax.div(i, 32)
        to_row = lax.rem(yh + dyh, 2) * 4 + lax.rem(x + sign * dx + 4, 4)
        to_col = lax.rem(z + sign * dz + 4, 4) * 4 + lax.rem(yl + dyl, 2) * 2 + lax.rem(core + dcore, 2)
        return to_row, to_col

    def rows_of(buf, device):
        return buf.at[pl.ds(pl.multiple_of(device * ROWS, ROWS), ROWS)]

    def message(i):
        to_row, to_col = partner(i, 1)
        return pltpu.make_async_remote_copy(
            src_ref=rows_of(outgoing, to_row * NCOL + to_col), dst_ref=rows_of(arrived, me),
            send_sem=exchange_send.at[i], recv_sem=exchange_recv.at[i],
            device_id=(to_row, to_col), device_id_type=MESH)

    def arrival(i):
        from_row, from_col = partner(i, -1)
        here = rows_of(arrived, from_row * NCOL + from_col)
        return pltpu.make_async_remote_copy(
            src_ref=here, dst_ref=here, send_sem=exchange_send.at[i], recv_sem=exchange_recv.at[i],
            device_id=(from_row, from_col), device_id_type=MESH)

    def start_message(i, carry):
        message(lax.rem(i * 37, DEVICES)).start()
        return carry

    def finish_message(i, carry):
        arrival(lax.rem(i * 37, DEVICES)).wait_recv()
        return carry

    def message_sent(i, carry):
        message(i).wait_send()
        return carry

    line, in_line = r * 2 + yl, z * 2 + core

    def other_line(i):
        dyl, dyh, dx = i % 2, i // 2 % 2, i // 4
        return row(dx, dyh), yl if dyl == 0 else 1 - yl

    def line_copy(i, to_line, here_line, device):
        return pltpu.make_async_remote_copy(
            src_ref=rows_of(tails, to_line), dst_ref=rows_of(relay_in, here_line),
            send_sem=tail_send.at[i], recv_sem=tail_recv.at[i], device_id=device, device_id_type=MESH)

    def pass_on(i, to, here, device):
        return pltpu.make_async_remote_copy(
            src_ref=rows_of(relay_out, to), dst_ref=rows_of(tails_arrived, here),
            send_sem=tail_send.at[i], recv_sem=tail_recv.at[i], device_id=device, device_id_type=MESH)

    tail_ops = []
    tail_waits = []
    for i in range(1, 2 * NROW):
        to_row, to_yl = other_line(i)
        device = (to_row, z * 4 + to_yl * 2 + core)
        op = line_copy(i, to_row * 2 + to_yl, line, device)
        op.start()
        tail_ops.append(op)
        from_row = row(-(i // 4), i // 2 % 2)
        tail_waits.append(line_copy(i, line, from_row * 2 + to_yl, device))
    keep_line = pltpu.make_async_copy(rows_of(tails, line), rows_of(relay_in, line), local.at[5])
    keep_line.start()
    own = pltpu.make_async_copy(rows_of(outgoing, me), rows_of(arrived, me), local.at[4])
    own.start()
    lax.fori_loop(1, DEVICES // 2, start_message, 0)
    keep_line.wait()
    for op in tail_waits:
        op.wait_recv()
    relay_wide[...] = relay_in[...].astype(F32)
    for j in range(2 * 4):
        for k in range(2):
            part = relay_wide[pl.ds(2 * j + k, 2 * NROW, stride=ROWS), :]
            relay_out[pl.ds(j * ROWS, ROWS), pl.ds(128 * k, 128)] = part.astype(BF16)
    pass_waits = []
    for i in range(1, 2 * 4):
        to_core = core if i % 2 == 0 else 1 - core
        to_z, from_z = lax.rem(z + i // 2, 4), lax.rem(z + 4 - i // 2, 4)
        device = (r, to_z * 4 + yl * 2 + to_core)
        op = pass_on(2 * NROW + i, to_z * 2 + to_core, in_line, device)
        op.start()
        tail_ops.append(op)
        pass_waits.append(pass_on(2 * NROW + i, in_line, from_z * 2 + to_core, device))
    keep_tails = pltpu.make_async_copy(rows_of(relay_out, in_line), rows_of(tails_arrived, in_line), local.at[6])
    keep_tails.start()
    lax.fori_loop(DEVICES // 2, DEVICES, start_message, 0)
    for op in started:
        op.wait_send()
    own.wait()
    keep_tails.wait()
    lax.fori_loop(1, DEVICES, finish_message, 0)
    for op in pass_waits:
        op.wait_recv()
    lax.fori_loop(1, DEVICES, message_sent, 0)
    for op in tail_ops:
        op.wait_send()


N_BLOCKS = 2 * PB * PB
WINDOWS = [
    (w, i) for w in range(3) for i in range(BS) if i * BS + BS > w * 256 and i * BS < w * 256 + 256
]


def ranks(owner_row):
    owner = jnp.broadcast_to(owner_row.astype(F32), (8, N_BLOCKS))
    same = owner.T[:, :1] == owner[:1]
    one = lax.broadcasted_iota(jnp.int32, (N_BLOCKS, N_BLOCKS), 0)
    two = lax.broadcasted_iota(jnp.int32, (N_BLOCKS, N_BLOCKS), 1)
    rank = jnp.sum(jnp.where(same & (one < two), 1.0, 0.0), axis=0, keepdims=True).astype(jnp.int32)
    rank_col = jnp.sum(jnp.where(same & (two < one), 1.0, 0.0), axis=1, keepdims=True).astype(jnp.int32)
    return rank, rank_col


def routing_tables(owner, place, hot, hot_tail, rank_at, tail_at):
    lane = lax.broadcasted_iota(jnp.int32, (WP, 256), 0)
    at = lax.broadcasted_iota(jnp.int32, (WP, 256), 1)
    entry = lane - lax.div(lane, BS) * BS
    slot = lax.div(at, TAIL)
    for k, (w, i) in enumerate(WINDOWS):
        if w < 2:
            place[k] = jnp.where(at - entry == i * BS - w * 256, 1.0, 0.0).astype(BF16)
        else:
            offset = at - slot * TAIL
            fits = (slot < 6) & (offset - entry == i * BS - w * 256) & (offset < ENT - 512)
            place[k] = jnp.where(fits, 1.0, 0.0).astype(BF16)
    rank, rank_col = ranks(owner[...])
    rank_at[...] = jnp.broadcast_to(rank_col, rank_at.shape)
    group = lax.div(lax.broadcasted_iota(jnp.int32, tail_at.shape, 1), TAIL)
    tail_at[...] = jnp.where(rank_col - lax.div(rank_col, 6) * 6 == group, 1.0, 0.0)
    own = owner[...]
    key = own * ROWS + rank
    last_key = own * ROWS + CAP + rank - lax.div(rank, 4) * 4
    to_row, to_col = lax.div(own, NCOL), lax.rem(own, NCOL)
    line = to_row * 2 + lax.rem(lax.div(to_col, 2), 2)
    in_line = lax.div(to_col, 4) * 2 + lax.rem(to_col, 2)
    tail_key = line * ROWS + in_line * 2 + lax.div(rank, 6)
    step = 512
    for k in range(0, DEVICES * ROWS, step):
        at = lax.broadcasted_iota(jnp.int32, (step, N_BLOCKS), 0) + k
        hot[pl.ds(k, step), pl.ds(0, N_BLOCKS)] = jnp.where(at == key, 1.0, 0.0).astype(BF16)
        hot[pl.ds(k, step), pl.ds(N_BLOCKS, N_BLOCKS)] = jnp.where(at == last_key, 1.0, 0.0).astype(BF16)
    at = lax.broadcasted_iota(jnp.int32, hot_tail.shape, 0)
    hot_tail[...] = jnp.where(at == tail_key, 1.0, 0.0).astype(BF16)


def fill(update, rank_at, tail_at, place, hot, hot_tail, blocks, outgoing, tails):
    n = N_BLOCKS
    half = PB // 2
    picks = []
    for g in range(2):
        bc = lax.broadcasted_iota(jnp.int32, (half, 256), 0) + g * half
        entry = lax.broadcasted_iota(jnp.int32, (half, 256), 1) + g * 128
        picks.append(jnp.where((entry >= bc * BS) & (entry < bc * BS + BS), 1.0, 0.0)[None])
    for w in (2, 0, 1):
        total = [None, None]
        for k, (wk, i) in enumerate(WINDOWS):
            if wk != w:
                continue
            u = [[update[h, j, pl.ds(i, PB, stride=BS), :] for j in range(WP // 128)] for h in range(2)]
            for g in range(2):
                rows = [
                    (jnp.concatenate(u[h][g : g + 2], axis=1)[:, None, :] * picks[g]).astype(BF16)
                    .reshape(PB * half, 256)
                    for h in range(2)
                ]
                term = jnp.dot(jnp.concatenate(rows, axis=0), place[k, pl.ds(128 * g, 256), :],
                               preferred_element_type=F32)
                total[g] = term if total[g] is None else total[g] + term
        both = [t.reshape(2 * PB, 1, half, 256) for t in total]
        both = jnp.concatenate(both, axis=1).reshape(n, 256)
        if w == 2:
            tail = (both[:, :128] * tail_at[...]).astype(BF16)
            tails[...] = jnp.dot(hot_tail[...], tail, preferred_element_type=F32).astype(BF16)
        elif w == 0:
            blocks[pl.ds(0, n), pl.ds(0, 256)] = both.astype(BF16)
        else:
            blocks[pl.ds(0, n), pl.ds(256, 128)] = both[:, :128].astype(BF16)
            rank = rank_at[...]
            for j in range(3):
                mine = (rank >= 4 * j) & (rank < 4 * j + 4)
                blocks[pl.ds(n, n), pl.ds(128 * j, 128)] = jnp.where(mine, both[:, 128:], 0.0).astype(BF16)
    step = 512
    for k in range(0, DEVICES * ROWS, step):
        outgoing[pl.ds(k, step), :] = jnp.dot(
            hot[pl.ds(k, step), :], blocks[...], preferred_element_type=F32).astype(BF16)


N_COPIES = sum(op[0] == SEND for op in FIRST_GATHER + SECOND_GATHER)


def stepped(density, pattern, keep, owner):
    anywhere = pl.BlockSpec(memory_space=pl.ANY)
    owner = owner.reshape(1, N_BLOCKS)
    return pl.pallas_call(
        whole_step,
        out_shape=(
            jax.ShapeDtypeStruct((DEVICES * ROWS, LANES), BF16),
            jax.ShapeDtypeStruct((DEVICES, 256), BF16),
        ),
        in_specs=[anywhere] * 4,
        out_specs=(anywhere, anywhere),
        scratch_shapes=[
            pltpu.VMEM(density.shape, BF16),
            pltpu.VMEM(pattern.shape, jnp.int32),
            pltpu.VMEM(keep.shape, jnp.int32),
            pltpu.VMEM(owner.shape, jnp.int32),
            pltpu.VMEM((NCOL, 2, W, WP), BF16),
            pltpu.VMEM((NROW, 2, WP, WP), BF16),
            pltpu.VMEM((NROW, 2, WP, WP), BF16),
            pltpu.VMEM((2, W, WP), BF16),
            pltpu.VMEM((2, W, WP), BF16),
            pltpu.VMEM((2 * W, WP), F32),
            pltpu.VMEM((2, WP // 128, W, 128), F32),
            pltpu.VMEM((len(WINDOWS), WP, 256), BF16),
            pltpu.VMEM((DEVICES * ROWS, 2 * N_BLOCKS), BF16),
            pltpu.VMEM((2 * NROW * ROWS, N_BLOCKS), BF16),
            pltpu.VMEM((N_BLOCKS, 128), jnp.int32),
            pltpu.VMEM((N_BLOCKS, 128), F32),
            pltpu.VMEM((2 * N_BLOCKS, LANES), BF16),
            pltpu.VMEM((DEVICES * ROWS, LANES), BF16),
            pltpu.VMEM((2 * NROW * ROWS, 128), BF16),
            pltpu.VMEM((2 * NROW * ROWS, 128), BF16),
            pltpu.VMEM((2 * NROW * ROWS, 128), F32),
            pltpu.VMEM((DEVICES, 256), BF16),
            pltpu.SemaphoreType.DMA((N_COPIES,)),
            pltpu.SemaphoreType.DMA((N_COPIES,)),
            pltpu.SemaphoreType.DMA((DEVICES,)),
            pltpu.SemaphoreType.DMA((DEVICES,)),
            pltpu.SemaphoreType.DMA((2 * NROW + 8,)),
            pltpu.SemaphoreType.DMA((2 * NROW + 8,)),
            pltpu.SemaphoreType.DMA((7,)),
        ],
        compiler_params=pltpu.CompilerParams(
            collective_id=0, has_side_effects=True, vmem_limit_bytes=56 * 1024 * 1024),
        name="whole_step",
    )(density, pattern, keep, owner)


def unpack(messages, tails, out, arrived, tails_in, wide, tails_wide, by_source, ready, sem):
    chunks = [pl.ds(128 * k, 128) for k in range(LANES // 128)]
    fetches = [
        pltpu.make_async_copy(messages.at[:, at], arrived.at[:, at], sem.at[CAP + k])
        for k, at in enumerate(chunks)
    ]
    fetch_tails = pltpu.make_async_copy(tails, tails_in, sem.at[CAP + len(chunks)])
    fetch_tails.start()
    for fetch in fetches:
        fetch.start()

    fetch_tails.wait()
    for k in range(2):
        tails_wide[k] = tails_in[:, pl.ds(128 * k, 128)].astype(F32)
        for j in range(8):
            for yl in range(2):
                source = j // 2 * 4 + yl * 2 + j % 2
                by_source[k, pl.ds(source, NROW, stride=NCOL), :] = tails_wide[k, pl.ds(j * ROWS + yl, NROW, stride=2), :]
        rows = by_source[k].T.astype(BF16)
        for s in range(6):
            ready[6 * k + s, pl.ds(512, ENT - 512), :] = rows[s * TAIL : s * TAIL + ENT - 512]
    copies = []
    for k, at in enumerate(chunks):
        fetches[k].wait()
        wide[k] = arrived[:, at].astype(F32)
        for s in range(4):
            fourth = wide[k, pl.ds(CAP + s, DEVICES, stride=ROWS), :]
            ready[4 * k + s, pl.ds(384, 128), :] = fourth.T.astype(BF16)
        for s in range(CAP):
            ready[s, at, :] = wide[k, pl.ds(s, DEVICES, stride=ROWS), :].T.astype(BF16)
            if k == len(chunks) - 1:
                copies.append(pltpu.make_async_copy(ready.at[s], out.at[s], sem.at[s]))
                copies[-1].start()
    for copy in copies:
        copy.wait()


def unpacked(messages, tails):
    anywhere = pl.BlockSpec(memory_space=pl.ANY)
    out = pl.pallas_call(
        unpack,
        out_shape=jax.ShapeDtypeStruct((CAP, ENT, DEVICES), BF16),
        in_specs=[anywhere] * 2,
        out_specs=anywhere,
        scratch_shapes=[
            pltpu.VMEM((DEVICES * ROWS, LANES), BF16),
            pltpu.VMEM((DEVICES, 256), BF16),
            pltpu.VMEM((LANES // 128, DEVICES * ROWS, 128), F32),
            pltpu.VMEM((2, DEVICES, 128), F32),
            pltpu.VMEM((2, DEVICES, 128), F32),
            pltpu.VMEM((CAP, ENT, DEVICES), BF16),
            pltpu.SemaphoreType.DMA((CAP + 4,)),
        ],
        compiler_params=pltpu.CompilerParams(vmem_limit_bytes=58 * 1024 * 1024),
        name="unpack",
    )(messages, tails)
    return out.transpose(2, 0, 1)[None]


def per_device(density, pattern, keep, owner):
    return unpacked(*stepped(density, pattern, keep, owner))


def solution(mesh):
    placed = (
        P(None, "row", "col"),
        P(None, "row", "col"),
        P(None, "row", "col"),
        P(("row", "col"), None, None),
    )
    return jax.shard_map(
        per_device,
        mesh=mesh,
        in_specs=placed,
        out_specs=P(("row", "col"), None, None, None),
        check_vma=False,
    )
```

time: 126 us -> 113 us (0.90)
  Pallas kernels: 124 us -> 112 us
  local copies, waits for them, and re-layouts: 1.58 us -> 0 us
    pallas_call x1, Pallas kernels: 121 us -> 109 us  [stepped(): pl.pallas_call(whole_step, out_shape=(jax.ShapeDtypeStruct((DEVICES * ROW...]
    unnamed x2 -> x0, local copies, waits for them, and re-layouts: 1.58 us -> none
where the time goes in v4:
time: 113 us; the launch traced here: 112 us
  Pallas kernels  112 us (99%)
    pallas_call x1, Pallas kernels, stepped(): pl.pallas_call(whole_step, out_shape=(jax.ShapeDtypeStruct((DEVICES * ROW...  109 us
    pallas_call x1, Pallas kernels, unpacked(): pl.pallas_call(unpack, out_shape=jax.ShapeDtypeStruct((CAP, ENT, DEVICES)...  3.5 us

profile of v4, /device:TPU:1, one launch (start us, length us, event | category | flops | bytes accessed | tf_op | source)
XLA Modules:
  0.0 112.5 jit_solution(2575498109952989167)
XLA Ops:
  0.0 108.8 %whole_step.1 = (bf16[2048,384]{1,0:T(8,128)(2,1)}, bf16[128,256]{1,0:T(8,128)(2,1)}) custom-call(bf16[2,368,368]{2,1,0:T(8,128)(2,1)} %dens_in.1, s32[2,16,16]{2,1,0:T(8,128)} %pat_in.1, s32[2,16,16]{2,1,0:T(8,128)} %keep_in.1, s32[1,512]{1,0:T(1,128)} %bitcast.4), custom_call_target="tpu_custom_call" | custom-call | tf_op jit(solution)/shard_map/whole_step/pallas_call | solution.py:502
  108.8 3.5 %unpack.1 = bf16[12,529,128]{2,1,0:T(8,128)(2,1)} custom-call(bf16[2048,384]{1,0:T(8,128)(2,1)} %get-tuple-element.7.messages, bf16[128,256]{1,0:T(8,128)(2,1)} %get-tuple-element.8.tails), custom_call_target="tpu_custom_call" | custom-call | tf_op jit(solution)/shard_map/unpack/pallas_call | solution.py:586

commit v5 on v4

--- a/solution.py
+++ b/solution.py
@@ -191,19 +191,20 @@
 
     def start(kind, d, f, q, from_kind, from_d, from_f, way):
         k = len(started)
+        group = 0 if kind in (LEFT, SIBLING) else 1
         if kind == RIGHT:
             src = piece(left, c, q) if (from_d, from_f) == (0, 0) else find(from_kind, from_d, from_f, q)
             dst = piece(right, r if from_kind == LEFT else row(from_d, from_f), q)
         else:
             src = dst = find(from_kind, from_d, from_f, q)
         op = pltpu.make_async_remote_copy(
-            src_ref=src, dst_ref=dst, send_sem=send.at[k], recv_sem=recv.at[k],
+            src_ref=src, dst_ref=dst, send_sem=send.at[group], recv_sem=recv.at[k],
             device_id=ways[way], device_id_type=MESH)
         op.start()
-        started.append(op)
+        started.append(kind)
         here = find(kind, d, f, q)
         arriving[kind, d, f, q] = pltpu.make_async_remote_copy(
-            src_ref=here, dst_ref=here, send_sem=send.at[k], recv_sem=recv.at[k],
+            src_ref=here, dst_ref=here, send_sem=send.at[group], recv_sem=recv.at[k],
             device_id=ways[way], device_id_type=MESH)
 
     def follow(table, own, work):
@@ -217,7 +218,7 @@
             else:
                 work[what[0]]()
 
-    def multiply(p, buf, h, fresh=False):
+    def multiply(p, buf, h):
         if h is None:
             two = [left[2 * p + k].reshape(2 * W, WP) for k in range(2)]
             at = pl.ds(0, 2 * W)
@@ -225,8 +226,7 @@
             two = [left[2 * p + k, h] for k in range(2)]
             at = pl.ds(h * W, W)
         rows = buf[pl.ds(lax.rem(2 * p, NROW), 2), lax.div(p, 4)].reshape(2 * WP, WP)
-        term = jnp.dot(jnp.concatenate(two, axis=1), rows, preferred_element_type=F32)
-        acc[at, :] = term if fresh else acc[at, :] + term
+        acc[at, :] += jnp.dot(jnp.concatenate(two, axis=1), rows, preferred_element_type=F32)
 
     def is_late(p):
         zp, yp = lax.div(p, 2), lax.rem(p, 2)
@@ -281,16 +281,21 @@
             return carry
 
         lax.fori_loop(0, NCOL // 2, add, 0)
-        sq[r, h, pl.ds(0, W)] = (acc[pl.ds(h * W, W), :] / ORDER * mask[h].astype(F32)).astype(BF16)
+        half = pl.ds(h * W, W)
+        sq[r, h, pl.ds(0, W)] = (acc[half, :] / ORDER * mask[h].astype(F32)).astype(BF16)
+        acc[half, :] = jnp.zeros((W, WP), F32)
 
     near = lax.div(x, 2)
 
-    def second(yhp, pair, fresh=False):
-        for h in range(2):
-            multiply((2 * h + yhp) * 2 + pair, sq, None, fresh and h == 0)
+    def second(yhp, pair):
+        def add(h, carry):
+            multiply((2 * h + yhp) * 2 + pair, sq, None)
+            return carry
+
+        lax.fori_loop(0, 2, add, 0)
 
     follow(SECOND_GATHER, own_square, {
-        NEAR_OWN: lambda: second(yh, near, True),
+        NEAR_OWN: lambda: second(yh, near),
         FAR_OWN: lambda: second(yh, 1 - near),
         NEAR_OTHER: lambda: second(1 - yh, near),
         FAR_OTHER: lambda: second(1 - yh, 1 - near),
@@ -304,106 +309,90 @@
 
     fill(update, rank_at, tail_at, place, hot, hot_tail, blocks, outgoing, tails)
 
-    def partner(i, sign):
+    def partner(i):
         dcore, dz = lax.rem(i, 2), lax.rem(lax.div(i, 2), 4)
         dyl, dyh, dx = lax.rem(lax.div(i, 8), 2), lax.rem(lax.div(i, 16), 2), lax.div(i, 32)
-        to_row = lax.rem(yh + dyh, 2) * 4 + lax.rem(x + sign * dx + 4, 4)
-        to_col = lax.rem(z + sign * dz + 4, 4) * 4 + lax.rem(yl + dyl, 2) * 2 + lax.rem(core + dcore, 2)
+        to_row = lax.rem(yh + dyh, 2) * 4 + lax.rem(x + dx, 4)
+        to_col = lax.rem(z + dz, 4) * 4 + lax.rem(yl + dyl, 2) * 2 + lax.rem(core + dcore, 2)
         return to_row, to_col
 
     def rows_of(buf, device):
         return buf.at[pl.ds(pl.multiple_of(device * ROWS, ROWS), ROWS)]
 
     def message(i):
-        to_row, to_col = partner(i, 1)
+        to_row, to_col = partner(i)
         return pltpu.make_async_remote_copy(
             src_ref=rows_of(outgoing, to_row * NCOL + to_col), dst_ref=rows_of(arrived, me),
-            send_sem=exchange_send.at[i], recv_sem=exchange_recv.at[i],
-            device_id=(to_row, to_col), device_id_type=MESH)
-
-    def arrival(i):
-        from_row, from_col = partner(i, -1)
-        here = rows_of(arrived, from_row * NCOL + from_col)
-        return pltpu.make_async_remote_copy(
-            src_ref=here, dst_ref=here, send_sem=exchange_send.at[i], recv_sem=exchange_recv.at[i],
-            device_id=(from_row, from_col), device_id_type=MESH)
+            send_sem=exchange_send, recv_sem=exchange_recv, device_id=(to_row, to_col), device_id_type=MESH)
 
     def start_message(i, carry):
         message(lax.rem(i * 37, DEVICES)).start()
         return carry
 
-    def finish_message(i, carry):
-        arrival(lax.rem(i * 37, DEVICES)).wait_recv()
-        return carry
-
-    def message_sent(i, carry):
-        message(i).wait_send()
-        return carry
-
     line, in_line = r * 2 + yl, z * 2 + core
 
     def other_line(i):
         dyl, dyh, dx = i % 2, i // 2 % 2, i // 4
         return row(dx, dyh), yl if dyl == 0 else 1 - yl
 
-    def line_copy(i, to_line, here_line, device):
+    def line_copy(to, here, device):
         return pltpu.make_async_remote_copy(
-            src_ref=rows_of(tails, to_line), dst_ref=rows_of(relay_in, here_line),
-            send_sem=tail_send.at[i], recv_sem=tail_recv.at[i], device_id=device, device_id_type=MESH)
-
-    def pass_on(i, to, here, device):
+            src_ref=to, dst_ref=here, send_sem=tail_send.at[0], recv_sem=tail_recv.at[0],
+            device_id=device, device_id_type=MESH)
+
+    def pass_on(to, here, device):
         return pltpu.make_async_remote_copy(
-            src_ref=rows_of(relay_out, to), dst_ref=rows_of(tails_arrived, here),
-            send_sem=tail_send.at[i], recv_sem=tail_recv.at[i], device_id=device, device_id_type=MESH)
-
-    tail_ops = []
-    tail_waits = []
+            src_ref=to, dst_ref=here, send_sem=tail_send.at[1], recv_sem=tail_recv.at[1],
+            device_id=device, device_id_type=MESH)
+
     for i in range(1, 2 * NROW):
         to_row, to_yl = other_line(i)
-        device = (to_row, z * 4 + to_yl * 2 + core)
-        op = line_copy(i, to_row * 2 + to_yl, line, device)
-        op.start()
-        tail_ops.append(op)
-        from_row = row(-(i // 4), i // 2 % 2)
-        tail_waits.append(line_copy(i, line, from_row * 2 + to_yl, device))
+        line_copy(rows_of(tails, to_row * 2 + to_yl), rows_of(relay_in, line),
+                  (to_row, z * 4 + to_yl * 2 + core)).start()
+    all_lines = line_copy(tails.at[pl.ds(0, (2 * NROW - 1) * ROWS)], relay_in.at[pl.ds(0, (2 * NROW - 1) * ROWS)],
+                          ways[CORE])
     keep_line = pltpu.make_async_copy(rows_of(tails, line), rows_of(relay_in, line), local.at[5])
     keep_line.start()
     own = pltpu.make_async_copy(rows_of(outgoing, me), rows_of(arrived, me), local.at[4])
     own.start()
     lax.fori_loop(1, DEVICES // 2, start_message, 0)
     keep_line.wait()
-    for op in tail_waits:
-        op.wait_recv()
+    all_lines.wait_recv()
     relay_wide[...] = relay_in[...].astype(F32)
     for j in range(2 * 4):
         for k in range(2):
             part = relay_wide[pl.ds(2 * j + k, 2 * NROW, stride=ROWS), :]
             relay_out[pl.ds(j * ROWS, ROWS), pl.ds(128 * k, 128)] = part.astype(BF16)
-    pass_waits = []
     for i in range(1, 2 * 4):
         to_core = core if i % 2 == 0 else 1 - core
-        to_z, from_z = lax.rem(z + i // 2, 4), lax.rem(z + 4 - i // 2, 4)
-        device = (r, to_z * 4 + yl * 2 + to_core)
-        op = pass_on(2 * NROW + i, to_z * 2 + to_core, in_line, device)
-        op.start()
-        tail_ops.append(op)
-        pass_waits.append(pass_on(2 * NROW + i, in_line, from_z * 2 + to_core, device))
+        to_z = lax.rem(z + i // 2, 4)
+        pass_on(rows_of(relay_out, to_z * 2 + to_core), rows_of(tails_arrived, in_line),
+                (r, to_z * 4 + yl * 2 + to_core)).start()
+    all_passed = pass_on(relay_out.at[pl.ds(0, 7 * ROWS)], tails_arrived.at[pl.ds(0, 7 * ROWS)], ways[CORE])
     keep_tails = pltpu.make_async_copy(rows_of(relay_out, in_line), rows_of(tails_arrived, in_line), local.at[6])
     keep_tails.start()
     lax.fori_loop(DEVICES // 2, DEVICES, start_message, 0)
-    for op in started:
-        op.wait_send()
+    for group, kinds in enumerate(((LEFT, SIBLING), (RIGHT, SQUARE))):
+        sent = left.at[pl.ds(0, sum(kind in kinds for kind in started) // len(QUARTERS))]
+        pltpu.make_async_remote_copy(
+            src_ref=sent, dst_ref=sent, send_sem=send.at[group], recv_sem=recv.at[0],
+            device_id=ways[CORE], device_id_type=MESH).wait_send()
     own.wait()
     keep_tails.wait()
-    lax.fori_loop(1, DEVICES, finish_message, 0)
-    for op in pass_waits:
-        op.wait_recv()
-    lax.fori_loop(1, DEVICES, message_sent, 0)
-    for op in tail_ops:
-        op.wait_send()
+    all_lines.wait_send()
+    all_passed.wait_send()
+    most = pl.ds(0, (DEVICES - 1) * ROWS)
+    others = pltpu.make_async_remote_copy(
+        src_ref=outgoing.at[most], dst_ref=arrived.at[most],
+        send_sem=exchange_send, recv_sem=exchange_recv, device_id=ways[CORE], device_id_type=MESH)
+    others.wait_send()
+    others.wait_recv()
+    all_passed.wait_recv()
 
 
 N_BLOCKS = 2 * PB * PB
+
+
 WINDOWS = [
     (w, i) for w in range(3) for i in range(BS) if i * BS + BS > w * 256 and i * BS < w * 256 + 256
 ]
@@ -424,13 +413,15 @@
     at = lax.broadcasted_iota(jnp.int32, (WP, 256), 1)
     entry = lane - lax.div(lane, BS) * BS
     slot = lax.div(at, TAIL)
-    for k, (w, i) in enumerate(WINDOWS):
-        if w < 2:
-            place[k] = jnp.where(at - entry == i * BS - w * 256, 1.0, 0.0).astype(BF16)
-        else:
-            offset = at - slot * TAIL
-            fits = (slot < 6) & (offset - entry == i * BS - w * 256) & (offset < ENT - 512)
-            place[k] = jnp.where(fits, 1.0, 0.0).astype(BF16)
+    def spread(k, carry):
+        w = lax.div(k, 12)
+        place[k] = jnp.where(at - entry == (k - w) * BS - w * 256, 1.0, 0.0).astype(BF16)
+        return carry
+
+    lax.fori_loop(0, 24, spread, 0)
+    offset = at - slot * TAIL
+    fits = (slot < 6) & (offset - entry == (BS - 1) * BS - 512) & (offset < ENT - 512)
+    place[24] = jnp.where(fits, 1.0, 0.0).astype(BF16)
     rank, rank_col = ranks(owner[...])
     rank_at[...] = jnp.broadcast_to(rank_col, rank_at.shape)
     group = lax.div(lax.broadcasted_iota(jnp.int32, tail_at.shape, 1), TAIL)
@@ -442,11 +433,16 @@
     line = to_row * 2 + lax.rem(lax.div(to_col, 2), 2)
     in_line = lax.div(to_col, 4) * 2 + lax.rem(to_col, 2)
     tail_key = line * ROWS + in_line * 2 + lax.div(rank, 6)
-    step = 512
-    for k in range(0, DEVICES * ROWS, step):
-        at = lax.broadcasted_iota(jnp.int32, (step, N_BLOCKS), 0) + k
-        hot[pl.ds(k, step), pl.ds(0, N_BLOCKS)] = jnp.where(at == key, 1.0, 0.0).astype(BF16)
-        hot[pl.ds(k, step), pl.ds(N_BLOCKS, N_BLOCKS)] = jnp.where(at == last_key, 1.0, 0.0).astype(BF16)
+    step = 256
+
+    def compare(k, carry):
+        rows = pl.ds(pl.multiple_of(k * step, step), step)
+        at = lax.broadcasted_iota(jnp.int32, (step, N_BLOCKS), 0) + k * step
+        hot[rows, pl.ds(0, N_BLOCKS)] = jnp.where(at == key, 1.0, 0.0).astype(BF16)
+        hot[rows, pl.ds(N_BLOCKS, N_BLOCKS)] = jnp.where(at == last_key, 1.0, 0.0).astype(BF16)
+        return carry
+
+    lax.fori_loop(0, DEVICES * ROWS // step, compare, 0)
     at = lax.broadcasted_iota(jnp.int32, hot_tail.shape, 0)
     hot_tail[...] = jnp.where(at == tail_key, 1.0, 0.0).astype(BF16)
 
@@ -519,7 +515,7 @@
             pltpu.VMEM((2, W, WP), BF16),
             pltpu.VMEM((2 * W, WP), F32),
             pltpu.VMEM((2, WP // 128, W, 128), F32),
-            pltpu.VMEM((len(WINDOWS), WP, 256), BF16),
+            pltpu.VMEM((25, WP, 256), BF16),
             pltpu.VMEM((DEVICES * ROWS, 2 * N_BLOCKS), BF16),
             pltpu.VMEM((2 * NROW * ROWS, N_BLOCKS), BF16),
             pltpu.VMEM((N_BLOCKS, 128), jnp.int32),
@@ -530,12 +526,12 @@
             pltpu.VMEM((2 * NROW * ROWS, 128), BF16),
             pltpu.VMEM((2 * NROW * ROWS, 128), F32),
             pltpu.VMEM((DEVICES, 256), BF16),
+            pltpu.SemaphoreType.DMA((2,)),
             pltpu.SemaphoreType.DMA((N_COPIES,)),
-            pltpu.SemaphoreType.DMA((N_COPIES,)),
-            pltpu.SemaphoreType.DMA((DEVICES,)),
-            pltpu.SemaphoreType.DMA((DEVICES,)),
-            pltpu.SemaphoreType.DMA((2 * NROW + 8,)),
-            pltpu.SemaphoreType.DMA((2 * NROW + 8,)),
+            pltpu.SemaphoreType.DMA,
+            pltpu.SemaphoreType.DMA,
+            pltpu.SemaphoreType.DMA((2,)),
+            pltpu.SemaphoreType.DMA((2,)),
             pltpu.SemaphoreType.DMA((7,)),
         ],
         compiler_params=pltpu.CompilerParams(

time: 113 us -> 108 us (0.956)
  Pallas kernels: 112 us -> 108 us
    pallas_call x1, Pallas kernels: 109 us -> 105 us  [stepped(): pl.pallas_call(whole_step, out_shape=(jax.ShapeDtypeStruct((DEVICES * ROW...]
where the time goes in v5:
time: 108 us
  Pallas kernels  108 us (100%)
    pallas_call x1, Pallas kernels, stepped(): pl.pallas_call(whole_step, out_shape=(jax.ShapeDtypeStruct((DEVICES * ROW...  105 us
    pallas_call x1, Pallas kernels, unpacked(): pl.pallas_call(unpack, out_shape=jax.ShapeDtypeStruct((CAP, ENT, DEVICES)...  3.5 us

profile of v5, /device:TPU:1, one launch (start us, length us, event | category | flops | bytes accessed | tf_op | source)
XLA Modules:
  0.0 108.2 jit_solution(1960912399071979749)
XLA Ops:
  0.0 104.7 %whole_step.1 = (bf16[2048,384]{1,0:T(8,128)(2,1)}, bf16[128,256]{1,0:T(8,128)(2,1)}) custom-call(bf16[2,368,368]{2,1,0:T(8,128)(2,1)} %dens_in.1, s32[2,16,16]{2,1,0:T(8,128)} %pat_in.1, s32[2,16,16]{2,1,0:T(8,128)} %keep_in.1, s32[1,512]{1,0:T(1,128)} %bitcast.4), custom_call_target="tpu_custom_call" | custom-call | tf_op jit(solution)/shard_map/whole_step/pallas_call | solution.py:498
  104.7 3.5 %unpack.1 = bf16[12,529,128]{2,1,0:T(8,128)(2,1)} custom-call(bf16[2048,384]{1,0:T(8,128)(2,1)} %get-tuple-element.7.messages, bf16[128,256]{1,0:T(8,128)(2,1)} %get-tuple-element.8.tails), custom_call_target="tpu_custom_call" | custom-call | tf_op jit(solution)/shard_map/unpack/pallas_call | solution.py:582

commit v6 on v5

--- a/solution.py
+++ b/solution.py
@@ -23,100 +23,111 @@
 BF16 = jnp.bfloat16
 
 
-QUARTERS = ((0, 0, 192), (0, 192, W), (1, 0, 192), (1, 192, W))
+QUARTERS = ((0, 0, 240), (0, 240, W), (1, 0, 240), (1, 240, W))
 
 OWN, SEND, WAIT, DO = range(4)
 LEFT, SIBLING, RIGHT, SQUARE = range(4)
 CORE, YA, YB, YY, ZP, ZM, XP, XM = range(8)
-PREPARE, EARLY, NEAR_OWN, FAR_OWN, NEAR_OTHER, FAR_OTHER = range(6)
+PREPARE, FIRST_PAIRS, EARLY, LATE, NEAR_OWN, FAR_OWN, NEAR_OTHER, FAR_OTHER = range(8)
 FIRST_GATHER = (
-    (OWN, 0), (SEND, LEFT, 1, 0, 0, LEFT, 0, 0, ZM), (SEND, LEFT, -1, 0, 0, LEFT, 0, 0, ZP),
+    (OWN, 0), (SEND, LEFT, 0, 1, 0, LEFT, 0, 0, YA), (SEND, LEFT, -1, 0, 0, LEFT, 0, 0, ZP), (WAIT, SIBLING, 0, 0, 0),
+    (SEND, SIBLING, 0, 0, 0, LEFT, 0, 0, CORE), (SEND, LEFT, 1, 0, 1, LEFT, 0, 0, ZM),
+    (SEND, RIGHT, -1, 0, 1, RIGHT, 0, 0, XP), (WAIT, RIGHT, 1, 0, 0), (SEND, RIGHT, 1, 0, 0, RIGHT, 0, 0, XM),
     (SEND, RIGHT, -1, 0, 0, RIGHT, 0, 0, XP), (SEND, LEFT, -1, 0, 1, LEFT, 0, 0, ZP),
-    (SEND, RIGHT, 1, 0, 1, RIGHT, 0, 0, XM), (SEND, LEFT, 0, 1, 0, LEFT, 0, 0, YA),
-    (SEND, LEFT, 1, 0, 1, LEFT, 0, 0, ZM), (SEND, RIGHT, 1, 0, 0, RIGHT, 0, 0, XM),
-    (SEND, RIGHT, -1, 0, 1, RIGHT, 0, 0, XP), (SEND, LEFT, 0, 1, 1, LEFT, 0, 0, YA),
-    (SEND, SIBLING, 0, 0, 0, LEFT, 0, 0, CORE), (SEND, SIBLING, 0, 0, 1, LEFT, 0, 0, CORE), (OWN, 1),
-    (SEND, SIBLING, 0, 0, 2, LEFT, 0, 0, CORE), (SEND, SIBLING, 0, 0, 3, LEFT, 0, 0, CORE), (DO, PREPARE),
-    (SEND, RIGHT, -1, 0, 2, RIGHT, 0, 0, XP), (SEND, LEFT, 1, 0, 2, LEFT, 0, 0, ZM),
-    (SEND, RIGHT, 1, 0, 2, RIGHT, 0, 0, XM), (SEND, LEFT, 0, 1, 3, LEFT, 0, 0, YA),
-    (SEND, LEFT, -1, 0, 2, LEFT, 0, 0, ZP), (WAIT, SIBLING, 0, 0, 0), (WAIT, SIBLING, 0, 0, 1),
-    (WAIT, SIBLING, 0, 0, 2), (WAIT, SIBLING, 0, 0, 3), (WAIT, LEFT, 1, 0, 0),
-    (SEND, SIBLING, 1, 0, 0, LEFT, 1, 0, CORE), (WAIT, LEFT, -1, 0, 0), (SEND, SIBLING, -1, 0, 0, LEFT, -1, 0, CORE),
-    (SEND, LEFT, 2, 0, 0, LEFT, 1, 0, ZM), (WAIT, RIGHT, 1, 0, 1), (SEND, LEFT, 0, 1, 2, LEFT, 0, 0, YA),
-    (SEND, RIGHT, -1, 0, 3, RIGHT, 0, 0, XP), (SEND, RIGHT, 1, 0, 3, RIGHT, 0, 0, XM),
-    (SEND, LEFT, -1, 0, 3, LEFT, 0, 0, ZP), (WAIT, RIGHT, -1, 0, 0), (WAIT, LEFT, 0, 1, 0),
-    (SEND, RIGHT, 0, 1, 0, LEFT, 0, 1, YB), (SEND, SIBLING, 0, 1, 0, LEFT, 0, 1, CORE), (WAIT, SIBLING, 1, 0, 0),
-    (WAIT, SIBLING, -1, 0, 0), (WAIT, LEFT, 1, 0, 1), (SEND, SIBLING, 1, 0, 1, LEFT, 1, 0, CORE),
-    (WAIT, SIBLING, 0, 1, 0), (WAIT, LEFT, -1, 0, 1), (SEND, SIBLING, -1, 0, 1, LEFT, -1, 0, CORE),
-    (WAIT, RIGHT, -1, 0, 1), (SEND, LEFT, 2, 0, 1, LEFT, -1, 0, ZP), (SEND, LEFT, 1, 0, 3, LEFT, 0, 0, ZM),
-    (SEND, RIGHT, 2, 0, 1, RIGHT, 1, 0, XM), (WAIT, RIGHT, 1, 0, 0), (SEND, LEFT, 1, 1, 0, LEFT, 1, 0, YA),
-    (WAIT, LEFT, 0, 1, 1), (SEND, RIGHT, 0, 1, 1, LEFT, 0, 1, YB), (SEND, SIBLING, 0, 1, 1, LEFT, 0, 1, CORE),
-    (WAIT, SIBLING, 1, 0, 1), (WAIT, SIBLING, -1, 0, 1), (WAIT, SIBLING, 0, 1, 1), (WAIT, LEFT, 1, 0, 2),
-    (SEND, SIBLING, 1, 0, 2, LEFT, 1, 0, CORE), (SEND, LEFT, -1, 1, 1, LEFT, 0, 1, ZP),
-    (SEND, LEFT, 2, 0, 2, LEFT, 1, 0, ZM), (WAIT, LEFT, -1, 0, 2), (SEND, RIGHT, 2, 0, 0, RIGHT, 1, 0, XM),
-    (SEND, SIBLING, -1, 0, 2, LEFT, -1, 0, CORE), (WAIT, RIGHT, -1, 0, 2), (SEND, RIGHT, 2, 0, 2, RIGHT, -1, 0, XP),
-    (WAIT, LEFT, 0, 1, 3), (SEND, SIBLING, 0, 1, 3, LEFT, 0, 1, CORE), (SEND, LEFT, 1, 1, 1, LEFT, 1, 0, YA),
-    (SEND, RIGHT, 0, 1, 3, LEFT, 0, 1, YB), (WAIT, RIGHT, 1, 0, 2), (WAIT, RIGHT, 0, 1, 0),
-    (SEND, RIGHT, -1, 1, 0, RIGHT, 0, 1, XP), (WAIT, SIBLING, 1, 0, 2), (WAIT, SIBLING, -1, 0, 2),
-    (WAIT, SIBLING, 0, 1, 3), (WAIT, LEFT, -1, 0, 3), (SEND, LEFT, -1, 1, 3, LEFT, 0, 1, ZP),
-    (SEND, SIBLING, -1, 0, 3, LEFT, -1, 0, CORE), (WAIT, RIGHT, -1, 0, 3), (WAIT, LEFT, 2, 0, 0),
-    (SEND, LEFT, 1, 1, 3, LEFT, 0, 1, ZM), (SEND, SIBLING, 2, 0, 0, LEFT, 2, 0, CORE), (WAIT, RIGHT, 1, 0, 3),
-    (SEND, RIGHT, 1, 1, 0, RIGHT, 0, 1, XM), (SEND, LEFT, -1, 1, 0, LEFT, -1, 0, YA), (WAIT, RIGHT, 0, 1, 1),
-    (SEND, RIGHT, -1, 1, 1, RIGHT, 0, 1, XP), (WAIT, LEFT, 0, 1, 2), (SEND, RIGHT, 0, 1, 2, LEFT, 0, 1, YB),
-    (SEND, SIBLING, 0, 1, 2, LEFT, 0, 1, CORE), (WAIT, SIBLING, -1, 0, 3), (WAIT, SIBLING, 2, 0, 0),
-    (WAIT, LEFT, 2, 0, 1), (SEND, SIBLING, 2, 0, 1, LEFT, 2, 0, CORE), (SEND, LEFT, -1, 1, 2, LEFT, 0, 1, ZP),
-    (WAIT, SIBLING, 0, 1, 2), (WAIT, LEFT, 1, 0, 3), (SEND, LEFT, 2, 0, 3, LEFT, 1, 0, ZM),
-    (SEND, SIBLING, 1, 0, 3, LEFT, 1, 0, CORE), (WAIT, RIGHT, 2, 0, 1), (WAIT, RIGHT, 0, 1, 3),
-    (SEND, RIGHT, -1, 1, 3, RIGHT, 0, 1, XP), (SEND, RIGHT, 1, 1, 3, RIGHT, 0, 1, XM),
-    (SEND, RIGHT, 1, 1, 2, RIGHT, 1, 0, YY), (WAIT, RIGHT, 2, 0, 2), (WAIT, LEFT, 1, 1, 0),
-    (SEND, SIBLING, 1, 1, 0, LEFT, 1, 1, CORE), (WAIT, SIBLING, 2, 0, 1), (WAIT, SIBLING, 1, 0, 3),
-    (WAIT, SIBLING, 1, 1, 0), (WAIT, LEFT, -1, 1, 1), (SEND, SIBLING, -1, 1, 1, LEFT, -1, 1, CORE),
-    (WAIT, LEFT, 2, 0, 2), (SEND, SIBLING, 2, 0, 2, LEFT, 2, 0, CORE), (SEND, LEFT, 1, 1, 2, LEFT, 0, 1, ZM),
-    (WAIT, RIGHT, 2, 0, 0), (WAIT, RIGHT, -1, 1, 0), (SEND, RIGHT, 1, 1, 1, RIGHT, 0, 1, XM), (WAIT, LEFT, 1, 1, 1),
-    (SEND, SIBLING, 1, 1, 1, LEFT, 1, 1, CORE), (WAIT, RIGHT, 0, 1, 2), (SEND, RIGHT, -1, 1, 2, RIGHT, 0, 1, XP),
-    (SEND, LEFT, 2, 1, 2, LEFT, 2, 0, YA), (WAIT, SIBLING, -1, 1, 1), (WAIT, SIBLING, 2, 0, 2),
-    (WAIT, SIBLING, 1, 1, 1), (WAIT, LEFT, -1, 1, 3), (SEND, LEFT, 2, 1, 3, LEFT, -1, 1, ZP),
-    (SEND, SIBLING, -1, 1, 3, LEFT, -1, 1, CORE), (WAIT, LEFT, 1, 1, 3), (SEND, SIBLING, 1, 1, 3, LEFT, 1, 1, CORE),
-    (WAIT, RIGHT, -1, 1, 1), (SEND, LEFT, 2, 1, 1, LEFT, 1, 1, ZM), (WAIT, RIGHT, 1, 1, 0),
-    (SEND, RIGHT, 2, 0, 3, RIGHT, 1, 0, XM), (SEND, RIGHT, 2, 1, 1, RIGHT, -1, 1, XP), (WAIT, LEFT, -1, 1, 0),
-    (SEND, LEFT, 2, 1, 0, LEFT, -1, 1, ZP), (SEND, SIBLING, -1, 1, 0, LEFT, -1, 1, CORE), (WAIT, SIBLING, -1, 1, 3),
-    (SEND, RIGHT, 2, 1, 0, RIGHT, 2, 0, YY), (WAIT, SIBLING, 1, 1, 3), (WAIT, SIBLING, -1, 1, 0),
-    (WAIT, LEFT, -1, 1, 2), (SEND, SIBLING, -1, 1, 2, LEFT, -1, 1, CORE), (WAIT, LEFT, 2, 0, 3),
-    (SEND, SIBLING, 2, 0, 3, LEFT, 2, 0, CORE), (WAIT, RIGHT, -1, 1, 3), (WAIT, RIGHT, 1, 1, 3),
-    (SEND, RIGHT, 2, 1, 3, RIGHT, -1, 1, XP), (WAIT, SIBLING, -1, 1, 2), (WAIT, RIGHT, 1, 1, 2),
-    (SEND, RIGHT, 2, 1, 2, RIGHT, 1, 1, XM), (WAIT, SIBLING, 2, 0, 3), (WAIT, LEFT, 2, 1, 3),
-    (SEND, SIBLING, 2, 1, 3, LEFT, 2, 1, CORE), (WAIT, LEFT, 1, 1, 2), (SEND, SIBLING, 1, 1, 2, LEFT, 1, 1, CORE),
-    (WAIT, RIGHT, 1, 1, 1), (WAIT, RIGHT, -1, 1, 2), (WAIT, LEFT, 2, 1, 2),
-    (SEND, SIBLING, 2, 1, 2, LEFT, 2, 1, CORE), (WAIT, SIBLING, 2, 1, 3), (WAIT, SIBLING, 1, 1, 2),
-    (WAIT, SIBLING, 2, 1, 2), (WAIT, LEFT, 2, 1, 0), (SEND, SIBLING, 2, 1, 0, LEFT, 2, 1, CORE),
-    (WAIT, LEFT, 2, 1, 1), (SEND, SIBLING, 2, 1, 1, LEFT, 2, 1, CORE), (WAIT, RIGHT, 2, 0, 3), (DO, EARLY),
-    (WAIT, RIGHT, 2, 1, 1), (WAIT, SIBLING, 2, 1, 0), (WAIT, RIGHT, 2, 1, 0), (WAIT, SIBLING, 2, 1, 1),
-    (WAIT, RIGHT, 2, 1, 3), (WAIT, RIGHT, 2, 1, 2),
+    (SEND, LEFT, 1, 0, 0, LEFT, 0, 0, ZM), (WAIT, SIBLING, 0, 0, 1), (SEND, SIBLING, 0, 0, 1, LEFT, 0, 0, CORE),
+    (OWN, 1), (SEND, LEFT, 0, 1, 1, LEFT, 0, 0, YA), (WAIT, SIBLING, 0, 0, 2),
+    (SEND, SIBLING, 0, 0, 2, LEFT, 0, 0, CORE), (SEND, RIGHT, 1, 0, 3, RIGHT, 0, 0, XM), (WAIT, SIBLING, 0, 0, 3),
+    (SEND, SIBLING, 0, 0, 3, LEFT, 0, 0, CORE), (DO, PREPARE), (SEND, LEFT, -1, 0, 3, LEFT, 0, 0, ZP),
+    (SEND, LEFT, 0, 1, 2, LEFT, 0, 0, YA), (SEND, LEFT, 1, 0, 2, LEFT, 0, 0, ZM), (WAIT, RIGHT, 1, 0, 1),
+    (SEND, RIGHT, 1, 0, 1, RIGHT, 0, 0, XM), (SEND, RIGHT, -1, 0, 2, RIGHT, 0, 0, XP), (WAIT, LEFT, 1, 0, 1),
+    (WAIT, SIBLING, 1, 0, 1), (SEND, SIBLING, 1, 0, 1, LEFT, 1, 0, CORE), (SEND, LEFT, -1, 0, 2, LEFT, 0, 0, ZP),
+    (WAIT, RIGHT, -1, 0, 1), (WAIT, LEFT, 0, 1, 0), (SEND, RIGHT, 0, 1, 0, LEFT, 0, 1, YB), (WAIT, SIBLING, 0, 1, 0),
+    (SEND, SIBLING, 0, 1, 0, LEFT, 0, 1, CORE), (SEND, LEFT, 0, 1, 3, LEFT, 0, 0, YA), (WAIT, RIGHT, 1, 0, 2),
+    (SEND, RIGHT, 1, 0, 2, RIGHT, 0, 0, XM), (WAIT, LEFT, -1, 0, 0), (WAIT, SIBLING, -1, 0, 0),
+    (SEND, SIBLING, -1, 0, 0, LEFT, -1, 0, CORE), (SEND, LEFT, 1, 0, 3, LEFT, 0, 0, ZM), (WAIT, RIGHT, 2, 0, 1),
+    (SEND, RIGHT, 2, 0, 1, RIGHT, -1, 0, XP), (WAIT, LEFT, 0, 1, 1), (WAIT, SIBLING, 0, 1, 1),
+    (SEND, SIBLING, 0, 1, 1, LEFT, 0, 1, CORE), (SEND, RIGHT, 0, 1, 1, LEFT, 0, 1, YB), (WAIT, LEFT, -1, 0, 1),
+    (SEND, LEFT, -1, 1, 0, LEFT, -1, 0, YA), (WAIT, SIBLING, -1, 0, 1), (SEND, SIBLING, -1, 0, 1, LEFT, -1, 0, CORE),
+    (SEND, LEFT, 2, 0, 1, LEFT, -1, 0, ZP), (WAIT, LEFT, 1, 0, 0), (SEND, LEFT, 1, 1, 0, LEFT, 0, 1, ZM),
+    (WAIT, SIBLING, 1, 0, 0), (SEND, SIBLING, 1, 0, 0, LEFT, 1, 0, CORE), (SEND, RIGHT, -1, 0, 3, RIGHT, 0, 0, XP),
+    (WAIT, RIGHT, -1, 0, 0), (WAIT, RIGHT, 1, 0, 3), (WAIT, RIGHT, 2, 0, 3), (SEND, RIGHT, 2, 0, 3, RIGHT, 1, 0, XM),
+    (WAIT, LEFT, -1, 0, 3), (WAIT, SIBLING, -1, 0, 3), (SEND, SIBLING, -1, 0, 3, LEFT, -1, 0, CORE),
+    (WAIT, LEFT, 0, 1, 2), (SEND, LEFT, 2, 0, 0, LEFT, -1, 0, ZP), (WAIT, SIBLING, 0, 1, 2),
+    (SEND, SIBLING, 0, 1, 2, LEFT, 0, 1, CORE), (SEND, RIGHT, 0, 1, 2, LEFT, 0, 1, YB),
+    (SEND, LEFT, -1, 1, 3, LEFT, -1, 0, YA), (SEND, RIGHT, 2, 0, 0, RIGHT, -1, 0, XP), (WAIT, RIGHT, 0, 1, 0),
+    (SEND, LEFT, 1, 1, 2, LEFT, 0, 1, ZM), (WAIT, RIGHT, 1, 1, 0), (SEND, RIGHT, 1, 1, 0, RIGHT, 0, 1, XM),
+    (WAIT, LEFT, 1, 0, 2), (WAIT, SIBLING, 1, 0, 2), (SEND, SIBLING, 1, 0, 2, LEFT, 1, 0, CORE),
+    (WAIT, RIGHT, -1, 0, 2), (WAIT, LEFT, 0, 1, 3), (WAIT, SIBLING, 0, 1, 3),
+    (SEND, SIBLING, 0, 1, 3, LEFT, 0, 1, CORE), (SEND, RIGHT, 0, 1, 3, LEFT, 0, 1, YB), (WAIT, LEFT, -1, 0, 2),
+    (SEND, LEFT, 1, 1, 1, LEFT, 1, 0, YA), (WAIT, SIBLING, -1, 0, 2), (SEND, SIBLING, -1, 0, 2, LEFT, -1, 0, CORE),
+    (SEND, LEFT, 2, 0, 3, LEFT, -1, 0, ZP), (WAIT, RIGHT, 0, 1, 1), (WAIT, RIGHT, 2, 0, 2),
+    (SEND, RIGHT, 2, 0, 2, RIGHT, -1, 0, XP), (WAIT, LEFT, 1, 0, 3), (SEND, RIGHT, 1, 1, 1, RIGHT, 0, 1, XM),
+    (WAIT, SIBLING, 1, 0, 3), (SEND, SIBLING, 1, 0, 3, LEFT, 1, 0, CORE), (WAIT, LEFT, 2, 0, 1),
+    (WAIT, SIBLING, 2, 0, 1), (SEND, SIBLING, 2, 0, 1, LEFT, 2, 0, CORE), (WAIT, RIGHT, -1, 1, 1),
+    (SEND, RIGHT, -1, 1, 1, RIGHT, -1, 0, YY), (SEND, LEFT, 2, 0, 2, LEFT, 1, 0, ZM), (WAIT, RIGHT, -1, 0, 3),
+    (SEND, LEFT, -1, 1, 1, LEFT, 0, 1, ZP), (WAIT, LEFT, -1, 1, 0), (WAIT, SIBLING, -1, 1, 0),
+    (SEND, SIBLING, -1, 1, 0, LEFT, -1, 1, CORE), (WAIT, LEFT, 1, 1, 0), (WAIT, SIBLING, 1, 1, 0),
+    (SEND, SIBLING, 1, 1, 0, LEFT, 1, 1, CORE), (WAIT, RIGHT, 0, 1, 2), (SEND, RIGHT, -1, 1, 3, RIGHT, -1, 0, YY),
+    (SEND, LEFT, 2, 1, 0, LEFT, -1, 1, ZP), (SEND, RIGHT, 1, 1, 2, RIGHT, 0, 1, XM), (WAIT, LEFT, -1, 1, 3),
+    (WAIT, SIBLING, -1, 1, 3), (SEND, SIBLING, -1, 1, 3, LEFT, -1, 1, CORE), (WAIT, RIGHT, -1, 1, 2),
+    (SEND, RIGHT, -1, 1, 2, RIGHT, 0, 1, XP), (WAIT, LEFT, 2, 0, 0), (WAIT, SIBLING, 2, 0, 0),
+    (SEND, SIBLING, 2, 0, 0, LEFT, 2, 0, CORE), (SEND, LEFT, 1, 1, 3, LEFT, 0, 1, ZM),
+    (SEND, LEFT, -1, 1, 2, LEFT, -1, 0, YA), (WAIT, RIGHT, 2, 0, 0), (WAIT, RIGHT, 0, 1, 3), (WAIT, RIGHT, 1, 1, 3),
+    (SEND, RIGHT, 1, 1, 3, RIGHT, 0, 1, XM), (WAIT, LEFT, 1, 1, 1), (WAIT, SIBLING, 1, 1, 1),
+    (SEND, SIBLING, 1, 1, 1, LEFT, 1, 1, CORE), (WAIT, LEFT, 1, 1, 2), (WAIT, SIBLING, 1, 1, 2),
+    (SEND, SIBLING, 1, 1, 2, LEFT, 1, 1, CORE), (WAIT, LEFT, 2, 0, 3), (SEND, LEFT, 2, 1, 2, LEFT, 1, 1, ZM),
+    (SEND, LEFT, 2, 1, 3, LEFT, -1, 1, ZP), (WAIT, RIGHT, -1, 1, 0), (SEND, RIGHT, -1, 1, 0, RIGHT, 0, 1, XP),
+    (WAIT, SIBLING, 2, 0, 3), (SEND, SIBLING, 2, 0, 3, LEFT, 2, 0, CORE), (WAIT, RIGHT, 1, 1, 1),
+    (WAIT, RIGHT, 2, 1, 1), (SEND, RIGHT, 2, 1, 1, RIGHT, 1, 1, XM), (WAIT, LEFT, -1, 1, 1),
+    (WAIT, SIBLING, -1, 1, 1), (SEND, SIBLING, -1, 1, 1, LEFT, -1, 1, CORE), (WAIT, RIGHT, 2, 1, 0),
+    (SEND, RIGHT, 2, 1, 0, RIGHT, 2, 0, YY), (SEND, LEFT, 2, 1, 1, LEFT, -1, 1, ZP), (WAIT, LEFT, 2, 0, 2),
+    (WAIT, SIBLING, 2, 0, 2), (SEND, SIBLING, 2, 0, 2, LEFT, 2, 0, CORE), (WAIT, RIGHT, 1, 1, 2),
+    (WAIT, RIGHT, 2, 1, 2), (SEND, RIGHT, 2, 1, 2, RIGHT, 1, 1, XM), (WAIT, RIGHT, -1, 1, 3), (WAIT, RIGHT, 2, 1, 3),
+    (SEND, RIGHT, 2, 1, 3, RIGHT, -1, 1, XP), (DO, FIRST_PAIRS), (WAIT, LEFT, 1, 1, 3), (WAIT, SIBLING, 1, 1, 3),
+    (SEND, SIBLING, 1, 1, 3, LEFT, 1, 1, CORE), (WAIT, LEFT, 2, 1, 0), (WAIT, SIBLING, 2, 1, 0),
+    (SEND, SIBLING, 2, 1, 0, LEFT, 2, 1, CORE), (WAIT, LEFT, -1, 1, 2), (WAIT, SIBLING, -1, 1, 2),
+    (SEND, SIBLING, -1, 1, 2, LEFT, -1, 1, CORE), (WAIT, LEFT, 2, 1, 3), (WAIT, SIBLING, 2, 1, 3),
+    (SEND, SIBLING, 2, 1, 3, LEFT, 2, 1, CORE), (WAIT, LEFT, 2, 1, 2), (WAIT, SIBLING, 2, 1, 2),
+    (SEND, SIBLING, 2, 1, 2, LEFT, 2, 1, CORE), (WAIT, LEFT, 2, 1, 1), (WAIT, SIBLING, 2, 1, 1),
+    (SEND, SIBLING, 2, 1, 1, LEFT, 2, 1, CORE), (DO, EARLY),
 )
 
 SECOND_GATHER = (
-    (OWN, 0), (SEND, SQUARE, 1, 0, 0, SQUARE, 0, 0, XM), (SEND, SQUARE, -1, 0, 1, SQUARE, 0, 0, XP),
-    (SEND, SQUARE, -1, 0, 0, SQUARE, 0, 0, XP), (SEND, SQUARE, 0, 1, 1, SQUARE, 0, 0, YY),
-    (SEND, SQUARE, 0, 1, 0, SQUARE, 0, 0, YY), (SEND, SQUARE, 1, 0, 1, SQUARE, 0, 0, XM), (OWN, 1),
-    (WAIT, SQUARE, -1, 0, 1), (SEND, SQUARE, -1, 0, 3, SQUARE, 0, 0, XP), (SEND, SQUARE, 0, 1, 2, SQUARE, 0, 0, YY),
-    (SEND, SQUARE, -1, 0, 2, SQUARE, 0, 0, XP), (SEND, SQUARE, 1, 0, 2, SQUARE, 0, 0, XM),
-    (SEND, SQUARE, 1, 0, 3, SQUARE, 0, 0, XM), (WAIT, SQUARE, 1, 0, 0), (WAIT, SQUARE, 0, 1, 1),
-    (SEND, SQUARE, 1, 1, 0, SQUARE, 1, 0, YY), (WAIT, SQUARE, 1, 0, 1), (WAIT, SQUARE, -1, 0, 0),
-    (WAIT, SQUARE, 0, 1, 0), (SEND, SQUARE, 2, 0, 0, SQUARE, -1, 0, XP), (SEND, SQUARE, 2, 0, 1, SQUARE, 1, 0, XM),
-    (SEND, SQUARE, 0, 1, 3, SQUARE, 0, 0, YY), (WAIT, SQUARE, -1, 0, 3), (WAIT, SQUARE, 1, 0, 2),
-    (SEND, SQUARE, 1, 1, 1, SQUARE, 0, 1, XM), (WAIT, SQUARE, 0, 1, 2), (SEND, SQUARE, -1, 1, 0, SQUARE, 0, 1, XP),
-    (SEND, SQUARE, 1, 1, 2, SQUARE, 1, 0, YY), (WAIT, SQUARE, 1, 0, 3), (SEND, SQUARE, 2, 0, 3, SQUARE, 1, 0, XM),
-    (WAIT, SQUARE, -1, 0, 2), (DO, NEAR_OWN), (SEND, SQUARE, 2, 0, 2, SQUARE, -1, 0, XP),
-    (SEND, SQUARE, -1, 1, 2, SQUARE, -1, 0, YY), (WAIT, SQUARE, 1, 1, 0), (WAIT, SQUARE, 2, 0, 1),
-    (WAIT, SQUARE, 2, 0, 0), (WAIT, SQUARE, 0, 1, 3), (SEND, SQUARE, 2, 1, 0, SQUARE, 2, 0, YY),
-    (SEND, SQUARE, 1, 1, 3, SQUARE, 0, 1, XM), (SEND, SQUARE, -1, 1, 3, SQUARE, 0, 1, XP), (WAIT, SQUARE, 1, 1, 1),
-    (SEND, SQUARE, 2, 1, 1, SQUARE, 1, 1, XM), (WAIT, SQUARE, -1, 1, 0), (WAIT, SQUARE, 1, 1, 2),
-    (SEND, SQUARE, -1, 1, 1, SQUARE, 0, 1, XP), (WAIT, SQUARE, 2, 0, 3), (WAIT, SQUARE, 2, 0, 2),
-    (SEND, SQUARE, 2, 1, 2, SQUARE, 2, 0, YY), (DO, FAR_OWN), (WAIT, SQUARE, -1, 1, 2), (WAIT, SQUARE, 1, 1, 3),
-    (SEND, SQUARE, 2, 1, 3, SQUARE, 1, 1, XM), (WAIT, SQUARE, -1, 1, 3), (WAIT, SQUARE, 2, 1, 0),
-    (WAIT, SQUARE, 2, 1, 1), (WAIT, SQUARE, -1, 1, 1), (DO, NEAR_OTHER), (WAIT, SQUARE, 2, 1, 2),
-    (WAIT, SQUARE, 2, 1, 3), (DO, FAR_OTHER),
+    (OWN, 0), (SEND, SQUARE, 0, 1, 1, SQUARE, 0, 0, YY), (WAIT, SQUARE, 1, 0, 0),
+    (SEND, SQUARE, 1, 0, 0, SQUARE, 0, 0, XM), (SEND, SQUARE, 0, 1, 0, SQUARE, 0, 0, YY),
+    (SEND, SQUARE, -1, 0, 1, SQUARE, 0, 0, XP), (SEND, SQUARE, -1, 0, 0, SQUARE, 0, 0, XP), (OWN, 1),
+    (SEND, SQUARE, 1, 0, 3, SQUARE, 0, 0, XM), (WAIT, SQUARE, -1, 0, 1), (SEND, SQUARE, 0, 1, 3, SQUARE, 0, 0, YY),
+    (WAIT, SQUARE, -1, 0, 3), (SEND, SQUARE, -1, 0, 3, SQUARE, 0, 0, XP), (WAIT, SQUARE, 2, 0, 1),
+    (SEND, SQUARE, 2, 0, 1, SQUARE, -1, 0, XP), (WAIT, SQUARE, 1, 0, 1), (SEND, SQUARE, 1, 0, 1, SQUARE, 0, 0, XM),
+    (SEND, SQUARE, 1, 0, 2, SQUARE, 0, 0, XM), (WAIT, SQUARE, 0, 1, 2), (SEND, SQUARE, 0, 1, 2, SQUARE, 0, 0, YY),
+    (WAIT, SQUARE, 0, 1, 1), (WAIT, SQUARE, 1, 0, 3), (SEND, SQUARE, -1, 0, 2, SQUARE, 0, 0, XP),
+    (WAIT, SQUARE, -1, 0, 0), (SEND, SQUARE, -1, 1, 0, SQUARE, -1, 0, YY), (WAIT, SQUARE, 1, 1, 1),
+    (SEND, SQUARE, 1, 1, 1, SQUARE, 0, 1, XM), (WAIT, SQUARE, 0, 1, 0), (WAIT, SQUARE, 0, 1, 3),
+    (WAIT, SQUARE, -1, 1, 3), (SEND, SQUARE, -1, 1, 3, SQUARE, 0, 1, XP), (WAIT, SQUARE, 2, 0, 3),
+    (SEND, SQUARE, 2, 0, 3, SQUARE, 1, 0, XM), (WAIT, SQUARE, 1, 0, 2), (SEND, SQUARE, 2, 0, 2, SQUARE, 1, 0, XM),
+    (WAIT, SQUARE, 1, 1, 2), (SEND, SQUARE, 1, 1, 2, SQUARE, 1, 0, YY), (SEND, SQUARE, -1, 1, 1, SQUARE, 0, 1, XP),
+    (WAIT, SQUARE, -1, 0, 2), (SEND, SQUARE, 1, 1, 3, SQUARE, 0, 1, XM), (WAIT, SQUARE, -1, 1, 2),
+    (SEND, SQUARE, -1, 1, 2, SQUARE, -1, 0, YY), (WAIT, SQUARE, 2, 0, 0), (SEND, SQUARE, 2, 0, 0, SQUARE, -1, 0, XP),
+    (DO, NEAR_OWN), (WAIT, SQUARE, -1, 1, 0), (WAIT, SQUARE, 2, 1, 0), (SEND, SQUARE, 2, 1, 0, SQUARE, -1, 1, XP),
+    (WAIT, SQUARE, 1, 1, 0), (SEND, SQUARE, 1, 1, 0, SQUARE, 0, 1, XM), (WAIT, SQUARE, -1, 1, 1),
+    (WAIT, SQUARE, 2, 0, 2), (WAIT, SQUARE, 2, 1, 2), (SEND, SQUARE, 2, 1, 2, SQUARE, 2, 0, YY),
+    (WAIT, SQUARE, 1, 1, 3), (WAIT, SQUARE, 2, 1, 3), (SEND, SQUARE, 2, 1, 3, SQUARE, 1, 1, XM),
+    (WAIT, SQUARE, 2, 1, 1), (SEND, SQUARE, 2, 1, 1, SQUARE, -1, 1, XP), (DO, FAR_OWN), (DO, NEAR_OTHER),
+    (DO, FAR_OTHER),
 )
+
+
+FORWARDED = {(*op[5:8], op[4]) for op in FIRST_GATHER + SECOND_GATHER if op[0] == SEND}
+GROUPS = 11
+
+
+def group_of(kind, d, f, q):
+    if (kind, d, f, q) in FORWARDED:
+        return None
+    if kind == SQUARE:
+        return (NEAR_OTHER if d < 2 else FAR_OTHER) if f else (NEAR_OWN if d < 2 else FAR_OWN)
+    work = LATE if (d, f) == (2, 1) else EARLY if f and (d or kind == RIGHT) else FIRST_PAIRS
+    return 7 + work if kind == SIBLING else work
 
 
 def grow_columns(mask):
@@ -177,6 +188,7 @@
 
     started = []
     arriving = {}
+    expected = [0] * GROUPS
 
     def piece(buf, slot, q):
         h, first, end = QUARTERS[q]
@@ -190,7 +202,12 @@
         return piece(right if kind == RIGHT else sq, row(d, f), q)
 
     def start(kind, d, f, q, from_kind, from_d, from_f, way):
-        k = len(started)
+        k = group_of(kind, d, f, q)
+        if k is None:
+            k = GROUPS + len(arriving)
+        else:
+            _, first, end = QUARTERS[q]
+            expected[k] += end - first
         group = 0 if kind in (LEFT, SIBLING) else 1
         if kind == RIGHT:
             src = piece(left, c, q) if (from_d, from_f) == (0, 0) else find(from_kind, from_d, from_f, q)
@@ -202,10 +219,21 @@
             device_id=ways[way], device_id_type=MESH)
         op.start()
         started.append(kind)
+        if k < GROUPS:
+            return
         here = find(kind, d, f, q)
         arriving[kind, d, f, q] = pltpu.make_async_remote_copy(
             src_ref=here, dst_ref=here, send_sem=send.at[group], recv_sem=recv.at[k],
             device_id=ways[way], device_id_type=MESH)
+
+    def join(group):
+        rows = expected[group]
+        if rows == 0:
+            return
+        all_rows = left.at[pl.ds(0, rows // (2 * W))] if rows % (2 * W) == 0 else outgoing.at[pl.ds(0, rows)]
+        pltpu.make_async_remote_copy(
+            src_ref=all_rows, dst_ref=all_rows, send_sem=send.at[0], recv_sem=recv.at[group],
+            device_id=ways[CORE], device_id_type=MESH).wait_recv()
 
     def follow(table, own, work):
         for op, *what in table:
@@ -214,8 +242,10 @@
             elif op == SEND:
                 start(*what)
             elif op == WAIT:
-                arriving[tuple(what)].wait_recv()
+                if group_of(*what) is None:
+                    arriving[tuple(what)].wait_recv()
             else:
+                join(what[0])
                 work[what[0]]()
 
     def multiply(p, buf, h):
@@ -260,20 +290,33 @@
             kept[h] = grow(keep[h]).astype(BF16)
         routing_tables(owner, place, hot, hot_tail, rank_at, tail_at)
 
-    def early():
+    def is_first(p):
+        zp, yp = lax.div(p, 2), lax.rem(p, 2)
+        return (lax.rem(zp, 2) == yh) & ((yp == yl) | (zp == z)) & jnp.logical_not(is_late(p))
+
+    def pairs(chosen, group):
         def add(p, carry):
-            @pl.when(jnp.logical_not(is_late(p)))
+            @pl.when(chosen(p))
             def _():
                 multiply(p, right, None)
             return carry
 
+        join(7 + group)
         lax.fori_loop(0, NCOL // 2, add, 0)
 
     fetches[0].wait()
     fetches[1].wait()
-    follow(FIRST_GATHER, own_density, {PREPARE: prepare, EARLY: early})
+    follow(FIRST_GATHER, own_density, {
+        PREPARE: prepare,
+        FIRST_PAIRS: lambda: pairs(is_first, FIRST_PAIRS),
+        EARLY: lambda: pairs(lambda p: jnp.logical_not(is_first(p) | is_late(p)), EARLY),
+    })
 
     def own_square(h):
+        if h == 0:
+            join(LATE)
+            join(7 + LATE)
+
         def add(p, carry):
             @pl.when(is_late(p))
             def _():
@@ -307,27 +350,24 @@
         for k in range(WP // 128):
             update[h, k] = new[:, k * 128 : k * 128 + 128]
 
-    fill(update, rank_at, tail_at, place, hot, hot_tail, blocks, outgoing, tails)
-
-    def partner(i):
-        dcore, dz = lax.rem(i, 2), lax.rem(lax.div(i, 2), 4)
-        dyl, dyh, dx = lax.rem(lax.div(i, 8), 2), lax.rem(lax.div(i, 16), 2), lax.div(i, 32)
-        to_row = lax.rem(yh + dyh, 2) * 4 + lax.rem(x + dx, 4)
-        to_col = lax.rem(z + dz, 4) * 4 + lax.rem(yl + dyl, 2) * 2 + lax.rem(core + dcore, 2)
-        return to_row, to_col
-
     def rows_of(buf, device):
         return buf.at[pl.ds(pl.multiple_of(device * ROWS, ROWS), ROWS)]
 
-    def message(i):
-        to_row, to_col = partner(i)
-        return pltpu.make_async_remote_copy(
-            src_ref=rows_of(outgoing, to_row * NCOL + to_col), dst_ref=rows_of(arrived, me),
-            send_sem=exchange_send, recv_sem=exchange_recv, device_id=(to_row, to_col), device_id_type=MESH)
-
-    def start_message(i, carry):
-        message(lax.rem(i * 37, DEVICES)).start()
-        return carry
+    def messages(yhp, xp, first):
+        at = pl.ds(pl.multiple_of((yhp * 2 + xp) * 512, 512), 512)
+        outgoing[at, :] = jnp.dot(hot[at, :], blocks[...], preferred_element_type=F32).astype(BF16)
+
+        def start_message(i, carry):
+            i = lax.rem(i * 13, 32)
+            dz, dyl, dcore, dx = lax.div(i, 8), lax.rem(lax.div(i, 4), 2), lax.rem(lax.div(i, 2), 2), lax.rem(i, 2)
+            to_row = yhp * 4 + xp * 2 + lax.rem(x + dx, 2)
+            to_col = lax.rem(z + dz, 4) * 4 + lax.rem(yl + dyl, 2) * 2 + lax.rem(core + dcore, 2)
+            pltpu.make_async_remote_copy(
+                src_ref=rows_of(outgoing, to_row * NCOL + to_col), dst_ref=rows_of(arrived, me),
+                send_sem=exchange_send, recv_sem=exchange_recv, device_id=(to_row, to_col), device_id_type=MESH).start()
+            return carry
+
+        lax.fori_loop(first, 32, start_message, 0)
 
     line, in_line = r * 2 + yl, z * 2 + core
 
@@ -345,17 +385,21 @@
             src_ref=to, dst_ref=here, send_sem=tail_send.at[1], recv_sem=tail_recv.at[1],
             device_id=device, device_id_type=MESH)
 
-    for i in range(1, 2 * NROW):
-        to_row, to_yl = other_line(i)
-        line_copy(rows_of(tails, to_row * 2 + to_yl), rows_of(relay_in, line),
-                  (to_row, z * 4 + to_yl * 2 + core)).start()
     all_lines = line_copy(tails.at[pl.ds(0, (2 * NROW - 1) * ROWS)], relay_in.at[pl.ds(0, (2 * NROW - 1) * ROWS)],
                           ways[CORE])
     keep_line = pltpu.make_async_copy(rows_of(tails, line), rows_of(relay_in, line), local.at[5])
-    keep_line.start()
-    own = pltpu.make_async_copy(rows_of(outgoing, me), rows_of(arrived, me), local.at[4])
-    own.start()
-    lax.fori_loop(1, DEVICES // 2, start_message, 0)
+
+    def send_tails():
+        for i in range(1, 2 * NROW):
+            to_row, to_yl = other_line(i)
+            line_copy(rows_of(tails, to_row * 2 + to_yl), rows_of(relay_in, line),
+                      (to_row, z * 4 + to_yl * 2 + core)).start()
+        keep_line.start()
+
+    fill(update, rank_at, tail_at, place, hot_tail, blocks, tails, send_tails)
+
+    messages(1 - yh, 1 - near, 0)
+    messages(yh, 1 - near, 0)
     keep_line.wait()
     all_lines.wait_recv()
     relay_wide[...] = relay_in[...].astype(F32)
@@ -371,11 +415,14 @@
     all_passed = pass_on(relay_out.at[pl.ds(0, 7 * ROWS)], tails_arrived.at[pl.ds(0, 7 * ROWS)], ways[CORE])
     keep_tails = pltpu.make_async_copy(rows_of(relay_out, in_line), rows_of(tails_arrived, in_line), local.at[6])
     keep_tails.start()
-    lax.fori_loop(DEVICES // 2, DEVICES, start_message, 0)
+    messages(1 - yh, near, 0)
+    messages(yh, near, 1)
+    own = pltpu.make_async_copy(rows_of(outgoing, me), rows_of(arrived, me), local.at[4])
+    own.start()
     for group, kinds in enumerate(((LEFT, SIBLING), (RIGHT, SQUARE))):
         sent = left.at[pl.ds(0, sum(kind in kinds for kind in started) // len(QUARTERS))]
         pltpu.make_async_remote_copy(
-            src_ref=sent, dst_ref=sent, send_sem=send.at[group], recv_sem=recv.at[0],
+            src_ref=sent, dst_ref=sent, send_sem=send.at[group], recv_sem=recv.at[group],
             device_id=ways[CORE], device_id_type=MESH).wait_send()
     own.wait()
     keep_tails.wait()
@@ -447,7 +494,7 @@
     hot_tail[...] = jnp.where(at == tail_key, 1.0, 0.0).astype(BF16)
 
 
-def fill(update, rank_at, tail_at, place, hot, hot_tail, blocks, outgoing, tails):
+def fill(update, rank_at, tail_at, place, hot_tail, blocks, tails, send_tails):
     n = N_BLOCKS
     half = PB // 2
     picks = []
@@ -475,6 +522,7 @@
         if w == 2:
             tail = (both[:, :128] * tail_at[...]).astype(BF16)
             tails[...] = jnp.dot(hot_tail[...], tail, preferred_element_type=F32).astype(BF16)
+            send_tails()
         elif w == 0:
             blocks[pl.ds(0, n), pl.ds(0, 256)] = both.astype(BF16)
         else:
@@ -483,13 +531,10 @@
             for j in range(3):
                 mine = (rank >= 4 * j) & (rank < 4 * j + 4)
                 blocks[pl.ds(n, n), pl.ds(128 * j, 128)] = jnp.where(mine, both[:, 128:], 0.0).astype(BF16)
-    step = 512
-    for k in range(0, DEVICES * ROWS, step):
-        outgoing[pl.ds(k, step), :] = jnp.dot(
-            hot[pl.ds(k, step), :], blocks[...], preferred_element_type=F32).astype(BF16)
-
-
-N_COPIES = sum(op[0] == SEND for op in FIRST_GATHER + SECOND_GATHER)
+
+
+N_ARRIVALS = GROUPS + sum(
+    op[0] == SEND and group_of(*op[1:5]) is None for op in FIRST_GATHER + SECOND_GATHER)
 
 
 def stepped(density, pattern, keep, owner):
@@ -527,7 +572,7 @@
             pltpu.VMEM((2 * NROW * ROWS, 128), F32),
             pltpu.VMEM((DEVICES, 256), BF16),
             pltpu.SemaphoreType.DMA((2,)),
-            pltpu.SemaphoreType.DMA((N_COPIES,)),
+            pltpu.SemaphoreType.DMA((N_ARRIVALS,)),
             pltpu.SemaphoreType.DMA,
             pltpu.SemaphoreType.DMA,
             pltpu.SemaphoreType.DMA((2,)),

time: 108 us -> 107 us (level)
  Pallas kernels: 108 us -> 106 us
    pallas_call x1, Pallas kernels: 105 us -> 103 us  [stepped(): pl.pallas_call(whole_step, out_shape=(jax.ShapeDtypeStruct((DEVICES * ROW...]
where the time goes in v6:
time: 107 us; the launch traced here: 106 us
  Pallas kernels  106 us (99%)
    pallas_call x1, Pallas kernels, stepped(): pl.pallas_call(whole_step, out_shape=(jax.ShapeDtypeStruct((DEVICES * ROW...  103 us
    pallas_call x1, Pallas kernels, unpacked(): pl.pallas_call(unpack, out_shape=jax.ShapeDtypeStruct((CAP, ENT, DEVICES)...  3.5 us

profile of v6, /device:TPU:1, one launch (start us, length us, event | category | flops | bytes accessed | tf_op | source)
XLA Modules:
  0.0 106.5 jit_solution(9995995351975850734)
XLA Ops:
  0.0 103.0 %whole_step.1 = (bf16[2048,384]{1,0:T(8,128)(2,1)}, bf16[128,256]{1,0:T(8,128)(2,1)}) custom-call(bf16[2,368,368]{2,1,0:T(8,128)(2,1)} %dens_in.1, s32[2,16,16]{2,1,0:T(8,128)} %pat_in.1, s32[2,16,16]{2,1,0:T(8,128)} %keep_in.1, s32[1,512]{1,0:T(1,128)} %bitcast.4), custom_call_target="tpu_custom_call" | custom-call | tf_op jit(solution)/shard_map/whole_step/pallas_call | solution.py:543
  103.0 3.5 %unpack.1 = bf16[12,529,128]{2,1,0:T(8,128)(2,1)} custom-call(bf16[2048,384]{1,0:T(8,128)(2,1)} %get-tuple-element.7.messages, bf16[128,256]{1,0:T(8,128)(2,1)} %get-tuple-element.8.tails), custom_call_target="tpu_custom_call" | custom-call | tf_op jit(solution)/shard_map/unpack/pallas_call | solution.py:627

commit v7 on v6

--- a/solution.py
+++ b/solution.py
@@ -186,7 +186,7 @@
     for dev in ways.values():
         pl.semaphore_signal(barrier, inc=1, device_id=dev, device_id_type=MESH)
 
-    started = []
+    started = [0, 0]
     arriving = {}
     expected = [0] * GROUPS
 
@@ -218,7 +218,7 @@
             src_ref=src, dst_ref=dst, send_sem=send.at[group], recv_sem=recv.at[k],
             device_id=ways[way], device_id_type=MESH)
         op.start()
-        started.append(kind)
+        started[group] += QUARTERS[q][2] - QUARTERS[q][1]
         if k < GROUPS:
             return
         here = find(kind, d, f, q)
@@ -419,8 +419,8 @@
     messages(yh, near, 1)
     own = pltpu.make_async_copy(rows_of(outgoing, me), rows_of(arrived, me), local.at[4])
     own.start()
-    for group, kinds in enumerate(((LEFT, SIBLING), (RIGHT, SQUARE))):
-        sent = left.at[pl.ds(0, sum(kind in kinds for kind in started) // len(QUARTERS))]
+    for group, rows in enumerate(started):
+        sent = left.at[pl.ds(0, rows // (2 * W))]
         pltpu.make_async_remote_copy(
             src_ref=sent, dst_ref=sent, send_sem=send.at[group], recv_sem=recv.at[group],
             device_id=ways[CORE], device_id_type=MESH).wait_send()
@@ -585,7 +585,7 @@
     )(density, pattern, keep, owner)
 
 
-def unpack(messages, tails, out, arrived, tails_in, wide, tails_wide, by_source, ready, sem):
+def unpack(messages, tails, out, arrived, tails_in, tails_wide, by_source, ready, sem):
     chunks = [pl.ds(128 * k, 128) for k in range(LANES // 128)]
     fetches = [
         pltpu.make_async_copy(messages.at[:, at], arrived.at[:, at], sem.at[CAP + k])
@@ -609,12 +609,11 @@
     copies = []
     for k, at in enumerate(chunks):
         fetches[k].wait()
-        wide[k] = arrived[:, at].astype(F32)
+        wide = jnp.transpose(arrived[:, at].astype(F32).reshape(DEVICES, ROWS, 128), (1, 0, 2))
         for s in range(4):
-            fourth = wide[k, pl.ds(CAP + s, DEVICES, stride=ROWS), :]
-            ready[4 * k + s, pl.ds(384, 128), :] = fourth.T.astype(BF16)
+            ready[4 * k + s, pl.ds(384, 128), :] = wide[CAP + s].T.astype(BF16)
         for s in range(CAP):
-            ready[s, at, :] = wide[k, pl.ds(s, DEVICES, stride=ROWS), :].T.astype(BF16)
+            ready[s, at, :] = wide[s].T.astype(BF16)
             if k == len(chunks) - 1:
                 copies.append(pltpu.make_async_copy(ready.at[s], out.at[s], sem.at[s]))
                 copies[-1].start()
@@ -632,7 +631,6 @@
         scratch_shapes=[
             pltpu.VMEM((DEVICES * ROWS, LANES), BF16),
             pltpu.VMEM((DEVICES, 256), BF16),
-            pltpu.VMEM((LANES // 128, DEVICES * ROWS, 128), F32),
             pltpu.VMEM((2, DEVICES, 128), F32),
             pltpu.VMEM((2, DEVICES, 128), F32),
             pltpu.VMEM((CAP, ENT, DEVICES), BF16),

time: 107 us -> 106 us (level)
  no operation moved by 1% of the time
where the time goes in v7:
time: 106 us
  Pallas kernels  106 us (100%)
    pallas_call x1, Pallas kernels, stepped(): pl.pallas_call(whole_step, out_shape=(jax.ShapeDtypeStruct((DEVICES * ROW...  103 us
    pallas_call x1, Pallas kernels, unpacked(): pl.pallas_call(unpack, out_shape=jax.ShapeDtypeStruct((CAP, ENT, DEVICES)...  3.26 us

profile of v7, /device:TPU:1, one launch (start us, length us, event | category | flops | bytes accessed | tf_op | source)
XLA Modules:
  0.0 106.2 jit_solution(17836704045308554003)
XLA Ops:
  0.0 103.0 %whole_step.1 = (bf16[2048,384]{1,0:T(8,128)(2,1)}, bf16[128,256]{1,0:T(8,128)(2,1)}) custom-call(bf16[2,368,368]{2,1,0:T(8,128)(2,1)} %dens_in.1, s32[2,16,16]{2,1,0:T(8,128)} %pat_in.1, s32[2,16,16]{2,1,0:T(8,128)} %keep_in.1, s32[1,512]{1,0:T(1,128)} %bitcast.4), custom_call_target="tpu_custom_call" | custom-call | tf_op jit(solution)/shard_map/whole_step/pallas_call | solution.py:543
  103.0 3.3 %unpack.1 = bf16[12,529,128]{2,1,0:T(8,128)(2,1)} custom-call(bf16[2048,384]{1,0:T(8,128)(2,1)} %get-tuple-element.7.messages, bf16[128,256]{1,0:T(8,128)(2,1)} %get-tuple-element.8.tails), custom_call_target="tpu_custom_call" | custom-call | tf_op jit(solution)/shard_map/unpack/pallas_call | solution.py:626

commit v8 on v7

--- a/solution.py
+++ b/solution.py
@@ -258,9 +258,12 @@
         rows = buf[pl.ds(lax.rem(2 * p, NROW), 2), lax.div(p, 4)].reshape(2 * WP, WP)
         acc[at, :] += jnp.dot(jnp.concatenate(two, axis=1), rows, preferred_element_type=F32)
 
+    def is_last_left(p):
+        return (lax.div(p, 2) == lax.rem(z + 2, 4)) & (lax.rem(p, 2) == 1 - yl)
+
     def is_late(p):
         zp, yp = lax.div(p, 2), lax.rem(p, 2)
-        in_left = (zp == lax.rem(z + 2, 4)) & (yp == 1 - yl)
+        in_left = is_last_left(p)
         in_right = (lax.rem(zp, 2) == 1 - yh) & (yp == lax.div(lax.rem(x + 2, 4), 2))
         return in_left | in_right
 
@@ -313,17 +316,18 @@
     })
 
     def own_square(h):
-        if h == 0:
-            join(LATE)
-            join(7 + LATE)
-
         def add(p, carry):
-            @pl.when(is_late(p))
+            @pl.when(is_late(p) & jnp.logical_not(is_last_left(p)))
             def _():
                 multiply(p, right, h)
             return carry
 
+        if h == 0:
+            join(LATE)
         lax.fori_loop(0, NCOL // 2, add, 0)
+        if h == 0:
+            join(7 + LATE)
+        multiply(lax.rem(z + 2, 4) * 2 + 1 - yl, right, h)
         half = pl.ds(h * W, W)
         sq[r, h, pl.ds(0, W)] = (acc[half, :] / ORDER * mask[h].astype(F32)).astype(BF16)
         acc[half, :] = jnp.zeros((W, WP), F32)

time: 106 us -> 106 us (level)
  no operation moved by 1% of the time
where the time goes in v8:
time: 106 us
  Pallas kernels  106 us (100%)
    pallas_call x1, Pallas kernels, stepped(): pl.pallas_call(whole_step, out_shape=(jax.ShapeDtypeStruct((DEVICES * ROW...  103 us
    pallas_call x1, Pallas kernels, unpacked(): pl.pallas_call(unpack, out_shape=jax.ShapeDtypeStruct((CAP, ENT, DEVICES)...  3.26 us

profile of v8, /device:TPU:1, one launch (start us, length us, event | category | flops | bytes accessed | tf_op | source)
XLA Modules:
  0.0 106.1 jit_solution(4869735121002022777)
XLA Ops:
  0.0 102.9 %whole_step.1 = (bf16[2048,384]{1,0:T(8,128)(2,1)}, bf16[128,256]{1,0:T(8,128)(2,1)}) custom-call(bf16[2,368,368]{2,1,0:T(8,128)(2,1)} %dens_in.1, s32[2,16,16]{2,1,0:T(8,128)} %pat_in.1, s32[2,16,16]{2,1,0:T(8,128)} %keep_in.1, s32[1,512]{1,0:T(1,128)} %bitcast.4), custom_call_target="tpu_custom_call" | custom-call | tf_op jit(solution)/shard_map/whole_step/pallas_call | solution.py:547
  102.9 3.3 %unpack.1 = bf16[12,529,128]{2,1,0:T(8,128)(2,1)} custom-call(bf16[2048,384]{1,0:T(8,128)(2,1)} %get-tuple-element.7.messages, bf16[128,256]{1,0:T(8,128)(2,1)} %get-tuple-element.8.tails), custom_call_target="tpu_custom_call" | custom-call | tf_op jit(solution)/shard_map/unpack/pallas_call | solution.py:630

commit v9 on v8

--- a/solution.py
+++ b/solution.py
@@ -371,7 +371,12 @@
                 send_sem=exchange_send, recv_sem=exchange_recv, device_id=(to_row, to_col), device_id_type=MESH).start()
             return carry
 
-        lax.fori_loop(first, 32, start_message, 0)
+        def start_two(i, carry):
+            return start_message(i + 16, start_message(i, carry))
+
+        if first == 1:
+            start_message(16, 0)
+        lax.fori_loop(first, 16, start_two, 0)
 
     line, in_line = r * 2 + yl, z * 2 + core
 

time: 106 us -> 106 us (level)
  no operation moved by 1% of the time
where the time goes in v9:
time: 106 us
  Pallas kernels  106 us (100%)
    pallas_call x1, Pallas kernels, stepped(): pl.pallas_call(whole_step, out_shape=(jax.ShapeDtypeStruct((DEVICES * ROW...  103 us
    pallas_call x1, Pallas kernels, unpacked(): pl.pallas_call(unpack, out_shape=jax.ShapeDtypeStruct((CAP, ENT, DEVICES)...  3.26 us

profile of v9, /device:TPU:1, one launch (start us, length us, event | category | flops | bytes accessed | tf_op | source)
XLA Modules:
  0.0 106.2 jit_solution(11697353492771042910)
XLA Ops:
  0.0 102.9 %whole_step.1 = (bf16[2048,384]{1,0:T(8,128)(2,1)}, bf16[128,256]{1,0:T(8,128)(2,1)}) custom-call(bf16[2,368,368]{2,1,0:T(8,128)(2,1)} %dens_in.1, s32[2,16,16]{2,1,0:T(8,128)} %pat_in.1, s32[2,16,16]{2,1,0:T(8,128)} %keep_in.1, s32[1,512]{1,0:T(1,128)} %bitcast.4), custom_call_target="tpu_custom_call" | custom-call | tf_op jit(solution)/shard_map/whole_step/pallas_call | solution.py:552
  102.9 3.3 %unpack.1 = bf16[12,529,128]{2,1,0:T(8,128)(2,1)} custom-call(bf16[2048,384]{1,0:T(8,128)(2,1)} %get-tuple-element.7.messages, bf16[128,256]{1,0:T(8,128)(2,1)} %get-tuple-element.8.tails), custom_call_target="tpu_custom_call" | custom-call | tf_op jit(solution)/shard_map/unpack/pallas_call | solution.py:635
